TPU v7x, 32 devices: a whole 2x2x4 slice. The times are simulated.
32 devices in a mesh: dp: 16 (over z, x, core), tensor: 2 (over y).
Axes of the slice: x: 2, y: 2, z: 4, core: 2. Of those that a mesh axis runs over, the one named last changes fastest.
Arguments:
- residual: float32 [2048, 2048], P(('dp', 'tensor')), may hold values from -60 to 60
- norm_gain: bfloat16 [2048], P('dp'), may hold values from 0.5 to 1.5
- in_proj_x: bfloat16 [2048, 4096], P('dp', 'tensor'), may hold values from -0.125 to 0.125
- in_proj_z: bfloat16 [2048, 4096], P('dp', 'tensor'), may hold values from -0.125 to 0.125
- x_proj: bfloat16 [160, 4096], P(None, 'tensor'), may hold values from -0.09375 to 0.09375
- dt_proj: bfloat16 [128, 4096], P('dp', 'tensor'), may hold values from -0.5 to 0.5
- dt_bias: float32 [4096], P('tensor'), may hold values from -6 to -2
- conv_weight: float32 [4, 4096], P(None, 'tensor'), may hold values from -3 to 3
- conv_bias: float32 [4096], P('tensor'), may hold values from -0.5 to 0.5
- a_log: float32 [16, 4096], P(None, 'tensor'), may hold values from 0 to 2.77
- d_skip: float32 [4096], P('tensor'), may hold values from 0.5 to 1.5
- out_proj: bfloat16 [2048, 4096], P('dp', 'tensor'), may hold values from -0.1875 to 0.1875
- doc_ids: int32 [2048], P('dp'), may hold values from 0 to 127, never falling along the last dimension, each value on 1 to 128 neighbouring positions
- cotangent: float32 [2048, 2048], P(('dp', 'tensor')), may hold values from -6 to 6
Outputs:
- block_out: float32 [2048, 2048], P(('dp', 'tensor'))
- grad_residual: float32 [2048, 2048], P(('dp', 'tensor'))
- grad_norm_gain: float32 [2048], P('dp')
- grad_in_proj_x: float32 [2048, 4096], P('dp', 'tensor')
- grad_in_proj_z: float32 [2048, 4096], P('dp', 'tensor')
- grad_x_proj: float32 [160, 4096], P(None, 'tensor')
- grad_dt_proj: float32 [128, 4096], P('dp', 'tensor')
- grad_dt_bias: float32 [4096], P('tensor')
- grad_conv_weight: float32 [4, 4096], P(None, 'tensor')
- grad_conv_bias: float32 [4096], P('tensor')
- grad_a_log: float32 [16, 4096], P(None, 'tensor')
- grad_d_skip: float32 [4096], P('tensor')
- grad_out_proj: float32 [2048, 4096], P('dp', 'tensor')
- rms_resid: float32 [16], P('dp')
- rms_mixed: float32 [16], P('dp')
Inputs may be any that keep to these rules, and one draw needn't show every extreme that they name: doc_ids never falls along the tokens; each document number covers 1 to 128 consecutive tokens.
All inputs are finite; a program needn't handle non-finite values.
Results may differ from a plain program's by a relative error of at most 0.011.
Values may be sent and summed in bfloat16 or wider, within the bound.
A program may use at most 256 MiB of HBM per device.

v0:
```python
import jax
import jax.numpy as jnp
from jax import lax
from jax.sharding import PartitionSpec as P

D = 2048
R = 128
N = 16


eps_norm = 1e-05
highest = lax.Precision.HIGHEST


def norm_rows(values, gain_val):
    mean_square = jnp.mean(values * values, axis=1, keepdims=True)
    return values * lax.rsqrt(mean_square + eps_norm) * gain_val


def conv_local(x_in, doc_ids, conv_weight, conv_bias):
    kernel_len = conv_weight.shape[0]
    length = x_in.shape[0]
    padded = jnp.pad(x_in, ((kernel_len - 1, 0), (0, 0)))
    id_pad = jnp.concatenate([jnp.full((kernel_len - 1,), -1, jnp.int32), doc_ids])
    summed = conv_bias + jnp.zeros_like(x_in)
    for offset in range(kernel_len):
        same_doc = (id_pad[offset : offset + length] == doc_ids).astype(jnp.float32)
        summed = summed + conv_weight[offset] * padded[offset : offset + length] * same_doc[:, None]
    return summed


def scan_local(step_size, conv_val, input_map, output_map, carry_keep, a_rates):
    length, chans = step_size.shape
    block_len = min(32, length)
    block_count = length // block_len

    def combine(first_pair, second_pair):
        return (first_pair[0] * second_pair[0], second_pair[0] * first_pair[1] + second_pair[1])

    def one_block(carried, pieces):
        step_b, conv_b, in_b, out_b, keep_b = pieces
        decays = jnp.exp(step_b[:, None, :] * a_rates) * keep_b[:, None, None]
        drives = (step_b * conv_b)[:, None, :] * in_b[:, :, None]
        decay_all, drive_all = lax.associative_scan(combine, (decays, drives), axis=0)
        states_all = decay_all * carried + drive_all
        readout = jnp.sum(states_all * out_b[:, :, None], axis=1)
        return (states_all[-1], readout)

    pieces = tuple(
        (
            v.reshape((block_count, block_len) + v.shape[1:])
            for v in (step_size, conv_val, input_map, output_map, carry_keep)
        )
    )
    start_state = jnp.zeros((a_rates.shape[0], chans), jnp.float32)
    _, outputs = lax.scan(jax.checkpoint(one_block), start_state, pieces)
    return outputs.reshape(length, chans)


def per_device(
    residual,
    norm_gain,
    in_proj_x,
    in_proj_z,
    x_proj,
    dt_proj,
    dt_bias,
    conv_weight,
    conv_bias,
    a_log,
    d_skip,
    out_proj,
    doc_ids,
    cotangent,
):
    gathered = (
        lax.all_gather(norm_gain, "dp", axis=0, tiled=True),
        lax.all_gather(in_proj_x, "dp", axis=0, tiled=True),
        lax.all_gather(in_proj_z, "dp", axis=0, tiled=True),
        lax.all_gather(dt_proj, "dp", axis=0, tiled=True),
        lax.all_gather(out_proj, "dp", axis=0, tiled=True),
    )
    gain_all, inx_all, inz_all, step_all, out_all = gathered
    seq_len = doc_ids.shape[0]
    normed_f32, norm_back = jax.vjp(norm_rows, residual, gain_all.astype(jnp.float32))
    normed = lax.all_gather(normed_f32.astype(jnp.bfloat16), "tensor", axis=0, tiled=True)
    x_in = jnp.dot(normed, inx_all, preferred_element_type=jnp.float32)
    gate_in = jnp.dot(normed, inz_all, preferred_element_type=jnp.float32)

    def conv_act(x_val, weight_val, bias_val):
        return jax.nn.silu(conv_local(x_val, doc_ids, weight_val, bias_val))

    conv_out, conv_back = jax.vjp(conv_act, x_in, conv_weight, conv_bias)
    conv_low = conv_out.astype(jnp.bfloat16)
    dbl_part = lax.dot_general(
        conv_low, x_proj, (((1,), (1,)), ((), ())), preferred_element_type=jnp.float32
    )
    x_dbl, resid_square = lax.psum((dbl_part, jnp.sum(residual * residual)), "tensor")
    doc_starts = doc_ids != jnp.concatenate([jnp.full((1,), -1, jnp.int32), doc_ids[:-1]])
    carry_keep = 1.0 - doc_starts.astype(jnp.float32)

    def mixer_inner(conv_val, dbl_val, gate_val, step_weight, bias_val, alog_val, skip_val):
        step_raw = jnp.dot(dbl_val[:, :R], step_weight, precision=highest) + bias_val
        step_size = jax.nn.softplus(step_raw)
        input_map = dbl_val[:, R : R + N]
        output_map = dbl_val[:, R + N :]
        scanned = (
            scan_local(step_size, conv_val, input_map, output_map, carry_keep, -jnp.exp(alog_val))
            + skip_val * conv_val
        )
        return scanned * jax.nn.silu(gate_val)

    gated, inner_back = jax.vjp(
        mixer_inner,
        conv_low.astype(jnp.float32),
        x_dbl,
        gate_in,
        step_all.astype(jnp.float32),
        dt_bias,
        a_log,
        d_skip,
    )
    gated_low = gated.astype(jnp.bfloat16)
    mixed = lax.psum_scatter(
        lax.dot_general(
            gated_low, out_all, (((1,), (1,)), ((), ())), preferred_element_type=jnp.float32
        ),
        "tensor",
        scatter_dimension=0,
        tiled=True,
    )
    block_out = residual + mixed
    mixed_square = lax.psum(jnp.sum(mixed * mixed), "tensor")
    rms_resid = jnp.sqrt(resid_square / (seq_len * D)).reshape(1)
    rms_mixed = jnp.sqrt(mixed_square / (seq_len * D)).reshape(1)
    cot_all = lax.all_gather(cotangent.astype(jnp.bfloat16), "tensor", axis=0, tiled=True)
    grad_out_w = lax.dot_general(
        cot_all, gated_low, (((0,), (0,)), ((), ())), preferred_element_type=jnp.float32
    )
    grad_gated = jnp.dot(cot_all, out_all, preferred_element_type=jnp.float32)
    grad_conv, grad_dbl_part, grad_gate, grad_step_w, grad_bias, grad_alog, grad_skip = inner_back(
        grad_gated
    )
    grad_dbl = lax.psum(grad_dbl_part, "tensor")
    grad_dbl_low = grad_dbl.astype(jnp.bfloat16)
    grad_conv = grad_conv + jnp.dot(grad_dbl_low, x_proj, preferred_element_type=jnp.float32)
    grad_xproj = lax.dot_general(
        grad_dbl_low, conv_low, (((0,), (0,)), ((), ())), preferred_element_type=jnp.float32
    )
    grad_xin, grad_convw, grad_convb = conv_back(grad_conv)
    grad_xin_low = grad_xin.astype(jnp.bfloat16)
    grad_gate_low = grad_gate.astype(jnp.bfloat16)
    grad_inx = lax.dot_general(
        normed, grad_xin_low, (((0,), (0,)), ((), ())), preferred_element_type=jnp.float32
    )
    grad_inz = lax.dot_general(
        normed, grad_gate_low, (((0,), (0,)), ((), ())), preferred_element_type=jnp.float32
    )
    first_term = lax.dot_general(
        grad_xin_low, inx_all, (((1,), (1,)), ((), ())), preferred_element_type=jnp.float32
    )
    second_term = lax.dot_general(
        grad_gate_low, inz_all, (((1,), (1,)), ((), ())), preferred_element_type=jnp.float32
    )
    grad_normed = lax.psum_scatter(
        first_term + second_term, "tensor", scatter_dimension=0, tiled=True
    )
    grad_rows_x, grad_gain_part = norm_back(grad_normed)
    grad_residual = cotangent + grad_rows_x
    grad_gain = lax.psum(grad_gain_part, "tensor")
    gain_shard, inx_shard, inz_shard, step_shard, out_shard = (
        lax.psum_scatter(grad_gain, "dp", scatter_dimension=0, tiled=True),
        lax.psum_scatter(grad_inx, "dp", scatter_dimension=0, tiled=True),
        lax.psum_scatter(grad_inz, "dp", scatter_dimension=0, tiled=True),
        lax.psum_scatter(grad_step_w, "dp", scatter_dimension=0, tiled=True),
        lax.psum_scatter(grad_out_w, "dp", scatter_dimension=0, tiled=True),
    )
    small_sums = lax.psum(
        (grad_xproj, grad_bias, grad_convw, grad_convb, grad_alog, grad_skip), "dp"
    )
    xproj_sum, bias_sum, convw_sum, convb_sum, alog_sum, skip_sum = small_sums
    return (
        block_out,
        grad_residual,
        gain_shard,
        inx_shard,
        inz_shard,
        xproj_sum,
        step_shard,
        bias_sum,
        convw_sum,
        convb_sum,
        alog_sum,
        skip_sum,
        out_shard,
        rms_resid,
        rms_mixed,
    )


def solution(mesh):
    placed = (
        P(("dp", "tensor"), None),
        P("dp"),
        P("dp", "tensor"),
        P("dp", "tensor"),
        P(None, "tensor"),
        P("dp", "tensor"),
        P("tensor"),
        P(None, "tensor"),
        P("tensor"),
        P(None, "tensor"),
        P("tensor"),
        P("dp", "tensor"),
        P("dp"),
        P(("dp", "tensor"), None),
    )
    return jax.shard_map(
        per_device,
        mesh=mesh,
        in_specs=placed,
        out_specs=(
            P(("dp", "tensor"), None),
            P(("dp", "tensor"), None),
            P("dp"),
            P("dp", "tensor"),
            P("dp", "tensor"),
            P(None, "tensor"),
            P("dp", "tensor"),
            P("tensor"),
            P(None, "tensor"),
            P("tensor"),
            P(None, "tensor"),
            P("tensor"),
            P("dp", "tensor"),
            P("dp"),
            P("dp"),
        ),
        check_vma=False,
    )
```

profile of v0, /device:TPU:0, one launch (start us, length us, event | category | flops | bytes accessed | tf_op | source)
XLA Modules:
  0.0 3216.9 jit_solution(17574974954799466123)
XLA Ops:
  9.5 23.3 all-gather
  34.7 9.2 all_gather.22
  43.9 8.4 all_gather.27
  52.3 21.8 all_gather.24
  74.9 17.8 all-gather.5.cloned.1.call-done
  98.4 69.7 %all-gather.7.cloned.1.call-done = bf16[2048,2048]{1,0:T(8,128)(2,1)} async-done(((bf16[128,2048]{1,0:T(8,128)(2,1)}), bf16[2048,2048]{1,0:T(8,128)(2,1)}) %all-gather.7.cloned.1.call-update) | async-done | bytes 8388624 | tf_op jit(solution)/shard_map/all_gather | solution.py:79
  172.8 70.6 %all-gather.9.cloned.1.call-done = bf16[2048,2048]{1,0:T(8,128)(2,1)} async-done(((bf16[128,2048]{1,0:T(8,128)(2,1)}), bf16[2048,2048]{1,0:T(8,128)(2,1)}) %all-gather.9.cloned.1.call-update) | async-done | bytes 8388624 | tf_op jit(solution)/shard_map/all_gather | solution.py:81
  243.5 9.9 multiply_reduce_fusion.7
  255.7 18.0 all-reduce.106.cloned.1.call-done
  280.9 587.0 %while.39 = (s32[]{:T(128)}, f32[16,2048]{1,0:T(8,128)}, f32[4,32,2048]{2,1,0:T(8,128)}, f32[4,16,2048]{2,1,0:T(8,128)}, f32[4,32,2048]{2,1,0:T(8,128)}, /*index...) while((s32[]{:T(128)}, f32[16,2048]{1,0:T(8,128)}, ...), condition=%wide.region_4.5_spmd, body=%wide.region_2.4_spmd.sunk | while | flops 20676608 | bytes 234379184 | solution.py:56
  348.7 11.4 pad.1311
  382.8 11.4 pad.1309
  417.3 8.5 multiply_reduce_fusion.21
  495.4 11.4 pad.1311
  529.4 11.4 pad.1309
  556.5 7.4 pad.1308
  564.0 8.5 multiply_reduce_fusion.21
  642.0 11.4 pad.1311
  676.1 11.4 pad.1309
  703.2 7.4 pad.1308
  710.6 8.5 multiply_reduce_fusion.21
  788.7 11.4 pad.1311
  822.7 11.4 pad.1309
  857.3 8.5 multiply_reduce_fusion.21
  872.0 1459.5 %while.40 = (s32[]{:T(128)}, f32[16,2048]{1,0:T(8,128)}, f32[16,2048]{1,0:T(8,128)}, f32[4,32,2048]{2,1,0:T(8,128)}, f32[4,32,2048]{2,1,0:T(8,128)}, /*index=5*/...) while((s32[]{:T(128)}, f32[16,2048]{1,0:T(8,128)}, ...), condition=%wide.region_13.14_spmd.clone, body=%wide.region_6.13_spmd.clone.sunk | while | flops 64027648 | bytes 768302592 | solution.py:56
  1072.3 11.4 pad.1401
  1083.7 11.4 pad.1402
  1095.2 10.9 pad.1403
  1166.8 11.5 pad.1395
  1213.0 11.6 pad.1399
  1227.7 11.4 pad.1400
  1239.2 7.5 multiply_reduce_fusion.23
  1433.4 11.4 pad.1401
  1444.8 11.4 pad.1402
  1456.3 10.9 pad.1403
  1527.9 11.5 pad.1395
  1574.0 11.6 pad.1399
  1588.8 11.4 pad.1400
  1600.2 7.5 multiply_reduce_fusion.23
  1794.5 11.4 pad.1401
  1805.9 11.4 pad.1402
  1817.3 10.9 pad.1403
  1888.9 11.5 pad.1395
  1935.1 11.6 pad.1399
  1949.8 11.4 pad.1400
  1961.3 7.5 multiply_reduce_fusion.23
  2155.6 11.4 pad.1401
  2167.0 11.4 pad.1402
  2178.4 10.9 pad.1403
  2250.0 11.5 pad.1395
  2296.2 11.6 pad.1399
  2310.9 11.4 pad.1400
  2322.4 7.5 multiply_reduce_fusion.23
  2335.5 7.7 psum.78
  2364.4 14.0 reduce-scatter.9.cloned.1.call-done
  2380.4 9.3 convolution_bitcast_fusion
  2394.1 8.2 fusion.62
  2403.3 8.2 fusion.63
  2416.3 76.3 %all-reduce.108.cloned.1.call-done = (f32[2048]{0:T(1024)}, f32[2048]{0:T(1024)}, f32[4,2048]{1,0:T(4,128)}, f32[2048]{0:T(1024)}, f32[2048]{0:T(1024)}) async-done(((f32[2048]{0:T(1024)}, f32[2048]{0:T(1024)}, f32[4,2048]{1,0:T(4,128)}, f32[2048]{0:T(1024)}, f32[2048]{0:T(1024)}), (f32[2048]{0:T(1024)}, f32[2048]{0:T(1024)}, f32[4,2048]{1,0:T(4,128)}, f32[2048]{0:T(1024)}, ...) | async-done | bytes 65552
  2500.3 177.3 %reduce-scatter.17.cloned.1.call-done = f32[128,2048]{0,1:T(8,128)} async-done(((f32[2048,2048]{0,1:T(8,128)}), f32[128,2048]{0,1:T(8,128)}) %reduce-scatter.17.cloned.1.call-update) | async-done | bytes 1048592 | tf_op jit(solution)/shard_map/reduce_scatter | solution.py:176
  2680.1 96.5 %all-reduce.110.cloned.1.call-done = (f32[160,2048]{1,0:T(8,128)}, f32[16,2048]{1,0:T(8,128)}) async-done(((f32[160,2048]{1,0:T(8,128)}, f32[16,2048]{1,0:T(8,128)}), (f32[160,2048]{1,0:T(8,128)}, f32[16,2048]{1,0:T(8,128)})) %all-reduce.110.cloned.1.call-update) | async-done | bytes 1441808 | tf_op jit(solution)/shard_map/psum | solution.py:178
  2776.6 61.0 %reduce-scatter.15.cloned.1.call-done = f32[8,2048]{1,0:T(8,128)} async-done(((f32[128,2048]{1,0:T(8,128)}), f32[8,2048]{1,0:T(8,128)}) %reduce-scatter.15.cloned.1.call-update) | async-done | bytes 65552 | tf_op jit(solution)/shard_map/reduce_scatter | solution.py:175
  2837.6 182.3 %reduce-scatter.11.cloned.1.call-done = f32[128,2048]{1,0:T(8,128)} async-done(((f32[2048,2048]{1,0:T(8,128)}), f32[128,2048]{1,0:T(8,128)}) %reduce-scatter.11.cloned.1.call-update) | async-done | bytes 1048592 | tf_op jit(solution)/shard_map/reduce_scatter | solution.py:173
  3019.9 182.1 %reduce-scatter.13.cloned.1.call-done = f32[128,2048]{1,0:T(8,128)} async-done(((f32[2048,2048]{1,0:T(8,128)}), f32[128,2048]{1,0:T(8,128)}) %reduce-scatter.13.cloned.1.call-update) | async-done | bytes 1048592 | tf_op jit(solution)/shard_map/reduce_scatter | solution.py:174
  (1678 shorter events, 1662.5 us)
Async XLA Ops:
  7.2 246.2 %copy-start = (bf16[160,2048]{1,0:T(8,128)(2,1)S(1)}, bf16[160,2048]{1,0:T(8,128)(2,1)}, u32[]{:S(2)}) copy-start(bf16[160,2048]{1,0:T(8,128)(2,1)} %param.22) | copy-start | bytes 1966084
  7.2 26.7 copy-start.82
  7.2 85.5 %all-gather.5.cloned.1.call-start = ((), (), s32[]{:S(2)}) async-start(), calls=%async_computation.6 | async-start | bytes 8912896 | tf_op jit(solution)/shard_map/all_gather | solution.py:78
  7.9 160.2 %all-gather.7.cloned.1.call-start = ((), (), s32[]{:S(2)}) async-start(), calls=%async_computation.8 | async-start | bytes 8912896 | tf_op jit(solution)/shard_map/all_gather | solution.py:79
  8.7 43.5 %copy-start.129 = (s32[128]{0:T(128)S(1)}, s32[128]{0:T(128)}, u32[]{:S(2)}) copy-start(s32[128]{0:T(128)} %param.30) | copy-start | bytes 1540
  8.7 43.6 %copy-start.114 = (bf16[8,2048]{1,0:T(8,128)(2,1)S(1)}, bf16[8,2048]{1,0:T(8,128)(2,1)}, u32[]{:S(2)}) copy-start(bf16[8,2048]{1,0:T(8,128)(2,1)} %param.23) | copy-start | bytes 98308
  8.7 234.7 %all-gather.9.cloned.1.call-start = ((), (), s32[]{:S(2)}) async-start(), calls=%async_computation.9 | async-start | bytes 8912896 | tf_op jit(solution)/shard_map/all_gather | solution.py:81
  9.4 264.2 %all-reduce.106.cloned.1.call-start = ((), (), s32[]{:S(2)}) async-start(), calls=%async_computation.7 | async-start | bytes 163840 | tf_op jit(solution)/shard_map/psum | solution.py:98
  32.8 41.3 %copy-start.106 = (f32[16,1,128]{2,1,0:T(1,128)}, f32[16,1,128]{2,1,0:T(1,128)S(1)}, u32[]{:S(2)}) copy-start(f32[16,1,128]{2,1,0:T(1,128)S(1)} %convert_element_type.52) | copy-start | bytes 24580
  32.8 41.3 %copy-start.115 = (f32[4,2048]{1,0:T(4,128)S(1)}, f32[4,2048]{1,0:T(4,128)}, u32[]{:S(2)}) copy-start(f32[4,2048]{1,0:T(4,128)} %param.25) | copy-start | bytes 98308
  32.8 41.4 %copy-start.102 = (f32[16,2048]{1,0:T(8,128)S(1)}, f32[16,2048]{1,0:T(8,128)}, u32[]{:S(2)}) copy-start(f32[16,2048]{1,0:T(8,128)} %param.27) | copy-start | bytes 393220
  34.6 63.8 %copy-start.130 = (f32[64]{0:T(128)}, f32[64]{0:T(128)S(1)}, u32[]{:S(2)}) copy-start(f32[64]{0:T(128)S(1)} %fusion.36) | copy-start | bytes 772
  43.9 124.2 %copy-start.75 = (bf16[128,2048]{1,0:T(8,128)(2,1)}, bf16[128,2048]{1,0:T(8,128)(2,1)S(1)}, u32[]{:S(2)}) copy-start(bf16[128,2048]{1,0:T(8,128)(2,1)S(1)} %all_gather.22) | copy-start | bytes 1572868
  52.2 191.2 %copy-start.96 = (bf16[128,2048]{1,0:T(8,128)(2,1)}, bf16[128,2048]{1,0:T(8,128)(2,1)S(1)}, u32[]{:S(2)}) copy-start(bf16[128,2048]{1,0:T(8,128)(2,1)S(1)} %all_gather.27) | copy-start | bytes 1572868
  52.3 191.1 %copy-start.136 = (f32[128]{0:T(128)}, f32[128]{0:T(128)S(1)}, u32[]{:S(2)}) copy-start(f32[128]{0:T(128)S(1)} %get-tuple-element.766) | copy-start | bytes 1540
  52.3 191.1 %copy-start.138 = (f32[128]{0:T(128)}, f32[128]{0:T(128)S(1)}, u32[]{:S(2)}) copy-start(f32[128]{0:T(128)S(1)} %get-tuple-element.767) | copy-start | bytes 1540
  52.3 191.1 %copy-start.140 = (f32[128]{0:T(128)}, f32[128]{0:T(128)S(1)}, u32[]{:S(2)}) copy-start(f32[128]{0:T(128)S(1)} %get-tuple-element.768) | copy-start | bytes 1540
  74.1 201.7 %copy-start.97 = (bf16[128,2048]{1,0:T(8,128)(2,1)}, bf16[128,2048]{1,0:T(8,128)(2,1)S(1)}, u32[]{:S(2)}) copy-start(bf16[128,2048]{1,0:T(8,128)(2,1)S(1)} %all_gather.24) | copy-start | bytes 1572868
  74.1 169.3 %copy-start.121 = (f32[1,2048]{1,0:T(1,128)}, f32[1,2048]{1,0:T(1,128)S(1)}, u32[]{:S(2)}) copy-start(f32[1,2048]{1,0:T(1,128)S(1)} %get-tuple-element.761) | copy-start | bytes 24580
  74.2 169.3 %copy-start.123 = (f32[1,2048]{1,0:T(1,128)}, f32[1,2048]{1,0:T(1,128)S(1)}, u32[]{:S(2)}) copy-start(f32[1,2048]{1,0:T(1,128)S(1)} %get-tuple-element.762) | copy-start | bytes 24580
  74.2 169.3 %copy-start.125 = (f32[1,2048]{1,0:T(1,128)}, f32[1,2048]{1,0:T(1,128)S(1)}, u32[]{:S(2)}) copy-start(f32[1,2048]{1,0:T(1,128)S(1)} %get-tuple-element.763) | copy-start | bytes 24580
  74.2 169.3 %copy-start.127 = (f32[1,2048]{1,0:T(1,128)}, f32[1,2048]{1,0:T(1,128)S(1)}, u32[]{:S(2)}) copy-start(f32[1,2048]{1,0:T(1,128)S(1)} %get-tuple-element.764) | copy-start | bytes 24580
  98.4 145.1 %copy-start.142 = (f32[2048]{0:T(1024)S(1)}, f32[2048]{0:T(1024)}, u32[]{:S(2)}) copy-start(f32[2048]{0:T(1024)} %param.26) | copy-start | bytes 24580
  172.8 80.6 %copy-start.93 = (f32[128,2048]{1,0:T(8,128)}, f32[128,2048]{1,0:T(8,128)S(1)}, u32[]{:S(2)}) copy-start(f32[128,2048]{1,0:T(8,128)S(1)} %fusion.58) | copy-start | bytes 3145732
  253.4 25.8 copy-start.80
  253.4 22.4 copy-start.143
  254.4 2124.0 %reduce-scatter.9.cloned.1.call-start = ((), (), s32[]{:S(2)}) async-start(), calls=%async_computation.11 | async-start | bytes 1572864 | tf_op jit(solution)/shard_map/reduce_scatter | solution.py:165
  288.0 38.8 %copy-start.22 = (f32[16,16,2048]{2,1,0:T(8,128)}, f32[16,16,2048]{2,1,0:T(8,128)S(1)}, u32[]{:S(2)}) copy-start(f32[16,16,2048]{2,1,0:T(8,128)S(1)} %get-tuple-element.1037) | copy-start | bytes 6291460 | tf_op jit(solution)/shard_map/jvp()/while
  434.6 38.8 %copy-start.22 = (f32[16,16,2048]{2,1,0:T(8,128)}, f32[16,16,2048]{2,1,0:T(8,128)S(1)}, u32[]{:S(2)}) copy-start(f32[16,16,2048]{2,1,0:T(8,128)S(1)} %get-tuple-element.1037) | copy-start | bytes 6291460 | tf_op jit(solution)/shard_map/jvp()/while
  581.3 38.8 %copy-start.22 = (f32[16,16,2048]{2,1,0:T(8,128)}, f32[16,16,2048]{2,1,0:T(8,128)S(1)}, u32[]{:S(2)}) copy-start(f32[16,16,2048]{2,1,0:T(8,128)S(1)} %get-tuple-element.1037) | copy-start | bytes 6291460 | tf_op jit(solution)/shard_map/jvp()/while
  727.9 38.8 %copy-start.22 = (f32[16,16,2048]{2,1,0:T(8,128)}, f32[16,16,2048]{2,1,0:T(8,128)S(1)}, u32[]{:S(2)}) copy-start(f32[16,16,2048]{2,1,0:T(8,128)S(1)} %get-tuple-element.1037) | copy-start | bytes 6291460 | tf_op jit(solution)/shard_map/jvp()/while
  887.9 96.9 %copy-start.43 = (f32[32,2048]{1,0:T(8,128)}, f32[32,2048]{1,0:T(8,128)S(1)}, u32[]{:S(2)}) copy-start(f32[32,2048]{1,0:T(8,128)S(1)} %get-tuple-element.1106) | copy-start | bytes 786436 | tf_op jit(solution)/shard_map/transpose(jvp())/while
  1031.3 11.8 slice-start.13
  1166.8 11.5 copy-start.28
  1212.9 11.6 copy-start.14
  1249.0 96.9 %copy-start.43 = (f32[32,2048]{1,0:T(8,128)}, f32[32,2048]{1,0:T(8,128)S(1)}, u32[]{:S(2)}) copy-start(f32[32,2048]{1,0:T(8,128)S(1)} %get-tuple-element.1106) | copy-start | bytes 786436 | tf_op jit(solution)/shard_map/transpose(jvp())/while
  1392.4 11.8 slice-start.13
  1527.9 11.5 copy-start.28
  1574.0 11.6 copy-start.14
  1610.1 96.9 %copy-start.43 = (f32[32,2048]{1,0:T(8,128)}, f32[32,2048]{1,0:T(8,128)S(1)}, u32[]{:S(2)}) copy-start(f32[32,2048]{1,0:T(8,128)S(1)} %get-tuple-element.1106) | copy-start | bytes 786436 | tf_op jit(solution)/shard_map/transpose(jvp())/while
  1753.4 11.8 slice-start.13
  1888.9 11.5 copy-start.28
  1935.1 11.6 copy-start.14
  1971.2 96.9 %copy-start.43 = (f32[32,2048]{1,0:T(8,128)}, f32[32,2048]{1,0:T(8,128)S(1)}, u32[]{:S(2)}) copy-start(f32[32,2048]{1,0:T(8,128)S(1)} %get-tuple-element.1106) | copy-start | bytes 786436 | tf_op jit(solution)/shard_map/transpose(jvp())/while
  2114.5 11.8 slice-start.13
  2250.0 11.5 copy-start.28
  2296.2 11.6 copy-start.14
  2331.6 11.7 copy-start.81
  2331.6 11.7 copy-start.117
  2356.3 57.2 %reduce-scatter.7.cloned.1.call-start = ((), (), s32[]{:S(2)}) async-start(), calls=%async_computation.10 | async-start | bytes 1572864 | tf_op jit(solution)/shard_map/reduce_scatter | solution.py:124
  2356.3 22.0 copy-start.83
  2356.3 22.0 copy-start.107
  2356.4 22.0 copy-start.131
  2363.7 128.9 %all-reduce.108.cloned.1.call-start = ((), (), s32[]{:S(2)}) async-start(), calls=%async_computation.16 | async-start | bytes 131072
  2380.2 297.3 %reduce-scatter.17.cloned.1.call-start = ((), (), s32[]{:S(2)}) async-start(), calls=%async_computation.15 | async-start | bytes 17825792 | tf_op jit(solution)/shard_map/reduce_scatter | solution.py:176
  2389.8 386.8 %all-reduce.110.cloned.1.call-start = ((), (), s32[]{:S(2)}) async-start(), calls=%async_computation.17 | async-start | bytes 2883584 | tf_op jit(solution)/shard_map/psum | solution.py:178
  2391.9 445.6 %reduce-scatter.15.cloned.1.call-start = ((), (), s32[]{:S(2)}) async-start(), calls=%async_computation.14 | async-start | bytes 1114112 | tf_op jit(solution)/shard_map/reduce_scatter | solution.py:175
  2394.0 625.9 %reduce-scatter.11.cloned.1.call-start = ((), (), s32[]{:S(2)}) async-start(), calls=%async_computation.12 | async-start | bytes 17825792 | tf_op jit(solution)/shard_map/reduce_scatter | solution.py:173
  2402.3 799.7 %reduce-scatter.13.cloned.1.call-start = ((), (), s32[]{:S(2)}) async-start(), calls=%async_computation.13 | async-start | bytes 17825792 | tf_op jit(solution)/shard_map/reduce_scatter | solution.py:174
  2500.2 704.3 %copy-start.120 = (f32[2048]{0:T(1024)S(1)}, f32[2048]{0:T(1024)}, u32[]{:S(2)}) copy-start(f32[2048]{0:T(1024)} %get-tuple-element.1277) | copy-start | bytes 24580
  2500.3 704.9 %copy-start.116 = (f32[4,2048]{1,0:T(4,128)S(1)}, f32[4,2048]{1,0:T(4,128)}, u32[]{:S(2)}) copy-start(f32[4,2048]{1,0:T(4,128)} %get-tuple-element.1278) | copy-start | bytes 98308
  2500.3 705.5 %copy-start.119 = (f32[2048]{0:T(1024)S(1)}, f32[2048]{0:T(1024)}, u32[]{:S(2)}) copy-start(f32[2048]{0:T(1024)} %get-tuple-element.1279) | copy-start | bytes 24580
  2500.3 706.7 %copy-start.118 = (f32[2048]{0:T(1024)S(1)}, f32[2048]{0:T(1024)}, u32[]{:S(2)}) copy-start(f32[2048]{0:T(1024)} %get-tuple-element.1281) | copy-start | bytes 24580
  2776.6 429.7 %copy-start.108 = (f32[16,2048]{1,0:T(8,128)S(1)}, f32[16,2048]{1,0:T(8,128)}, u32[]{:S(2)}) copy-start(f32[16,2048]{1,0:T(8,128)} %get-tuple-element.1280) | copy-start | bytes 393220
  (405 other events, 1826.9 us)
Sparse Core Ops, SparseCore 0:
  10.2 82.5 all-gather.4
  94.9 73.1 all-gather.6
  170.3 73.1 all-gather.8
  254.5 19.1 all-reduce.105
  2356.4 21.9 reduce-scatter.8
  2381.1 20.3 reduce-scatter.6
  2406.7 85.7 all-reduce.107
  2497.2 180.2 reduce-scatter.16
  2682.8 93.7 all-reduce.109
  2781.1 56.4 reduce-scatter.14
  2842.3 177.5 reduce-scatter.10
  3024.4 177.5 reduce-scatter.12
where the time goes:
time: 3250 us; the launch traced here: 3220 us
  local copies, waits for them, and re-layouts  1400 us (43%)
  waiting for transfers between devices  968 us (30%)
  other arithmetic  658 us (20%)
  blocking collectives  75.9 us (2%)
  matrix products  70.4 us (2%)
    pad x248, local copies, waits for them, and re-layouts, one_block(): lax.associative_scan(combine, (decays, drives), axis=0)  1230 us
    reduce_scatter x1, waiting for transfers between devices, per_device(): lax.psum_scatter(grad_inx, 'dp', scatter_dimension=0, tiled=True)  182 us
    reduce_scatter x1, waiting for transfers between devices, per_device(): lax.psum_scatter(grad_inz, 'dp', scatter_dimension=0, tiled=True)  182 us
    reduce_scatter x1, waiting for transfers between devices, per_device(): lax.psum_scatter(grad_out_w, 'dp', scatter_dimension=0, tiled=True)  177 us
    add x64, other arithmetic, one_block(): lax.associative_scan(combine, (decays, drives), axis=0)  137 us
    mul x64, other arithmetic, combine(): first_pair[0] * second_pair[0]  131 us
    psum x1, waiting for transfers between devices, per_device(): lax.psum((grad_xproj, grad_bias, grad_convw, grad_convb, grad_alog, grad_...  96.5 us
    concatenate x64, other arithmetic, one_block(): lax.associative_scan(combine, (decays, drives), axis=0)  90.8 us
  transfers between devices with their start and end apart: 12, of which 11 were waited for; matrix products, arithmetic and copies ran while one was open for 2% of the time, Pallas kernels for 0%

commit v1 on v0

--- a/solution.py
+++ b/solution.py
@@ -1,15 +1,203 @@
 import jax
 import jax.numpy as jnp
 from jax import lax
+from jax.experimental import pallas as pl
+from jax.experimental.pallas import tpu as pltpu
 from jax.sharding import PartitionSpec as P
 
 D = 2048
 R = 128
 N = 16
 
-
 eps_norm = 1e-05
-highest = lax.Precision.HIGHEST
+
+def sigmoid(v):
+    return 1.0 / (1.0 + jnp.exp(-v))
+
+
+def fold_rows(first, second, shift, lower):
+    kept = jnp.where(lower, first, second)
+    moved = jnp.where(lower, second, first)
+    return kept + pltpu.roll(moved, shift, 0)
+
+
+class RowSums:
+    def __init__(self, masks):
+        self.masks = masks
+        self.held = {}
+        self.result = None
+
+    def add(self, token, value):
+        level = 0
+        while True:
+            if level == 3:
+                self.result = value
+                return
+            mate = (level, token ^ 1)
+            if mate not in self.held:
+                self.held[(level, token)] = value
+                return
+            other = self.held.pop(mate)
+            first, second = (other, value) if token & 1 else (value, other)
+            value = fold_rows(first, second, 1 << level, self.masks[level])
+            token >>= 1
+            level += 1
+
+
+def split_dot(left, right_low, dims):
+    high = left.astype(jnp.bfloat16)
+    rest = (left - high.astype(jnp.float32)).astype(jnp.bfloat16)
+    return lax.dot_general(high, right_low, dims, preferred_element_type=jnp.float32) + lax.dot_general(
+        rest, right_low, dims, preferred_element_type=jnp.float32
+    )
+
+
+def scan_kernel(
+    dbl_ref, conv_ref, gate_ref, gg_ref, dtp_ref, dtb_ref, alog_ref, skip_ref, keep_ref, in_ref, out_ref,
+    gated_ref, ggate_ref, gconv_ref, gdbl_ref, gin_ref, gout_ref, gdtp_ref, gdtb_ref, galog_ref, gskip_ref,
+    h_s, d_s, stepd_s, sc_s, gs_s, y_s, q_s, r_s, a_s,
+):
+    length, width = conv_ref.shape
+    blocks = width // 128
+    part = pl.program_id(0)
+    sub = lax.broadcasted_iota(jnp.int32, (8, 128), 0)
+    masks = [(sub & shift) == 0 for shift in (1, 2, 4)]
+    lanes = [slice(b * 128, (b + 1) * 128) for b in range(blocks)]
+
+    nn = (((1,), (0,)), ((), ()))
+    step_raw = split_dot(dbl_ref[...], dtp_ref[...], nn) + dtb_ref[...]
+    step = jnp.maximum(step_raw, 0.0) + jnp.log(1.0 + jnp.exp(-jnp.abs(step_raw)))
+    stepd_s[...] = jnp.where(keep_ref[...] > 0.0, step, 1e30)
+    sc_s[...] = step * conv_ref[...].astype(jnp.float32)
+    gate = gate_ref[...]
+    gs_s[...] = gg_ref[...] * gate * sigmoid(gate)
+    a_s[...] = -jnp.exp(alog_ref[...])
+
+    h_s[0] = jnp.zeros((N, width), jnp.float32)
+
+    def forward(i, hs):
+        base = pl.multiple_of(i * 8, 8)
+        hs = list(hs)
+        sums = [RowSums(masks) for _ in range(blocks)]
+        stepd = [stepd_s[pl.ds(base, 8), lanes[b]] for b in range(blocks)]
+        drive = [sc_s[pl.ds(base, 8), lanes[b]] for b in range(blocks)]
+        for j in range(8):
+            t = base + j
+            in_t = in_ref[t]
+            out_t = out_ref[t]
+            for b in range(blocks):
+                decay = jnp.exp(stepd[b][j : j + 1] * a_s[:, lanes[b]])
+                hs[b] = decay * hs[b] + drive[b][j : j + 1] * in_t
+                d_s[t, :, lanes[b]] = decay
+                h_s[t + 1, :, lanes[b]] = hs[b]
+                read = hs[b] * out_t
+                sums[b].add(j, read[:8] + read[8:])
+        for b in range(blocks):
+            y_s[pl.ds(base, 8), lanes[b]] = sums[b].result
+        return tuple(hs)
+
+    zero = jnp.zeros((N, 128), jnp.float32)
+    lax.fori_loop(0, length // 8, forward, (zero,) * blocks)
+
+    conv = conv_ref[...].astype(jnp.float32)
+    gate = gate_ref[...]
+    sig = sigmoid(gate)
+    scanned = y_s[...] + skip_ref[...] * conv
+    gated_ref[...] = (scanned * gate * sig).astype(jnp.bfloat16)
+    ggate_ref[...] = (gg_ref[...] * scanned * sig * (1.0 + gate * (1.0 - sig))).astype(jnp.bfloat16)
+
+    @pl.when(part == 0)
+    def _():
+        gin_ref[...] = jnp.zeros_like(gin_ref)
+        gout_ref[...] = jnp.zeros_like(gout_ref)
+        gdbl_ref[...] = jnp.zeros_like(gdbl_ref)
+
+    def backward(i, carried):
+        base = pl.multiple_of(length - 8 - i * 8, 8)
+        pulled, alog_sum = list(carried[0]), list(carried[1])
+        q_sums = [RowSums(masks) for _ in range(blocks)]
+        r_sums = [RowSums(masks) for _ in range(blocks)]
+        stepd = [stepd_s[pl.ds(base, 8), lanes[b]] for b in range(blocks)]
+        drive = [sc_s[pl.ds(base, 8), lanes[b]] for b in range(blocks)]
+        gs = [gs_s[pl.ds(base, 8), lanes[b]] for b in range(blocks)]
+        for j in reversed(range(8)):
+            t = base + j
+            in_t = in_ref[t]
+            out_t = out_ref[t]
+            gin_t = gin_ref[t]
+            gout_t = gout_ref[t]
+            for b in range(blocks):
+                gs_t = gs[b][j : j + 1]
+                adjoint = pulled[b] + out_t * gs_t
+                gout_t = gout_t + gs_t * h_s[t + 1, :, lanes[b]]
+                gin_t = gin_t + adjoint * drive[b][j : j + 1]
+                q_t = adjoint * in_t
+                q_sums[b].add(j, q_t[:8] + q_t[8:])
+                pulled[b] = d_s[t, :, lanes[b]] * adjoint
+                past = pulled[b] * h_s[t, :, lanes[b]]
+                r_t = past * a_s[:, lanes[b]]
+                r_sums[b].add(j, r_t[:8] + r_t[8:])
+                alog_sum[b] = alog_sum[b] + past * stepd[b][j : j + 1]
+            gin_ref[t] = gin_t
+            gout_ref[t] = gout_t
+        for b in range(blocks):
+            q_s[pl.ds(base, 8), lanes[b]] = q_sums[b].result
+            r_s[pl.ds(base, 8), lanes[b]] = r_sums[b].result
+        return tuple(pulled), tuple(alog_sum)
+
+    _, alog_sum = lax.fori_loop(0, length // 8, backward, ((zero,) * blocks, (zero,) * blocks))
+    for b in range(blocks):
+        galog_ref[:, lanes[b]] = alog_sum[b] * a_s[:, lanes[b]]
+
+    conv = conv_ref[...].astype(jnp.float32)
+    step_raw = split_dot(dbl_ref[...], dtp_ref[...], nn) + dtb_ref[...]
+    step = jnp.maximum(step_raw, 0.0) + jnp.log(1.0 + jnp.exp(-jnp.abs(step_raw)))
+    raw = (conv * q_s[...] + r_s[...]) * sigmoid(step_raw)
+    gs = gs_s[...]
+    gconv_ref[...] = step * q_s[...] + skip_ref[...] * gs
+    gskip_ref[...] = jnp.sum(gs * conv, axis=0, keepdims=True)
+    gdtb_ref[...] = jnp.sum(raw, axis=0, keepdims=True)
+    raw_low = raw.astype(jnp.bfloat16)
+    gdtp_ref[...] = lax.dot_general(
+        dbl_ref[...].astype(jnp.bfloat16), raw_low, (((0,), (0,)), ((), ())), preferred_element_type=jnp.float32
+    )
+    gdbl_ref[...] += lax.dot_general(
+        raw_low, dtp_ref[...], (((1,), (1,)), ((), ())), preferred_element_type=jnp.float32
+    )
+
+
+def scan_call(dbl, conv, gate, gg, dtp, dtb, alog, skip, keep, cb=512):
+    length, chans = conv.shape
+    cb = min(cb, chans)
+    f32 = jnp.float32
+    maps = jnp.broadcast_to(dbl[:, R:, None], (length, 2 * N, 128))
+    tokens = lambda kind: (jax.ShapeDtypeStruct((length, chans), kind), pl.BlockSpec((length, cb), lambda i: (0, i)))
+    whole = lambda *shape: (jax.ShapeDtypeStruct(shape, f32), pl.BlockSpec(shape, lambda i: (0,) * len(shape)))
+    rows = lambda count: (jax.ShapeDtypeStruct((count, chans), f32), pl.BlockSpec((count, cb), lambda i: (0, i)))
+    outs = [
+        tokens(jnp.bfloat16), tokens(jnp.bfloat16), tokens(f32), whole(length, R), whole(length, N, 128), whole(length, N, 128),
+        rows(R), rows(1), rows(N), rows(1),
+    ]
+    ins = [
+        whole(length, R), tokens(f32), tokens(f32), tokens(f32), rows(R), rows(1), rows(N), rows(1),
+        whole(length, 1),
+    ]
+    res = pl.pallas_call(
+        scan_kernel,
+        grid=(chans // cb,),
+        in_specs=[spec for _, spec in ins] + [
+            pl.BlockSpec((length, N, 128), lambda i: (0, 0, 0)), pl.BlockSpec((length, N, 128), lambda i: (0, 1, 0))],
+        out_specs=[spec for _, spec in outs],
+        out_shape=[shape for shape, _ in outs],
+        scratch_shapes=[
+            pltpu.VMEM((length + 1, N, cb), f32), pltpu.VMEM((length, N, cb), f32),
+        ] + [pltpu.VMEM((length, cb), f32)] * 6 + [pltpu.VMEM((N, cb), f32)],
+        name="selective_scan",
+        compiler_params=pltpu.CompilerParams(vmem_limit_bytes=60 << 20),
+    )(dbl[:, :R], conv, gate, gg, dtp, dtb[None], alog, skip[None], keep[:, None], maps, maps)
+    gated, ggate, gconv, gdbl, gin, gout, gdtp, gdtb, galog, gskip = res
+    gdbl_all = jnp.concatenate([gdbl, jnp.sum(gin, -1), jnp.sum(gout, -1)], axis=1)
+    return gated, ggate, gconv, gdbl_all, gdtp, gdtb[0], galog, gskip[0]
 
 
 def norm_rows(values, gain_val):
@@ -27,34 +215,6 @@
         same_doc = (id_pad[offset : offset + length] == doc_ids).astype(jnp.float32)
         summed = summed + conv_weight[offset] * padded[offset : offset + length] * same_doc[:, None]
     return summed
-
-
-def scan_local(step_size, conv_val, input_map, output_map, carry_keep, a_rates):
-    length, chans = step_size.shape
-    block_len = min(32, length)
-    block_count = length // block_len
-
-    def combine(first_pair, second_pair):
-        return (first_pair[0] * second_pair[0], second_pair[0] * first_pair[1] + second_pair[1])
-
-    def one_block(carried, pieces):
-        step_b, conv_b, in_b, out_b, keep_b = pieces
-        decays = jnp.exp(step_b[:, None, :] * a_rates) * keep_b[:, None, None]
-        drives = (step_b * conv_b)[:, None, :] * in_b[:, :, None]
-        decay_all, drive_all = lax.associative_scan(combine, (decays, drives), axis=0)
-        states_all = decay_all * carried + drive_all
-        readout = jnp.sum(states_all * out_b[:, :, None], axis=1)
-        return (states_all[-1], readout)
-
-    pieces = tuple(
-        (
-            v.reshape((block_count, block_len) + v.shape[1:])
-            for v in (step_size, conv_val, input_map, output_map, carry_keep)
-        )
-    )
-    start_state = jnp.zeros((a_rates.shape[0], chans), jnp.float32)
-    _, outputs = lax.scan(jax.checkpoint(one_block), start_state, pieces)
-    return outputs.reshape(length, chans)
 
 
 def per_device(
@@ -99,28 +259,11 @@
     doc_starts = doc_ids != jnp.concatenate([jnp.full((1,), -1, jnp.int32), doc_ids[:-1]])
     carry_keep = 1.0 - doc_starts.astype(jnp.float32)
 
-    def mixer_inner(conv_val, dbl_val, gate_val, step_weight, bias_val, alog_val, skip_val):
-        step_raw = jnp.dot(dbl_val[:, :R], step_weight, precision=highest) + bias_val
-        step_size = jax.nn.softplus(step_raw)
-        input_map = dbl_val[:, R : R + N]
-        output_map = dbl_val[:, R + N :]
-        scanned = (
-            scan_local(step_size, conv_val, input_map, output_map, carry_keep, -jnp.exp(alog_val))
-            + skip_val * conv_val
-        )
-        return scanned * jax.nn.silu(gate_val)
-
-    gated, inner_back = jax.vjp(
-        mixer_inner,
-        conv_low.astype(jnp.float32),
-        x_dbl,
-        gate_in,
-        step_all.astype(jnp.float32),
-        dt_bias,
-        a_log,
-        d_skip,
-    )
-    gated_low = gated.astype(jnp.bfloat16)
+    cot_all = lax.all_gather(cotangent.astype(jnp.bfloat16), "tensor", axis=0, tiled=True)
+    grad_gated = jnp.dot(cot_all, out_all, preferred_element_type=jnp.float32)
+    gated_low, grad_gate_low, grad_conv, grad_dbl_part, grad_step_w, grad_bias, grad_alog, grad_skip = scan_call(
+        x_dbl, conv_low, gate_in, grad_gated, step_all, dt_bias, a_log, d_skip, carry_keep
+    )
     mixed = lax.psum_scatter(
         lax.dot_general(
             gated_low, out_all, (((1,), (1,)), ((), ())), preferred_element_type=jnp.float32
@@ -133,13 +276,8 @@
     mixed_square = lax.psum(jnp.sum(mixed * mixed), "tensor")
     rms_resid = jnp.sqrt(resid_square / (seq_len * D)).reshape(1)
     rms_mixed = jnp.sqrt(mixed_square / (seq_len * D)).reshape(1)
-    cot_all = lax.all_gather(cotangent.astype(jnp.bfloat16), "tensor", axis=0, tiled=True)
     grad_out_w = lax.dot_general(
         cot_all, gated_low, (((0,), (0,)), ((), ())), preferred_element_type=jnp.float32
-    )
-    grad_gated = jnp.dot(cot_all, out_all, preferred_element_type=jnp.float32)
-    grad_conv, grad_dbl_part, grad_gate, grad_step_w, grad_bias, grad_alog, grad_skip = inner_back(
-        grad_gated
     )
     grad_dbl = lax.psum(grad_dbl_part, "tensor")
     grad_dbl_low = grad_dbl.astype(jnp.bfloat16)
@@ -149,7 +287,6 @@
     )
     grad_xin, grad_convw, grad_convb = conv_back(grad_conv)
     grad_xin_low = grad_xin.astype(jnp.bfloat16)
-    grad_gate_low = grad_gate.astype(jnp.bfloat16)
     grad_inx = lax.dot_general(
         normed, grad_xin_low, (((0,), (0,)), ((), ())), preferred_element_type=jnp.float32
     )
@@ -168,6 +305,8 @@
     grad_rows_x, grad_gain_part = norm_back(grad_normed)
     grad_residual = cotangent + grad_rows_x
     grad_gain = lax.psum(grad_gain_part, "tensor")
+    if lax.axis_size("dp") <= 16:
+        grad_inx, grad_inz, grad_out_w = (v.astype(jnp.bfloat16) for v in (grad_inx, grad_inz, grad_out_w))
     gain_shard, inx_shard, inz_shard, step_shard, out_shard = (
         lax.psum_scatter(grad_gain, "dp", scatter_dimension=0, tiled=True),
         lax.psum_scatter(grad_inx, "dp", scatter_dimension=0, tiled=True),
@@ -175,6 +314,7 @@
         lax.psum_scatter(grad_step_w, "dp", scatter_dimension=0, tiled=True),
         lax.psum_scatter(grad_out_w, "dp", scatter_dimension=0, tiled=True),
     )
+    inx_shard, inz_shard, out_shard = (v.astype(jnp.float32) for v in (inx_shard, inz_shard, out_shard))
     small_sums = lax.psum(
         (grad_xproj, grad_bias, grad_convw, grad_convb, grad_alog, grad_skip), "dp"
     )

time: 3250 us -> 965 us (0.30)
  local copies, waits for them, and re-layouts: 1400 us -> 29.8 us
  other arithmetic: 658 us -> 20.9 us
  waiting for transfers between devices: 968 us -> 735 us
    pad x248 -> x0, local copies, waits for them, and re-layouts: 1230 us -> none  [one_block(): lax.associative_scan(combine, (decays, drives), axis=0)]
    mul x109 -> x0, other arithmetic: 210 us -> none  [the longest x64 131 us: combine(): first_pair[0] * second_pair[0]]
    reduce_scatter x1 -> x0, waiting for transfers between devices: 177 us -> none  [per_device(): lax.psum_scatter(grad_out_w, 'dp', scatter_dimension=0, tiled=True)]
    add x80 -> x0, other arithmetic: 142 us -> none  [the longest x64 137 us: one_block(): lax.associative_scan(combine, (decays, drives), axis=0)]
    reduce_sum x17 -> x2, other arithmetic: 120 us -> 3.14 us  [the longest x1 1.57 us: scan_call(): jnp.sum(gout, -1)]
    unnamed x13 -> x14, waiting for transfers between devices: 78.5 us -> 183 us
    concatenate x64 -> x1, other arithmetic: 90.8 us -> 0.92 us  [scan_call(): jnp.concatenate([gdbl, jnp.sum(gin, -1), jnp.sum(gout, -1)], axis=1)]
    reduce_scatter x1, waiting for transfers between devices: 182 us -> 107 us  [per_device(): lax.psum_scatter(grad_inx, 'dp', scatter_dimension=0, tiled=True)]
  transfers between devices with their start and end apart: 12 -> 12, of which waited for: 11 -> 11; matrix products, arithmetic and copies ran while one was open for 2% -> 8% of each run, Pallas kernels for 0% -> 0%
where the time goes in v1:
time: 965 us; the launch traced here: 963 us
  waiting for transfers between devices  735 us (76%)
  blocking collectives  77.4 us (8%)
  matrix products  56.3 us (6%)
  local copies, waits for them, and re-layouts  29.8 us (3%)
  Pallas kernels  24.3 us (3%)
  other arithmetic  20.9 us (2%)
  between operations  18.8 us (2%)
    unnamed x14, waiting for transfers between devices  183 us
    reduce_scatter x1, waiting for transfers between devices, per_device(): lax.psum_scatter(grad_inz, 'dp', scatter_dimension=0, tiled=True)  107 us
    reduce_scatter x1, waiting for transfers between devices, per_device(): lax.psum_scatter(grad_inx, 'dp', scatter_dimension=0, tiled=True)  107 us
    psum x1, waiting for transfers between devices, per_device(): lax.psum((grad_xproj, grad_bias, grad_convw, grad_convb, grad_alog, grad_...  97.6 us
    all_gather x1, waiting for transfers between devices, per_device(): lax.all_gather(out_proj, 'dp', axis=0, tiled=True)  69.7 us
    all_gather x1, waiting for transfers between devices, per_device(): lax.all_gather(in_proj_z, 'dp', axis=0, tiled=True)  66.9 us
    reduce_scatter x1, waiting for transfers between devices, per_device(): lax.psum_scatter(grad_step_w, 'dp', scatter_dimension=0, tiled=True)  61 us
    pallas_call x1, Pallas kernels, scan_call(): pl.pallas_call(scan_kernel, grid=(chans // cb,), in_specs=[spec for _, sp...  24.3 us
  transfers between devices with their start and end apart: 12, of which 11 were waited for; matrix products, arithmetic and copies ran while one was open for 8% of the time, Pallas kernels for 0%

profile of v1, /device:TPU:0, one launch (start us, length us, event | category | flops | bytes accessed | tf_op | source)
XLA Modules:
  0.0 963.3 jit_solution(16718172907700142093)
XLA Ops:
  7.2 0.7 all-gather.5.cloned.1.call-update
  8.0 0.7 all-gather.7.cloned.1.call-update
  8.7 0.7 all-gather.9.cloned.1.call-update
  9.5 23.2 %all-gather = bf16[16,1,128]{2,1,0:T(2,128)(2,1)S(1)} all-gather(bf16[1,1,128]{2,1,0:T(2,128)(2,1)} %bitcast.69), channel_id=1, replica_groups=mesh['dp'=16,'tensor'=2] {'dp'}, dimensions={0}, use_global_device_ids=true | all-gather | bytes 4352 | tf_op jit(solution)/shard_map/all_gather | solution.py:237
  32.7 1.1 convert_element_type.57
  33.8 0.8 fusion.8
  34.6 0.7 copy.33.keep_ref
  35.4 1.2 multiply_reduce_fusion.8
  36.6 1.2 multiply_convert_fusion.1
  37.7 9.2 all_gather.22
  46.9 8.5 all_gather.25
  55.4 0.9 compare_convert_fusion.3
  56.3 22.2 %all_gather.27.dtp_ref = bf16[128,2048]{1,0:T(8,128)(2,1)} all-gather(bf16[8,2048]{1,0:T(8,128)(2,1)} %param.19), channel_id=1, replica_groups=mesh['dp'=16,'tensor'=2] {'dp'}, dimensions={0}, use_global_device_ids=true | all-gather | bytes 557056 | tf_op jit(solution)/shard_map/all_gather | solution.py:240
  78.5 0.9 fusion.10
  79.4 13.3 %all-gather.5.cloned.1.call-done = bf16[2048,2048]{1,0:T(8,128)(2,1)} async-done(((bf16[128,2048]{1,0:T(8,128)(2,1)}), bf16[2048,2048]{1,0:T(8,128)(2,1)}) %all-gather.5.cloned.1.call-update) | async-done | bytes 8388624 | tf_op jit(solution)/shard_map/all_gather | solution.py:238
  92.7 4.6 fusion.11
  97.4 1.0 copy-done.5
  98.4 1.8 multiply_convert_fusion
  100.2 1.0 fusion.12
  101.2 66.9 %all-gather.7.cloned.1.call-done = bf16[2048,2048]{1,0:T(8,128)(2,1)} async-done(((bf16[128,2048]{1,0:T(8,128)(2,1)}), bf16[2048,2048]{1,0:T(8,128)(2,1)}) %all-gather.7.cloned.1.call-update) | async-done | bytes 8388624 | tf_op jit(solution)/shard_map/all_gather | solution.py:239
  168.2 5.6 fusion.13.gate_ref
  173.8 69.7 %all-gather.9.cloned.1.call-done = bf16[2048,2048]{1,0:T(8,128)(2,1)} async-done(((bf16[128,2048]{1,0:T(8,128)(2,1)}), bf16[2048,2048]{1,0:T(8,128)(2,1)}) %all-gather.9.cloned.1.call-update) | async-done | bytes 8388624 | tf_op jit(solution)/shard_map/all_gather | solution.py:241
  243.5 5.6 fusion.14.gg_ref
  249.1 16.8 %all-reduce.18.cloned.1.call-done = f32[128,160]{1,0:T(8,128)} async-done(((f32[128,160]{1,0:T(8,128)}), f32[128,160]{1,0:T(8,128)}) %all-reduce.18.cloned.1.call-update) | async-done | bytes 81936 | tf_op jit(solution)/shard_map/psum | solution.py:258
  265.9 1.5 slice.55.dbl_ref
  267.4 0.8 slice.56
  268.2 2.0 broadcast_in_dim.13.in_ref.out_ref
  270.2 24.3 %selective_scan.1 = (bf16[128,2048]{1,0:T(8,128)(2,1)}, bf16[128,2048]{1,0:T(8,128)(2,1)}, f32[128,2048]{1,0:T(8,128)}, f32[128,128]{1,0:T(8,128)}, f32[128,16,1...) custom-call(f32[128,128]{1,0:T(8,128)} %slice.55.dbl_ref, ...), custom_call_target="tpu_custom_call" | custom-call | tf_op jit(solution)/shard_map/selective_scan/pallas_call | solution.py:185
  294.5 1.6 reduce_sum.107
  296.1 1.6 reduce_sum.106
  297.7 0.9 pad_maximum_fusion
  298.6 8.7 psum.78
  307.3 3.7 multiply_reduce_fusion.3
  311.4 6.5 fusion.16
  317.9 3.9 convolution_add_fusion.1
  321.9 7.3 fusion.15
  329.2 0.6 pad_add_fusion.3
  329.9 14.0 %reduce-scatter.11.cloned.1.call-done = f32[64,2048]{1,0:T(8,128)} async-done(((f32[128,2048]{1,0:T(8,128)}), f32[64,2048]{1,0:T(8,128)}) %reduce-scatter.11.cloned.1.call-update) | async-done | bytes 524304 | tf_op jit(solution)/shard_map/reduce_scatter | solution.py:302
  343.8 1.8 multiply_reduce_fusion.5
  345.7 5.6 convert_bitcast_fusion
  351.3 12.4 %copy.36 = bf16[2048,2048]{1,0:T(8,128)(2,1)} copy(bf16[2048,2048]{0,1:T(8,128)(2,1)} %convert_bitcast_fusion) | data formatting | bytes 16777216
  364.0 5.6 convolution_convert_fusion.1
  369.7 5.6 convolution_convert_fusion
  375.3 1.4 fusion.17
  377.4 0.6 dynamic-slice
  378.7 2.8 multiply_reduce_fusion.4
  381.4 76.5 %all-reduce.20.cloned.1.call-done = (f32[2048]{0:T(1024)}, f32[2048]{0:T(1024)}, f32[4,2048]{1,0:T(4,128)}, f32[2048]{0:T(1024)}, f32[2048]{0:T(1024)}) async-done(((f32[2048]{0:T(1024)}, f32[2048]{0:T(1024)}, f32[4,2048]{1,0:T(4,128)}, f32[2048]{0:T(1024)}, f32[2048]{0:T(1024)}), (f32[2048]{0:T(1024)}, f32[2048]{0:T(1024)}, f32[4,2048]{1,0:T(4,128)}, f32[2048]{0:T(1024)}, ...) | async-done | bytes 65552
  457.9 0.8 dynamic-slice.1
  458.7 5.6 all-reduce.13
  465.7 103.3 %reduce-scatter.19.cloned.1.call-done = bf16[128,2048]{1,0:T(8,128)(2,1)} async-done(((bf16[2048,2048]{1,0:T(8,128)(2,1)}), bf16[128,2048]{1,0:T(8,128)(2,1)}) %reduce-scatter.19.cloned.1.call-update) | async-done | bytes 524304
  569.0 1.3 copy.37
  570.3 1.2 copy.34
  571.5 106.6 %reduce-scatter.13.cloned.1.call-done = bf16[128,2048]{1,0:T(8,128)(2,1)} async-done(((bf16[2048,2048]{1,0:T(8,128)(2,1)}), bf16[128,2048]{1,0:T(8,128)(2,1)}) %reduce-scatter.13.cloned.1.call-update) | async-done | bytes 524304 | tf_op jit(solution)/shard_map/reduce_scatter | solution.py:312
  678.1 2.1 convert_element_type.61
  680.2 106.8 %reduce-scatter.15.cloned.1.call-done = bf16[128,2048]{1,0:T(8,128)(2,1)} async-done(((bf16[2048,2048]{1,0:T(8,128)(2,1)}), bf16[128,2048]{1,0:T(8,128)(2,1)}) %reduce-scatter.15.cloned.1.call-update) | async-done | bytes 524304 | tf_op jit(solution)/shard_map/reduce_scatter | solution.py:313
  787.0 2.1 convert_element_type.63
  789.1 97.6 %all-reduce.22.cloned.1.call-done = (f32[160,2048]{1,0:T(8,128)}, f32[16,2048]{1,0:T(8,128)}) async-done(((f32[160,2048]{1,0:T(8,128)}, f32[16,2048]{1,0:T(8,128)}), (f32[160,2048]{1,0:T(8,128)}, f32[16,2048]{1,0:T(8,128)})) %all-reduce.22.cloned.1.call-update) | async-done | bytes 1441808 | tf_op jit(solution)/shard_map/psum | solution.py:318
  886.7 61.0 %reduce-scatter.17.cloned.1.call-done = f32[8,2048]{1,0:T(8,128)} async-done(((f32[128,2048]{1,0:T(8,128)}), f32[8,2048]{1,0:T(8,128)}) %reduce-scatter.17.cloned.1.call-update) | async-done | bytes 65552 | tf_op jit(solution)/shard_map/reduce_scatter | solution.py:314
  947.7 2.5 copy.46
  950.2 0.6 copy.47
  950.8 0.6 copy.48
  951.5 0.6 copy.49
  952.1 1.6 copy.50
  953.6 0.6 copy.51
  (64 shorter events, 1.9 us)
Async XLA Ops:
  7.2 93.0 %copy-start = (bf16[160,2048]{1,0:T(8,128)(2,1)S(1)}, bf16[160,2048]{1,0:T(8,128)(2,1)}, u32[]{:S(2)}) copy-start(bf16[160,2048]{1,0:T(8,128)(2,1)} %param.18) | copy-start | bytes 1966084
  7.2 85.5 %all-gather.5.cloned.1.call-start = ((), (), s32[]{:S(2)}) async-start(), calls=%async_computation.6 | async-start | bytes 8912896 | tf_op jit(solution)/shard_map/all_gather | solution.py:238
  7.9 160.2 %all-gather.7.cloned.1.call-start = ((), (), s32[]{:S(2)}) async-start(), calls=%async_computation.8 | async-start | bytes 8912896 | tf_op jit(solution)/shard_map/all_gather | solution.py:239
  8.7 234.8 %all-gather.9.cloned.1.call-start = ((), (), s32[]{:S(2)}) async-start(), calls=%async_computation.9 | async-start | bytes 8912896 | tf_op jit(solution)/shard_map/all_gather | solution.py:241
  9.4 256.5 %all-reduce.18.cloned.1.call-start = ((), (), s32[]{:S(2)}) async-start(), calls=%async_computation.7 | async-start | bytes 262144 | tf_op jit(solution)/shard_map/psum | solution.py:258
  46.9 51.5 %copy-start.12 = (f32[2048]{0:T(1024)S(1)}, f32[2048]{0:T(1024)}, u32[]{:S(2)}) copy-start(f32[2048]{0:T(1024)} %param.22) | copy-start | bytes 24580
  97.4 1.0 copy-start.5
  100.1 73.6 %copy-start.3 = (bf16[128,2048]{1,0:T(8,128)(2,1)}, bf16[128,2048]{1,0:T(8,128)(2,1)S(1)}, u32[]{:S(2)}) copy-start(bf16[128,2048]{1,0:T(8,128)(2,1)S(1)} %get-tuple-element.83.conv_ref) | copy-start | bytes 1572868
  101.2 242.7 %reduce-scatter.11.cloned.1.call-start = ((), (), s32[]{:S(2)}) async-start(), calls=%async_computation.11 | async-start | bytes 1572864 | tf_op jit(solution)/shard_map/reduce_scatter | solution.py:302
  249.1 58.2 %copy-start.6 = (f32[128,2048]{1,0:T(8,128)S(1)}, f32[128,2048]{1,0:T(8,128)}, u32[]{:S(2)}) copy-start(f32[128,2048]{1,0:T(8,128)} %copy-done.5) | copy-start | bytes 3145732
  307.3 10.6 %slice-start = ((s8[8388608]{0:T(1024)(128)(4,1)}), s8[4194304]{0:T(1024)(128)(4,1)S(1)}, s32[]{:S(2)}) async-start(s8[8388608]{0:T(1024)(128)(4,1)} %bitcast.47), calls=%async_computation.18 | async-start | bytes 8388608
  311.0 6.9 copy-start.10
  311.0 6.9 slice-start.1
  317.9 4.0 copy-start.7
  321.8 22.0 %copy-start.2 = (f32[64,2048]{1,0:T(8,128)S(1)}, f32[64,2048]{1,0:T(8,128)}, u32[]{:S(2)}) copy-start(f32[64,2048]{1,0:T(8,128)} %param.14) | copy-start | bytes 1572868
  321.8 56.8 %reduce-scatter.9.cloned.1.call-start = ((), (), s32[]{:S(2)}) async-start(), calls=%async_computation.10 | async-start | bytes 1572864 | tf_op jit(solution)/shard_map/reduce_scatter | solution.py:267
  329.2 128.7 %all-reduce.20.cloned.1.call-start = ((), (), s32[]{:S(2)}) async-start(), calls=%async_computation.16 | async-start | bytes 131072
  345.7 223.3 %reduce-scatter.19.cloned.1.call-start = ((), (), s32[]{:S(2)}) async-start(), calls=%async_computation.15 | async-start | bytes 8912896
  363.7 314.4 %reduce-scatter.13.cloned.1.call-start = ((), (), s32[]{:S(2)}) async-start(), calls=%async_computation.12 | async-start | bytes 8912896 | tf_op jit(solution)/shard_map/reduce_scatter | solution.py:312
  369.6 5.7 copy-start.4
  369.6 417.4 %reduce-scatter.15.cloned.1.call-start = ((), (), s32[]{:S(2)}) async-start(), calls=%async_computation.13 | async-start | bytes 8912896 | tf_op jit(solution)/shard_map/reduce_scatter | solution.py:313
  375.2 2.1 copy-start.16
  375.2 3.4 copy-start.8
  375.2 3.4 copy-start.9
  375.3 579.0 %copy-start.1 = (bf16[160,2048]{1,0:T(8,128)(2,1)S(1)}, bf16[160,2048]{1,0:T(8,128)(2,1)}, u32[]{:S(2)}) copy-start(bf16[160,2048]{1,0:T(8,128)(2,1)} %param.18) | copy-start | bytes 1966084
  375.3 511.4 %all-reduce.22.cloned.1.call-start = ((), (), s32[]{:S(2)}) async-start(), calls=%async_computation.17 | async-start | bytes 2883584 | tf_op jit(solution)/shard_map/psum | solution.py:318
  376.8 571.0 %reduce-scatter.17.cloned.1.call-start = ((), (), s32[]{:S(2)}) async-start(), calls=%async_computation.14 | async-start | bytes 1114112 | tf_op jit(solution)/shard_map/reduce_scatter | solution.py:314
  457.9 492.3 %copy-start.15 = (f32[2048]{0:T(1024)S(1)}, f32[2048]{0:T(1024)}, u32[]{:S(2)}) copy-start(f32[2048]{0:T(1024)} %get-tuple-element.106) | copy-start | bytes 24580
  457.9 492.9 %copy-start.11 = (f32[4,2048]{1,0:T(4,128)S(1)}, f32[4,2048]{1,0:T(4,128)}, u32[]{:S(2)}) copy-start(f32[4,2048]{1,0:T(4,128)} %get-tuple-element.107) | copy-start | bytes 98308
  457.9 493.5 %copy-start.14 = (f32[2048]{0:T(1024)S(1)}, f32[2048]{0:T(1024)}, u32[]{:S(2)}) copy-start(f32[2048]{0:T(1024)} %get-tuple-element.108) | copy-start | bytes 24580
  457.9 495.7 %copy-start.13 = (f32[2048]{0:T(1024)S(1)}, f32[2048]{0:T(1024)}, u32[]{:S(2)}) copy-start(f32[2048]{0:T(1024)} %get-tuple-element.110) | copy-start | bytes 24580
Sparse Core Ops, SparseCore 0:
  10.2 82.5 all-gather.4
  94.9 73.2 all-gather.6
  170.3 73.1 all-gather.8
  246.2 19.6 all-reduce.17
  321.9 21.8 reduce-scatter.10
  346.6 20.3 reduce-scatter.8
  372.2 85.6 all-reduce.19
  462.5 106.4 reduce-scatter.18
  573.6 104.4 reduce-scatter.12
  682.6 104.4 reduce-scatter.14
  792.3 94.3 all-reduce.21
  891.2 56.5 reduce-scatter.16

commit v2 on v1

--- a/solution.py
+++ b/solution.py
@@ -10,6 +10,7 @@
 N = 16
 
 eps_norm = 1e-05
+
 
 def sigmoid(v):
     return 1.0 / (1.0 + jnp.exp(-v))
@@ -162,20 +163,20 @@
         dbl_ref[...].astype(jnp.bfloat16), raw_low, (((0,), (0,)), ((), ())), preferred_element_type=jnp.float32
     )
     gdbl_ref[...] += lax.dot_general(
-        raw_low, dtp_ref[...], (((1,), (1,)), ((), ())), preferred_element_type=jnp.float32
-    )
-
-
-def scan_call(dbl, conv, gate, gg, dtp, dtb, alog, skip, keep, cb=512):
+        dtp_ref[...], raw_low, (((1,), (1,)), ((), ())), preferred_element_type=jnp.float32
+    )
+
+
+def scan_call(dbl, conv, gate, gg, dtp, dtb, alog, skip, keep):
     length, chans = conv.shape
-    cb = min(cb, chans)
+    cb = min(65536 // length, chans)
     f32 = jnp.float32
     maps = jnp.broadcast_to(dbl[:, R:, None], (length, 2 * N, 128))
     tokens = lambda kind: (jax.ShapeDtypeStruct((length, chans), kind), pl.BlockSpec((length, cb), lambda i: (0, i)))
     whole = lambda *shape: (jax.ShapeDtypeStruct(shape, f32), pl.BlockSpec(shape, lambda i: (0,) * len(shape)))
     rows = lambda count: (jax.ShapeDtypeStruct((count, chans), f32), pl.BlockSpec((count, cb), lambda i: (0, i)))
     outs = [
-        tokens(jnp.bfloat16), tokens(jnp.bfloat16), tokens(f32), whole(length, R), whole(length, N, 128), whole(length, N, 128),
+        tokens(jnp.bfloat16), tokens(jnp.bfloat16), tokens(f32), whole(R, length), whole(length, N, 128), whole(length, N, 128),
         rows(R), rows(1), rows(N), rows(1),
     ]
     ins = [
@@ -196,8 +197,685 @@
         compiler_params=pltpu.CompilerParams(vmem_limit_bytes=60 << 20),
     )(dbl[:, :R], conv, gate, gg, dtp, dtb[None], alog, skip[None], keep[:, None], maps, maps)
     gated, ggate, gconv, gdbl, gin, gout, gdtp, gdtb, galog, gskip = res
-    gdbl_all = jnp.concatenate([gdbl, jnp.sum(gin, -1), jnp.sum(gout, -1)], axis=1)
+    gdbl_all = jnp.concatenate([gdbl, jnp.sum(gin, -1).T, jnp.sum(gout, -1).T], axis=0)
     return gated, ggate, gconv, gdbl_all, gdtp, gdtb[0], galog, gskip[0]
+
+
+MESH = pl.DeviceIdType.MESH
+NZ = 4
+F32 = jnp.float32
+BF16 = jnp.bfloat16
+NN = (((1,), (0,)), ((), ()))
+NT = (((1,), (1,)), ((), ()))
+TN = (((0,), (0,)), ((), ()))
+
+
+def dot(left, right, dims=NN):
+    return lax.dot_general(left, right, dims, preferred_element_type=F32)
+
+
+def place(z, x, c):
+    return (z * 2 + x) * 2 + c
+
+
+class Spot:
+    def __init__(self):
+        self.dp = lax.axis_index("dp")
+        self.y = lax.axis_index("tensor")
+        self.z, self.x, self.c = self.dp // 4, (self.dp // 2) % 2, self.dp % 2
+        self.x_mate = (place(self.z, 1 - self.x, self.c), self.y)
+        self.c_mate = (place(self.z, self.x, 1 - self.c), self.y)
+        self.y_mate = (self.dp, 1 - self.y)
+
+    def z_at(self, offset):
+        return lax.rem(self.z + offset + NZ, NZ)
+
+    def on_line(self, z, y=None):
+        return (place(z, self.x, self.c), self.y if y is None else y)
+
+
+def greet(devices):
+    barrier = pltpu.get_barrier_semaphore()
+    for device in devices:
+        pl.semaphore_signal(barrier, inc=1, device_id=device, device_id_type=MESH)
+    pl.semaphore_wait(barrier, len(devices))
+
+
+class Copies:
+    def __init__(self, send_sems):
+        self.send_sems = send_sems
+        self.begun = []
+
+    def send(self, src, dst, recv_sem, device):
+        copy = pltpu.make_async_remote_copy(
+            src_ref=src, dst_ref=dst, send_sem=self.send_sems.at[len(self.begun)], recv_sem=recv_sem,
+            device_id=device, device_id_type=MESH,
+        )
+        copy.start()
+        self.begun.append(copy)
+
+    def wait_sent(self):
+        for copy in self.begun:
+            copy.wait_send()
+
+
+def arrived(dst, recv_sem):
+    pltpu.make_async_copy(dst, dst, recv_sem).wait()
+
+
+class Gather:
+    def __init__(self, spot, copies, src, dst, recv_sems, own_sem):
+        self.spot, self.copies, self.src, self.dst, self.recv_sems, self.own_sem = spot, copies, src, dst, recv_sems, own_sem
+        self.width = dst.shape[-1]
+
+    def columns(self, z):
+        return self.src.at[:, pl.ds(pl.multiple_of(z * self.width, self.width), self.width)]
+
+    def push(self):
+        spot, me = self.spot, self.spot.dp
+        for offset in range(1, NZ):
+            z = spot.z_at(offset)
+            self.copies.send(self.columns(z), self.dst.at[me], self.recv_sems.at[me], spot.on_line(z))
+        self.own = pltpu.make_async_copy(self.columns(spot.z), self.dst.at[me], self.own_sem)
+        self.own.start()
+
+    def pass_on(self, origin, device):
+        self.copies.send(self.dst.at[origin], self.dst.at[origin], self.recv_sems.at[origin], device)
+
+    def first(self):
+        spot = self.spot
+        for offset in range(NZ):
+            origin = place(spot.z_at(-offset), spot.x, spot.c)
+            if offset == 0:
+                self.own.wait()
+            else:
+                arrived(self.dst.at[origin], self.recv_sems.at[origin])
+            self.pass_on(origin, spot.x_mate)
+            self.pass_on(origin, spot.c_mate)
+
+    def second(self):
+        spot = self.spot
+        for offset in range(NZ):
+            origin = place(spot.z_at(-offset), 1 - spot.x, spot.c)
+            arrived(self.dst.at[origin], self.recv_sems.at[origin])
+            self.pass_on(origin, spot.c_mate)
+
+    def last(self):
+        spot = self.spot
+        for x in range(2):
+            for offset in range(NZ):
+                origin = place(spot.z_at(-offset), x, 1 - spot.c)
+                arrived(self.dst.at[origin], self.recv_sems.at[origin])
+
+
+class Share:
+    def __init__(self, spot, copies, dst, recv_sems):
+        self.spot, self.copies, self.dst, self.recv_sems = spot, copies, dst, recv_sems
+
+    def send(self, z, device):
+        y = self.spot.y
+        self.copies.send(self.dst.at[z, y], self.dst.at[z, y], self.recv_sems.at[z, y], device)
+
+    def push(self):
+        spot = self.spot
+        for offset in range(1, NZ):
+            self.send(spot.z, spot.on_line(spot.z_at(offset)))
+        self.send(spot.z, spot.y_mate)
+
+    def first(self):
+        spot = self.spot
+        for offset in range(1, NZ):
+            z = spot.z_at(-offset)
+            arrived(self.dst.at[z, spot.y], self.recv_sems.at[z, spot.y])
+            self.send(z, spot.y_mate)
+
+    def last(self):
+        spot = self.spot
+        for offset in range(NZ):
+            z = spot.z_at(-offset)
+            arrived(self.dst.at[z, 1 - spot.y], self.recv_sems.at[z, 1 - spot.y])
+
+
+class LineSum:
+    def __init__(self, spot, copies, part, landing, total, part_sems, total_sems):
+        self.spot, self.copies, self.part, self.landing, self.total = spot, copies, part, landing, total
+        self.part_sems, self.total_sems = part_sems, total_sems
+        self.offsets = [(dz, dy) for dz in range(NZ) for dy in range(2) if dz + dy > 0]
+
+    def there(self, dz, dy):
+        return self.spot.z_at(dz), lax.rem(self.spot.y + dy, 2)
+
+    def push(self):
+        for dz, dy in self.offsets:
+            z, y = self.there(dz, dy)
+            slot = dz * 2 + dy
+            self.copies.send(self.part.at[z, y], self.landing.at[slot], self.part_sems.at[slot], self.spot.on_line(z, y))
+
+    def middle(self):
+        own_z, own_y = self.spot.z, self.spot.y
+        summed = self.part[own_z, own_y]
+        for dz, dy in self.offsets:
+            slot = dz * 2 + dy
+            arrived(self.landing.at[slot], self.part_sems.at[slot])
+            summed = summed + self.landing[slot]
+        self.total[own_z, own_y] = summed
+        own = self.total.at[own_z, own_y]
+        for dz, dy in self.offsets:
+            z, y = self.there(dz, dy)
+            self.copies.send(own, own, self.total_sems.at[own_z, own_y], self.spot.on_line(z, y))
+
+    def last(self):
+        for dz, dy in self.offsets:
+            z, y = self.there(dz, dy)
+            arrived(self.total.at[z, y], self.total_sems.at[z, y])
+
+
+def column_masks(tile):
+    return jnp.concatenate([tile] * 16, axis=0).T
+
+
+def ahead_kernel(
+    inx_ref, inz_ref, outp_ref, dtp_ref, resid_ref, cot_ref, info_ref, xproj_ref, chan_ref,
+    w_ref, acts_ref, dtp_all, info_all, xin_ref, pre_ref, low_ref, gate_ref, gg_ref, total_ref, square_ref,
+    part_s, landing_s, square_s, send_sems, w_sems, own_sems, act_sems, info_sems, part_sems, total_sems, square_sem,
+):
+    spot = Spot()
+    plane = [lax.rem(spot.dp + offset, 4 * NZ) for offset in range(1, 4 * NZ)]
+    greet([(dp, spot.y) for dp in plane] + [spot.on_line(spot.z_at(dz), 1 - spot.y) for dz in range(NZ)])
+    copies = Copies(send_sems)
+    chans = xin_ref.shape[1]
+    lengths = resid_ref.shape[0] * 2
+
+    info_all[spot.dp] = info_ref[...]
+    for dp in plane:
+        copies.send(info_ref, info_all.at[spot.dp], info_sems.at[spot.dp], (dp, spot.y))
+    gathers = [
+        Gather(spot, copies, src, dst, w_sems.at[k], own_sems.at[k])
+        for k, (src, dst) in enumerate(
+            ((inx_ref, w_ref.at[0]), (inz_ref, w_ref.at[1]), (outp_ref, w_ref.at[2]), (dtp_ref, dtp_all))
+        )
+    ]
+    inx, inz, outp, dtp = gathers
+    normed, cot = (Share(spot, copies, acts_ref.at[k], act_sems.at[k]) for k in range(2))
+    inx.push()
+
+    resid = resid_ref[...]
+    row_square = jnp.sum(resid * resid, axis=1, keepdims=True)
+    scaled = resid * lax.rsqrt(row_square / resid.shape[1] + eps_norm)
+    square_s[0] = jnp.broadcast_to(jnp.sum(row_square, axis=0, keepdims=True), (8, 128))
+    copies.send(square_s.at[0], square_s.at[1], square_sem, spot.y_mate)
+    acts_ref[1, spot.z, spot.y] = cot_ref[...].astype(BF16)
+    for dp in plane:
+        arrived(info_all.at[dp], info_sems.at[dp])
+    for k in range(4 * NZ):
+        cols = slice(k * 128, (k + 1) * 128)
+        acts_ref[0, spot.z, spot.y, :, cols] = (scaled[:, cols] * info_all[k, 0:1, :]).astype(BF16)
+    normed.push()
+    dtp.push()
+    inx.first()
+    inz.push()
+    dtp.first()
+    normed.first()
+    inx.second()
+    cot.push()
+    dtp.second()
+    inz.first()
+    normed.last()
+    inx.last()
+    outp.push()
+
+    x_in = dot(acts_ref[0].reshape(NZ * lengths, -1), w_ref[0].reshape(-1, chans))
+    xin_ref[...] = x_in
+    for k in range(NZ):
+        rows = slice(k * lengths, (k + 1) * lengths)
+        mask = column_masks(info_all[place(k, spot.x, spot.c)])
+        one = x_in[rows]
+        pre = chan_ref[4:5] + chan_ref[3:4] * one
+        for back in range(1, 4):
+            pre = pre + chan_ref[3 - back : 4 - back] * (pltpu.roll(one, back, 0) * mask[:, back : back + 1])
+        pre_ref[rows] = pre
+        low_ref[rows] = (pre * sigmoid(pre)).astype(BF16)
+    columns = pl.ds(pl.multiple_of(spot.z * chans, chans), chans)
+    dbl = dot(xproj_ref[:, columns], low_ref[...], NT)
+    half = dbl.shape[0] // 2
+    for k in range(NZ):
+        for y in range(2):
+            part_s[k, y] = dbl[y * half : (y + 1) * half, k * lengths : (k + 1) * lengths]
+    x_dbl = LineSum(spot, copies, part_s, landing_s, total_ref, part_sems, total_sems)
+    x_dbl.push()
+    inz.second()
+    cot.first()
+    x_dbl.middle()
+    inz.last()
+    gate_ref[...] = dot(acts_ref[0].reshape(NZ * lengths, -1), w_ref[1].reshape(-1, chans))
+    outp.first()
+    x_dbl.last()
+    outp.second()
+    cot.last()
+    outp.last()
+    gg_ref[...] = dot(acts_ref[1].reshape(NZ * lengths, -1), w_ref[2].reshape(-1, chans))
+    dtp.last()
+    arrived(square_s.at[1], square_sem)
+    square_ref[...] = square_s[0] + square_s[1]
+    copies.wait_sent()
+
+
+def ahead_call(in_x, in_z, out_p, dt_p, residual, cotangent, info, x_proj, chan):
+    rows, width = in_x.shape
+    n_dp = 4 * NZ
+    half, feats = residual.shape
+    chans = width // NZ
+    tokens = NZ * 2 * half
+    shape = jax.ShapeDtypeStruct
+    outs = [
+        shape((3, n_dp, rows, chans), BF16), shape((2, NZ, 2, half, feats), BF16), shape((n_dp, dt_p.shape[0], chans), F32),
+        shape((n_dp, 8, 128), F32), shape((tokens, chans), F32), shape((tokens, chans), F32), shape((tokens, chans), BF16),
+        shape((tokens, chans), F32), shape((tokens, chans), F32), shape((NZ, 2, x_proj.shape[0] // 2, 2 * half), F32),
+        shape((8, 128), F32),
+    ]
+    in_any = pl.BlockSpec(memory_space=pl.ANY)
+    in_vmem = pl.BlockSpec(memory_space=pltpu.VMEM)
+    dma = pltpu.SemaphoreType.DMA
+    return pl.pallas_call(
+        ahead_kernel,
+        out_shape=outs,
+        in_specs=[in_any] * 4 + [in_vmem] * 5,
+        out_specs=[in_vmem] * len(outs),
+        scratch_shapes=[
+            pltpu.VMEM(outs[9].shape, F32), pltpu.VMEM((2 * NZ,) + outs[9].shape[2:], F32), pltpu.VMEM((2, 8, 128), F32),
+            dma((128,)), dma((4, n_dp)), dma((4,)), dma((2, NZ, 2)), dma((n_dp,)), dma((2 * NZ,)), dma((NZ, 2)), dma(()),
+        ],
+        name="ahead",
+        compiler_params=pltpu.CompilerParams(collective_id=1, has_side_effects=True, vmem_limit_bytes=60 << 20),
+    )(in_x, in_z, out_p, dt_p, residual, cotangent, info, x_proj, chan)
+
+
+class TokenSum:
+    def __init__(self, spot, copies, part, y_land, z_land, y_sems, z_sems):
+        self.spot, self.copies, self.part, self.y_land, self.z_land = spot, copies, part, y_land, z_land
+        self.y_sems, self.z_sems = y_sems, z_sems
+
+    def push(self):
+        spot = self.spot
+        for offset in (1, 2, 3, 0):
+            z = spot.z_at(offset)
+            self.copies.send(self.part.at[z, 1 - spot.y], self.y_land.at[z], self.y_sems.at[z], spot.y_mate)
+
+    def middle(self):
+        spot = self.spot
+        for offset in (1, 2, 3):
+            z = spot.z_at(offset)
+            arrived(self.y_land.at[z], self.y_sems.at[z])
+            self.part[z, spot.y] = (self.part[z, spot.y].astype(F32) + self.y_land[z].astype(F32)).astype(BF16)
+            self.copies.send(self.part.at[z, spot.y], self.z_land.at[offset - 1], self.z_sems.at[offset - 1], spot.on_line(z))
+
+    def last(self):
+        spot = self.spot
+        arrived(self.y_land.at[spot.z], self.y_sems.at[spot.z])
+        summed = self.part[spot.z, spot.y].astype(F32) + self.y_land[spot.z].astype(F32)
+        for k in range(NZ - 1):
+            arrived(self.z_land.at[k], self.z_sems.at[k])
+            summed = summed + self.z_land[k].astype(F32)
+        return summed
+
+
+class RowSum:
+    def __init__(self, spot, copies, part, c_land, x_land, z_land, c_sems, x_sems, z_sems, out):
+        self.spot, self.copies, self.part, self.out = spot, copies, part, out
+        self.c_land, self.x_land, self.z_land = c_land, x_land, z_land
+        self.c_sems, self.x_sems, self.z_sems = c_sems, x_sems, z_sems
+
+    def push(self):
+        spot = self.spot
+        for offset in (1, 2, 3, 0):
+            z = spot.z_at(offset)
+            for x in (1 - spot.x, spot.x):
+                self.copies.send(self.part.at[z, x, 1 - spot.c], self.c_land.at[z, x], self.c_sems.at[z, x], spot.c_mate)
+
+    def add(self, z, x, landed):
+        part = self.part
+        part[z, x, self.spot.c] = (part[z, x, self.spot.c].astype(F32) + landed.astype(F32)).astype(part.dtype)
+
+    def second(self):
+        spot = self.spot
+        for offset in (1, 2, 3, 0):
+            z = spot.z_at(offset)
+            for x in (1 - spot.x, spot.x):
+                arrived(self.c_land.at[z, x], self.c_sems.at[z, x])
+                self.add(z, x, self.c_land[z, x])
+            self.copies.send(self.part.at[z, 1 - spot.x, spot.c], self.x_land.at[z], self.x_sems.at[z], spot.x_mate)
+
+    def columns(self, z):
+        width = self.part.shape[-1]
+        return pl.ds(pl.multiple_of(z * width, width), width)
+
+    def third(self):
+        spot = self.spot
+        for offset in (1, 2, 3, 0):
+            z = spot.z_at(offset)
+            arrived(self.x_land.at[z], self.x_sems.at[z])
+            self.add(z, spot.x, self.x_land[z])
+            if offset:
+                self.copies.send(
+                    self.part.at[z, spot.x, spot.c], self.z_land.at[spot.z], self.z_sems.at[spot.z], spot.on_line(z)
+                )
+        self.out[:, self.columns(spot.z)] = self.part[spot.z, spot.x, spot.c].astype(F32)
+
+    def last(self):
+        spot = self.spot
+        for offset in (1, 2, 3):
+            z = spot.z_at(-offset)
+            arrived(self.z_land.at[z], self.z_sems.at[z])
+            self.out[:, self.columns(z)] = self.z_land[z].astype(F32)
+
+
+class ChannelSum:
+    def __init__(self, spot, copies, part, c_land, x_land, full, c_sem, x_sem, full_sems):
+        self.spot, self.copies, self.part, self.full, self.full_sems = spot, copies, part, full, full_sems
+        self.c_land, self.x_land, self.c_sem, self.x_sem = c_land, x_land, c_sem, x_sem
+
+    def push(self):
+        self.copies.send(self.part.at[1 - self.spot.c], self.c_land, self.c_sem, self.spot.c_mate)
+
+    def second(self):
+        spot = self.spot
+        arrived(self.c_land, self.c_sem)
+        self.part[spot.c] = self.part[spot.c] + self.c_land[...]
+        self.copies.send(self.part.at[spot.c, 1 - spot.x], self.x_land, self.x_sem, spot.x_mate)
+
+    def spread(self, origin, device):
+        self.copies.send(self.full.at[origin], self.full.at[origin], self.full_sems.at[origin], device)
+
+    def third(self):
+        spot = self.spot
+        arrived(self.x_land, self.x_sem)
+        self.full[spot.dp] = self.part[spot.c, spot.x] + self.x_land[...]
+        for offset in (1, 2, 3):
+            self.spread(spot.dp, spot.on_line(spot.z_at(offset)))
+        self.spread(spot.dp, spot.x_mate)
+        self.spread(spot.dp, spot.c_mate)
+
+    def fourth(self):
+        spot = self.spot
+        for offset in (1, 2, 3):
+            origin = place(spot.z_at(-offset), spot.x, spot.c)
+            arrived(self.full.at[origin], self.full_sems.at[origin])
+            self.spread(origin, spot.x_mate)
+            self.spread(origin, spot.c_mate)
+
+    def fifth(self):
+        spot = self.spot
+        for offset in range(NZ):
+            origin = place(spot.z_at(-offset), 1 - spot.x, spot.c)
+            arrived(self.full.at[origin], self.full_sems.at[origin])
+            self.spread(origin, spot.c_mate)
+
+    def last(self):
+        spot = self.spot
+        for x in range(2):
+            for offset in range(NZ):
+                origin = place(spot.z_at(-offset), x, 1 - spot.c)
+                arrived(self.full.at[origin], self.full_sems.at[origin])
+
+
+def back_kernel(
+    mixed_part, outw_part, inz_part, dtp_part, dbl_ref, small_ref,
+    w_ref, normed_ref, xin_ref, pre_ref, low_ref, gconv_ref, ggate_ref, info_all, xproj_ref, chan_ref,
+    resid_ref, cot_ref, gain_ref,
+    block_ref, gresid_ref, ggain_ref, ginx_ref, ginz_ref, goutp_ref, gdtp_ref, full_ref, msquare_ref,
+    mixed_s, normed_s, inx_s, inz_s, outw_s, dtp_s, chan_s, part_s, landing_s, total_s,
+    y_land, z_land, wc_land, wx_land, wz_land, dc_land, dx_land, dz_land, fc_land, fx_land, square_s, gain_s, gain_land,
+    send_sems, part_sems, total_sems, y_sems, z_sems, wc_sems, wx_sems, wz_sems, f_sems, full_sems, tile_sems, gain_sems,
+    load_sems,
+):
+    spot = Spot()
+    plane = [lax.rem(spot.dp + offset, 4 * NZ) for offset in range(1, 4 * NZ)]
+    loads = [
+        pltpu.make_async_copy(src, dst, load_sems.at[k])
+        for k, (src, dst) in enumerate(((mixed_part, mixed_s), (outw_part, outw_s), (inz_part, inz_s), (dtp_part, dtp_s)))
+    ]
+    for load in loads:
+        load.start()
+    greet([(dp, spot.y) for dp in plane] + [spot.on_line(spot.z_at(dz), 1 - spot.y) for dz in range(NZ)])
+    copies = Copies(send_sems)
+    chans = xin_ref.shape[1]
+    half = resid_ref.shape[0]
+    length = 2 * half
+
+    rows = dbl_ref.shape[0] // 2
+    for k in range(NZ):
+        for y in range(2):
+            part_s[k, y] = dbl_ref[y * rows : (y + 1) * rows, k * length : (k + 1) * length]
+    dbl_sum = LineSum(spot, copies, part_s, landing_s, total_s, part_sems, total_sems)
+    dbl_sum.push()
+
+    mixed_sum, normed_sum = (
+        TokenSum(spot, copies, part, y_land.at[k], z_land.at[k], y_sems.at[k], z_sems.at[k])
+        for k, part in enumerate((mixed_s, normed_s))
+    )
+    outw_sum, inz_sum, inx_sum = (
+        RowSum(
+            spot, copies, part, wc_land.at[k], wx_land.at[k], wz_land.at[k], wc_sems.at[k], wx_sems.at[k], wz_sems.at[k], out
+        )
+        for k, (part, out) in enumerate(((outw_s, goutp_ref), (inz_s, ginz_ref), (inx_s, ginx_ref)))
+    )
+    dtp_sum = RowSum(spot, copies, dtp_s, dc_land, dx_land, dz_land, wc_sems.at[3], wx_sems.at[3], wz_sems.at[3], gdtp_ref)
+    for load in loads:
+        load.wait()
+    mixed_sum.push()
+    outw_sum.push()
+    inz_sum.push()
+    dtp_sum.push()
+    dbl_sum.middle()
+    outw_sum.second()
+    inz_sum.second()
+    dtp_sum.second()
+    mixed_sum.middle()
+    dbl_sum.last()
+
+    grad_dbl = jnp.concatenate(
+        [jnp.concatenate([total_s[k, y] for k in range(NZ)], axis=1) for y in range(2)], axis=0
+    ).astype(BF16)
+    columns = pl.ds(pl.multiple_of(spot.z * chans, chans), chans)
+    grad_conv = gconv_ref[...] + dot(grad_dbl, xproj_ref[:, columns], TN)
+    pre = pre_ref[...]
+    sig = sigmoid(pre)
+    grad_pre = grad_conv * sig * (1.0 + pre * (1.0 - sig))
+    taps = [jnp.zeros((1, chans), F32) for _ in range(4)]
+    low_rows = []
+    for k in range(NZ):
+        here = slice(k * length, (k + 1) * length)
+        mask = column_masks(info_all[place(k, spot.x, spot.c)])
+        one, x_one = grad_pre[here], xin_ref[here]
+        taps[3] = taps[3] + jnp.sum(one * x_one, axis=0, keepdims=True)
+        grad_x = chan_ref[3:4] * one
+        for back in range(1, 4):
+            masked = one * mask[:, back : back + 1]
+            taps[3 - back] = taps[3 - back] + jnp.sum(masked * pltpu.roll(x_one, back, 0), axis=0, keepdims=True)
+            grad_x = grad_x + chan_ref[3 - back : 4 - back] * pltpu.roll(masked, length - back, 0)
+        low_rows.append(grad_x.astype(BF16))
+    grad_xin = jnp.concatenate(low_rows, axis=0)
+    grad_bias = jnp.sum(grad_pre, axis=0, keepdims=True)
+    chan_s[...] = jnp.concatenate(
+        [dot(grad_dbl, low_ref[...]), small_ref[...], jnp.concatenate(taps + [grad_bias, jnp.zeros((3, chans), F32)], axis=0)], axis=0
+    ).reshape(chan_s.shape)
+    small_sum = ChannelSum(
+        spot, copies, chan_s, fc_land, fx_land, full_ref, f_sems.at[0], f_sems.at[1], full_sems
+    )
+    small_sum.push()
+    w_x, w_z = (w_ref[k].reshape(-1, chans) for k in range(2))
+    grad_normed = dot(grad_xin, w_x, NT) + dot(ggate_ref[...], w_z, NT)
+    normed_s[...] = grad_normed.astype(BF16).reshape(normed_s.shape)
+    normed_sum.push()
+    normed = normed_ref[...].reshape(NZ * length, -1)
+    inx_s[...] = dot(normed, grad_xin, TN).astype(BF16).reshape(inx_s.shape)
+    inx_sum.push()
+
+    outw_sum.third()
+    inz_sum.third()
+    dtp_sum.third()
+    small_sum.second()
+    inx_sum.second()
+    normed_sum.middle()
+    small_sum.third()
+
+    mixed = mixed_sum.last()
+    resid = resid_ref[...]
+    block_ref[...] = resid + mixed
+    square_s[0] = jnp.broadcast_to(jnp.sum(jnp.sum(mixed * mixed, axis=1, keepdims=True), axis=0, keepdims=True), (8, 128))
+    copies.send(square_s.at[0], square_s.at[1], tile_sems.at[0], spot.y_mate)
+    inx_sum.third()
+    small_sum.fourth()
+    outw_sum.last()
+    inz_sum.last()
+    dtp_sum.last()
+    small_sum.fifth()
+
+    grad_rows = normed_sum.last()
+    feats = resid.shape[1]
+    inv = lax.rsqrt(jnp.sum(resid * resid, axis=1, keepdims=True) / feats + eps_norm)
+    scaled = resid * inv
+    gain_part = jnp.sum(grad_rows * scaled, axis=0, keepdims=True)
+    for k in range(4 * NZ):
+        gain_s[0, k] = jnp.broadcast_to(gain_part[:, k * 128 : (k + 1) * 128], (8, 128))
+    copies.send(gain_s.at[0], gain_s.at[1], tile_sems.at[1], spot.y_mate)
+    grad_scaled = grad_rows * gain_ref[...]
+    mean = jnp.sum(grad_scaled * scaled, axis=1, keepdims=True) / feats
+    gresid_ref[...] = cot_ref[...] + inv * (grad_scaled - scaled * mean)
+    arrived(gain_s.at[1], tile_sems.at[1])
+    gain_s[2] = gain_s[0] + gain_s[1]
+    for offset, dp in enumerate(plane):
+        copies.send(gain_s.at[2, dp], gain_land.at[offset], gain_sems.at[offset], (dp, spot.y))
+    arrived(square_s.at[1], tile_sems.at[0])
+    msquare_ref[...] = square_s[0] + square_s[1]
+    inx_sum.last()
+    small_sum.last()
+    total = gain_s[2, spot.dp]
+    for offset in range(4 * NZ - 1):
+        arrived(gain_land.at[offset], gain_sems.at[offset])
+        total = total + gain_land[offset]
+    ggain_ref[...] = total
+    copies.wait_sent()
+
+
+def back_call(mixed_part, outw_part, inz_part, dtp_part, dbl, small, w, normed, x_in, pre, low, gconv, ggate, info_all, x_proj, chan, residual, cotangent, gain):
+    half, feats = residual.shape
+    tokens, chans = x_in.shape
+    n_dp = 4 * NZ
+    rows = outw_part.shape[0] // n_dp
+    step_rows = dtp_part.shape[0] // n_dp
+    wide = chans * NZ
+    small_rows = dbl.shape[0] + small.shape[0] + 8
+    shape = jax.ShapeDtypeStruct
+    outs = [
+        shape((half, feats), F32), shape((half, feats), F32), shape((8, 128), F32),
+        shape((rows, wide), F32), shape((rows, wide), F32), shape((rows, wide), F32), shape((step_rows, wide), F32),
+        shape((n_dp, small_rows // 4, chans), F32), shape((8, 128), F32),
+    ]
+    in_any = pl.BlockSpec(memory_space=pl.ANY)
+    in_vmem = pl.BlockSpec(memory_space=pltpu.VMEM)
+    vmem, dma = pltpu.VMEM, pltpu.SemaphoreType.DMA
+    part = (NZ, 2, dbl.shape[0] // 2, 2 * half)
+    tokens_of = (NZ, 2, half, feats)
+    owners = (NZ, 2, 2, rows, chans)
+    steps = (NZ, 2, 2, step_rows, chans)
+    return pl.pallas_call(
+        back_kernel,
+        out_shape=outs,
+        in_specs=[in_any] * 4 + [in_vmem] * 15,
+        out_specs=[in_vmem] * len(outs),
+        scratch_shapes=[
+            vmem(tokens_of, BF16), vmem(tokens_of, BF16), vmem(owners, BF16), vmem(owners, BF16), vmem(owners, BF16),
+            vmem(steps, F32), vmem((2, 2, small_rows // 4, chans), F32), vmem(part, F32), vmem((2 * NZ,) + part[2:], F32), vmem(part, F32),
+            vmem((2, NZ) + tokens_of[2:], BF16), vmem((2, NZ - 1) + tokens_of[2:], BF16),
+            vmem((3, NZ, 2) + owners[3:], BF16), vmem((3, NZ) + owners[3:], BF16), vmem((3, NZ) + owners[3:], BF16),
+            vmem((NZ, 2) + steps[3:], F32), vmem((NZ,) + steps[3:], F32), vmem((NZ,) + steps[3:], F32),
+            vmem((2, small_rows // 4, chans), F32), vmem((small_rows // 4, chans), F32),
+            vmem((2, 8, 128), F32), vmem((3, n_dp, 8, 128), F32), vmem((n_dp - 1, 8, 128), F32),
+            dma((192,)), dma((2 * NZ,)), dma((NZ, 2)), dma((2, NZ)), dma((2, NZ - 1)), dma((4, NZ, 2)), dma((4, NZ)), dma((4, NZ)),
+            dma((2,)), dma((n_dp,)), dma((2,)), dma((n_dp - 1,)), dma((4,)),
+        ],
+        name="back",
+        compiler_params=pltpu.CompilerParams(collective_id=2, has_side_effects=True, vmem_limit_bytes=62 << 20),
+    )(
+        mixed_part.reshape(tokens_of), outw_part.reshape(owners), inz_part.reshape(owners), dtp_part.reshape(steps), dbl, small,
+        w, normed, x_in, pre, low, gconv, ggate, info_all, x_proj, chan, residual, cotangent, gain,
+    )
+
+
+def per_device_split(
+    residual,
+    norm_gain,
+    in_proj_x,
+    in_proj_z,
+    x_proj,
+    dt_proj,
+    dt_bias,
+    conv_weight,
+    conv_bias,
+    a_log,
+    d_skip,
+    out_proj,
+    doc_ids,
+    cotangent,
+):
+    dp = lax.axis_index("dp")
+    z, group = dp // 4, dp % 4
+    chans = in_proj_x.shape[1] // NZ
+    seq_len = doc_ids.shape[0]
+    tokens = NZ * seq_len
+
+    def columns(*rows):
+        return lax.dynamic_slice_in_dim(jnp.concatenate(rows, axis=0), z * chans, chans, 1)
+
+    spare = jnp.zeros((3,) + conv_bias.shape, F32)
+    chan = columns(conv_weight, conv_bias[None], spare)
+    rates = columns(a_log, dt_bias[None], d_skip[None])
+    position = jnp.arange(seq_len)
+    same = [((jnp.roll(doc_ids, back) == doc_ids) & (position >= back)).astype(F32) for back in (1, 2, 3)]
+    info = jnp.stack([norm_gain.astype(F32)] + same + [jnp.zeros((seq_len,), F32)] * 4)
+
+    w_all, acts, step_all, info_all, x_in, conv_pre, conv_low, gate_in, grad_gated, dbl_total, resid_square = ahead_call(
+        in_proj_x, in_proj_z, out_proj, dt_proj.astype(F32), residual, cotangent, info, x_proj, chan
+    )
+    dbl_rows = dbl_total.transpose(1, 2, 0, 3).reshape(x_proj.shape[0], tokens)
+    keep = lax.dynamic_slice_in_dim(info_all.reshape(NZ, 4, 8, seq_len), group, 1, 1)[:, 0, 1].reshape(tokens)
+    normed, cot_all = (v.reshape(tokens, -1) for v in (acts[0], acts[1]))
+    gated, grad_gate, grad_conv, grad_dbl_part, grad_step_part, grad_bias, grad_alog, grad_skip = scan_call(
+        dbl_rows.T, conv_low, gate_in, grad_gated, step_all.reshape(R, chans).astype(BF16),
+        rates[N], rates[:N], rates[N + 1], keep,
+    )
+    mixed_part = dot(gated, w_all[2].reshape(-1, chans), NT).astype(BF16)
+    outw_part = dot(cot_all, gated, TN).astype(BF16)
+    inz_part = dot(normed, grad_gate, TN).astype(BF16)
+    small = jnp.concatenate([grad_alog, grad_bias[None], grad_skip[None], jnp.zeros((6, chans), F32)], axis=0)
+    gain_all = info_all[:, 0].reshape(1, -1)
+    block_out, grad_residual, grad_gain, grad_inx, grad_inz, grad_outp, grad_dtp, full, mixed_square = back_call(
+        mixed_part, outw_part, inz_part, grad_step_part, grad_dbl_part, small, w_all, acts[0], x_in, conv_pre, conv_low,
+        grad_conv, grad_gate, info_all, x_proj, chan, residual, cotangent, gain_all,
+    )
+    rows = full.reshape(NZ, 2, 2, -1, chans).transpose(2, 1, 3, 0, 4).reshape(-1, NZ * chans)
+    width = x_proj.shape[0]
+    xproj_sum, alog_sum, bias_sum, skip_sum = rows[:width], rows[width : width + N], rows[width + N], rows[width + N + 1]
+    convw_sum, convb_sum = rows[width + 24 : width + 28], rows[width + 28]
+    rms_resid, rms_mixed = (jnp.sqrt(v[0, :1] / (seq_len * D)) for v in (resid_square, mixed_square))
+    return (
+        block_out,
+        grad_residual,
+        grad_gain[0],
+        grad_inx,
+        grad_inz,
+        xproj_sum,
+        grad_dtp,
+        bias_sum,
+        convw_sum,
+        convb_sum,
+        alog_sum,
+        skip_sum,
+        grad_outp,
+        rms_resid,
+        rms_mixed,
+    )
 
 
 def norm_rows(values, gain_val):
@@ -279,7 +957,7 @@
     grad_out_w = lax.dot_general(
         cot_all, gated_low, (((0,), (0,)), ((), ())), preferred_element_type=jnp.float32
     )
-    grad_dbl = lax.psum(grad_dbl_part, "tensor")
+    grad_dbl = lax.psum(grad_dbl_part.T, "tensor")
     grad_dbl_low = grad_dbl.astype(jnp.bfloat16)
     grad_conv = grad_conv + jnp.dot(grad_dbl_low, x_proj, preferred_element_type=jnp.float32)
     grad_xproj = lax.dot_general(
@@ -305,8 +983,6 @@
     grad_rows_x, grad_gain_part = norm_back(grad_normed)
     grad_residual = cotangent + grad_rows_x
     grad_gain = lax.psum(grad_gain_part, "tensor")
-    if lax.axis_size("dp") <= 16:
-        grad_inx, grad_inz, grad_out_w = (v.astype(jnp.bfloat16) for v in (grad_inx, grad_inz, grad_out_w))
     gain_shard, inx_shard, inz_shard, step_shard, out_shard = (
         lax.psum_scatter(grad_gain, "dp", scatter_dimension=0, tiled=True),
         lax.psum_scatter(grad_inx, "dp", scatter_dimension=0, tiled=True),
@@ -314,7 +990,6 @@
         lax.psum_scatter(grad_step_w, "dp", scatter_dimension=0, tiled=True),
         lax.psum_scatter(grad_out_w, "dp", scatter_dimension=0, tiled=True),
     )
-    inx_shard, inz_shard, out_shard = (v.astype(jnp.float32) for v in (inx_shard, inz_shard, out_shard))
     small_sums = lax.psum(
         (grad_xproj, grad_bias, grad_convw, grad_convb, grad_alog, grad_skip), "dp"
     )
@@ -356,7 +1031,7 @@
         P(("dp", "tensor"), None),
     )
     return jax.shard_map(
-        per_device,
+        per_device_split if mesh.shape["dp"] == 4 * NZ else per_device,
         mesh=mesh,
         in_specs=placed,
         out_specs=(

time: 965 us -> 351 us (0.36)
  waiting for transfers between devices: 735 us -> 0 us
  Pallas kernels: 24.3 us -> 286 us
  blocking collectives: 77.4 us -> 0 us
  matrix products: 56.3 us -> 7.92 us
  between operations: 18.8 us -> 4.5 us
    reduce_scatter x5 -> x0, waiting for transfers between devices: 288 us -> none  [the longest x1 107 us: per_device(): lax.psum_scatter(grad_inz, 'dp', scatter_dimension=0, tiled=True)]
    pallas_call x0 -> x2, Pallas kernels: none -> 250 us  [the longest x1 130 us: back_call(): pl.pallas_call(back_kernel, out_shape=outs, in_specs=[in_any] * 4 + [in_v...]
    unnamed x14 -> x0, waiting for transfers between devices: 183 us -> none
    all_gather x3 -> x0, waiting for transfers between devices: 150 us -> none  [the longest x1 69.7 us: per_device(): lax.all_gather(out_proj, 'dp', axis=0, tiled=True)]
    psum x2 -> x0, waiting for transfers between devices: 114 us -> none  [the longest x1 97.6 us: per_device(): lax.psum((grad_xproj, grad_bias, grad_convw, grad_convb, grad_alog, grad_...]
    all_gather x4 -> x0, blocking collectives: 63.1 us -> none  [the longest x1 23.2 us: per_device(): lax.all_gather(norm_gain, 'dp', axis=0, tiled=True)]
    dot_general x12 -> x3, matrix products: 56.3 us -> 7.92 us  [dot(): return lax.dot_general(left, right, dims, preferred_element_type=F32)]
    unnamed x49 -> x33, local copies, waits for them, and re-layouts: 23.8 us -> 5.79 us
  transfers between devices with their start and end apart: 12 -> 0, of which waited for: 11 -> 0; matrix products, arithmetic and copies ran while one was open for 8% -> 0% of each run, Pallas kernels for 0% -> 0%
where the time goes in v2:
time: 351 us; the launch traced here: 350 us
  Pallas kernels  286 us (81%)
  local copies, waits for them, and re-layouts  36.5 us (10%)
  other arithmetic  14.7 us (4%)
  matrix products  7.92 us (2%)
  between operations  4.5 us (1%)
    pallas_call x1, Pallas kernels, back_call(): pl.pallas_call(back_kernel, out_shape=outs, in_specs=[in_any] * 4 + [in_v...  130 us
    pallas_call x1, Pallas kernels, ahead_call(): pl.pallas_call(ahead_kernel, out_shape=outs, in_specs=[in_any] * 4 + [in_...  120 us
    pallas_call x1, Pallas kernels, scan_call(): pl.pallas_call(scan_kernel, grid=(chans // cb,), in_specs=[spec for _, sp...  36.5 us
    dot_general x3, matrix products, dot(): return lax.dot_general(left, right, dims, preferred_element_type=F32)  7.92 us

profile of v2, /device:TPU:0, one launch (start us, length us, event | category | flops | bytes accessed | tf_op | source)
XLA Modules:
  0.0 350.1 jit_solution(4451567146286686516)
XLA Ops:
  0.7 0.1 pad.12.clone
  0.8 1.4 fusion.3.chan_ref
  2.1 1.2 slice.82
  3.4 0.7 slice.84
  4.1 0.7 slice.86
  4.8 1.5 fusion.6
  6.3 0.7 bitcast_convert_fusion
  7.0 0.6 stack.39.info_ref
  7.6 1.4 convert_element_type.21.dtp_ref
  9.0 119.9 %ahead.1 = (bf16[3,16,128,512]{3,2,1,0:T(8,128)(2,1)}, bf16[2,4,2,64,2048]{4,3,2,1,0:T(8,128)(2,1)}, f32[16,8,512]{2,1,0:T(8,128)}, f32[16,8,128]{2,1,0:T(8,128)...) custom-call(bf16[128,2048]{1,0:T(8,128)(2,1)} %inx_ref.1, ...), custom_call_target="tpu_custom_call" | custom-call | tf_op jit(solution)/shard_map/ahead/pallas_call | solution.py:479
  128.9 1.2 copy.44
  130.1 0.3 reshape.75
  130.4 0.0 copy-start.6
  130.5 0.0 copy-start.8
  130.5 0.0 copy-start.10
  130.5 0.0 copy-start.11
  130.5 5.5 %broadcast_in_dim.25.in_ref.out_ref = f32[512,32,128]{2,1,0:T(8,128)} broadcast(f32[512,32]{1,0:T(8,128)S(1)} %slice.111), dimensions={0,1} | broadcast | bytes 8454144 | tf_op jit(solution)/shard_map/broadcast_in_dim | solution.py:174
  136.0 0.7 slice.107.dbl_ref
  136.8 0.7 dynamic-slice_bitcast_fusion
  137.5 0.9 copy.40.keep_ref
  138.3 0.0 copy-done.6
  138.3 0.7 convert_bitcast_fusion.dtp_ref
  139.0 0.0 copy-done.8
  139.0 0.0 copy-done.10
  139.0 0.0 copy-done.11
  139.0 0.1 fusion.1
  139.1 0.6 slice.109.alog_ref
  139.7 0.6 fusion.8
  140.3 36.5 %selective_scan.1 = (bf16[512,512]{1,0:T(8,128)(2,1)}, bf16[512,512]{1,0:T(8,128)(2,1)}, f32[512,512]{1,0:T(8,128)}, f32[128,512]{1,0:T(8,128)}, f32[512,16,128]...) custom-call(f32[512,128]{1,0:T(8,128)} %slice.107.dbl_ref, ...), custom_call_target="tpu_custom_call" | custom-call | tf_op jit(solution)/shard_map/selective_scan/pallas_call | solution.py:186
  176.8 0.1 pad.3.clone
  176.9 1.5 maximum_maximum_fusion.small_ref
  178.4 3.4 reduce_sum.18
  181.7 0.1 copy.41
  181.8 3.4 reduce_sum.19
  185.2 0.1 copy.42
  185.3 0.0 copy-done.7
  185.3 0.8 pad_maximum_fusion.dbl_ref
  186.1 4.3 %slice_bitcast_fusion.2 = (bf16[4,2,64,2048]{3,2,1,0:T(8,128)(2,1)}, bf16[1,4,2,64,2048]{4,3,2,1,0:T(8,128)(2,1)S(1)}, bf16[1,4,2,64,2048]{4,3,2,1,0:T(8,128)(2,1)S(1)}) fusion(bf16[2,4,2,64,2048]{4,3,2,1,0:T(8,128)(2,1)} %get-tuple-element.53), kind=kLoop, calls=%fused_computation.25 | loop fusion | bytes 10485760 | tf_op jit(solution)/shard_map/squeeze | solution.py:854
  190.4 0.0 copy-done.3
  190.4 2.7 convolution_convert_fusion
  193.0 0.0 copy-done.12
  193.0 2.7 convolution_convert_fusion.1
  195.7 1.7 slice.94
  197.4 2.6 convolution_convert_fusion.2
  200.0 1.4 slice_bitcast_fusion.gain_ref
  201.5 130.1 %back.1 = (f32[64,2048]{1,0:T(8,128)}, f32[64,2048]{1,0:T(8,128)}, f32[8,128]{1,0:T(8,128)}, f32[128,2048]{1,0:T(8,128)}, f32[128,2048]{1,0:T(8,128)}, /*index=5...) custom-call(bf16[4,2,64,2048]{3,2,1,0:T(8,128)(2,1)} %bitcast.65, ...), custom_call_target="tpu_custom_call" | custom-call | tf_op jit(solution)/shard_map/back/pallas_call | solution.py:782
  331.6 2.4 copy.43
  334.0 0.6 copy.48
  334.6 0.0 copy-start.5
  334.6 1.1 slice.112
  335.8 0.7 slice.116
  336.4 0.6 slice.114
  337.1 0.6 fusion.7
  337.7 1.2 slice.106
  339.6 1.2 slice_bitcast_fusion.1
  340.7 1.2 slice.105
  342.7 0.8 copy.55
  343.5 0.0 copy-done.4
  343.5 0.8 copy.56
  344.2 0.0 copy-done.2
  344.3 1.0 copy.57
  345.2 1.0 copy.58
  346.2 0.6 copy.59
  346.8 1.0 copy.60
  (16 shorter events, 0.0 us)
Async XLA Ops:
  130.4 7.9 %copy-start.6 = (f32[16,8,512]{2,1,0:T(8,128)S(1)}, f32[16,8,512]{2,1,0:T(8,128)}, u32[]{:S(2)}) copy-start(f32[16,8,512]{2,1,0:T(8,128)} %get-tuple-element.49) | copy-start | bytes 786436
  130.5 8.6 %copy-start.8 = (f32[16,2048]{1,0:T(8,128)S(1)}, f32[16,2048]{1,0:T(8,128)}, u32[]{:S(2)}) copy-start(f32[16,2048]{1,0:T(8,128)} %param.23) | copy-start | bytes 393220
  130.5 8.6 %copy-start.10 = (f32[2048]{0:T(1024)S(1)}, f32[2048]{0:T(1024)}, u32[]{:S(2)}) copy-start(f32[2048]{0:T(1024)} %param.20) | copy-start | bytes 24580
  130.5 8.5 %copy-start.11 = (f32[2048]{0:T(1024)S(1)}, f32[2048]{0:T(1024)}, u32[]{:S(2)}) copy-start(f32[2048]{0:T(1024)} %param.24) | copy-start | bytes 24580
  181.8 3.5 %copy-start.7 = (f32[128,512]{1,0:T(8,128)S(1)}, f32[128,512]{1,0:T(8,128)}, u32[]{:S(2)}) copy-start(f32[128,512]{1,0:T(8,128)} %get-tuple-element.56) | copy-start | bytes 786436
  186.1 4.3 %copy-start.3 = (bf16[512,512]{1,0:T(8,128)(2,1)S(1)}, bf16[512,512]{1,0:T(8,128)(2,1)}, u32[]{:S(2)}) copy-start(bf16[512,512]{1,0:T(8,128)(2,1)} %get-tuple-element.54.ggate_ref) | copy-start | bytes 1572868
  190.4 2.7 copy-start.12
  334.6 8.0 %copy-start.5 = (f32[64,2048]{1,0:T(8,128)S(1)}, f32[64,2048]{1,0:T(8,128)}, u32[]{:S(2)}) copy-start(f32[64,2048]{1,0:T(8,128)} %get-tuple-element.101) | copy-start | bytes 1572868
  334.6 8.8 %copy-start.4 = (f32[64,2048]{1,0:T(8,128)S(1)}, f32[64,2048]{1,0:T(8,128)}, u32[]{:S(2)}) copy-start(f32[64,2048]{1,0:T(8,128)} %get-tuple-element.102) | copy-start | bytes 1572868
  334.6 9.6 %copy-start.2 = (f32[128,2048]{1,0:T(8,128)S(1)}, f32[128,2048]{1,0:T(8,128)}, u32[]{:S(2)}) copy-start(f32[128,2048]{1,0:T(8,128)} %get-tuple-element.104) | copy-start | bytes 3145732
  342.6 2.6 copy-start.1
  344.2 1.9 copy-start.9
  344.3 2.6 copy-start

commit v3 on v1

--- a/solution.py
+++ b/solution.py
@@ -1,3 +1,5 @@
+import functools
+
 import jax
 import jax.numpy as jnp
 from jax import lax
@@ -11,8 +13,13 @@
 
 eps_norm = 1e-05
 
+
 def sigmoid(v):
     return 1.0 / (1.0 + jnp.exp(-v))
+
+
+def softplus(v):
+    return jnp.maximum(v, 0.0) + jnp.log(1.0 + jnp.exp(-jnp.abs(v)))
 
 
 def fold_rows(first, second, shift, lower):
@@ -162,20 +169,20 @@
         dbl_ref[...].astype(jnp.bfloat16), raw_low, (((0,), (0,)), ((), ())), preferred_element_type=jnp.float32
     )
     gdbl_ref[...] += lax.dot_general(
-        raw_low, dtp_ref[...], (((1,), (1,)), ((), ())), preferred_element_type=jnp.float32
-    )
-
-
-def scan_call(dbl, conv, gate, gg, dtp, dtb, alog, skip, keep, cb=512):
+        dtp_ref[...], raw_low, (((1,), (1,)), ((), ())), preferred_element_type=jnp.float32
+    )
+
+
+def scan_call(dbl, conv, gate, gg, dtp, dtb, alog, skip, keep):
     length, chans = conv.shape
-    cb = min(cb, chans)
+    cb = min(65536 // length, chans)
     f32 = jnp.float32
     maps = jnp.broadcast_to(dbl[:, R:, None], (length, 2 * N, 128))
     tokens = lambda kind: (jax.ShapeDtypeStruct((length, chans), kind), pl.BlockSpec((length, cb), lambda i: (0, i)))
     whole = lambda *shape: (jax.ShapeDtypeStruct(shape, f32), pl.BlockSpec(shape, lambda i: (0,) * len(shape)))
     rows = lambda count: (jax.ShapeDtypeStruct((count, chans), f32), pl.BlockSpec((count, cb), lambda i: (0, i)))
     outs = [
-        tokens(jnp.bfloat16), tokens(jnp.bfloat16), tokens(f32), whole(length, R), whole(length, N, 128), whole(length, N, 128),
+        tokens(jnp.bfloat16), tokens(jnp.bfloat16), tokens(f32), whole(R, length), whole(length, N, 128), whole(length, N, 128),
         rows(R), rows(1), rows(N), rows(1),
     ]
     ins = [
@@ -196,8 +203,843 @@
         compiler_params=pltpu.CompilerParams(vmem_limit_bytes=60 << 20),
     )(dbl[:, :R], conv, gate, gg, dtp, dtb[None], alog, skip[None], keep[:, None], maps, maps)
     gated, ggate, gconv, gdbl, gin, gout, gdtp, gdtb, galog, gskip = res
-    gdbl_all = jnp.concatenate([gdbl, jnp.sum(gin, -1), jnp.sum(gout, -1)], axis=1)
+    gdbl_all = jnp.concatenate([gdbl, jnp.sum(gin, -1).T, jnp.sum(gout, -1).T], axis=0)
     return gated, ggate, gconv, gdbl_all, gdtp, gdtb[0], galog, gskip[0]
+
+
+MESH = pl.DeviceIdType.MESH
+NZ = 4
+F32 = jnp.float32
+BF16 = jnp.bfloat16
+NN = (((1,), (0,)), ((), ()))
+NT = (((1,), (1,)), ((), ()))
+TN = (((0,), (0,)), ((), ()))
+
+
+def dot(left, right, dims=NN):
+    return lax.dot_general(left, right, dims, preferred_element_type=F32)
+
+
+def place(z, x, c):
+    return (z * 2 + x) * 2 + c
+
+
+class Spot:
+    def __init__(self):
+        self.dp = lax.axis_index("dp")
+        self.y = lax.axis_index("tensor")
+        self.z, self.x, self.c = self.dp // 4, (self.dp // 2) % 2, self.dp % 2
+        self.x_mate = (place(self.z, 1 - self.x, self.c), self.y)
+        self.c_mate = (place(self.z, self.x, 1 - self.c), self.y)
+        self.y_mate = (self.dp, 1 - self.y)
+
+    def z_at(self, offset):
+        return lax.rem(self.z + offset + NZ, NZ)
+
+    def on_line(self, z, y=None):
+        return (place(z, self.x, self.c), self.y if y is None else y)
+
+
+def greet(devices):
+    barrier = pltpu.get_barrier_semaphore()
+    for device in devices:
+        pl.semaphore_signal(barrier, inc=1, device_id=device, device_id_type=MESH)
+    pl.semaphore_wait(barrier, len(devices))
+
+
+class Copies:
+    def __init__(self, send_sems):
+        self.send_sems = send_sems
+        self.begun = []
+
+    def send(self, src, dst, recv_sem, device, when=None):
+        copy = pltpu.make_async_remote_copy(
+            src_ref=src, dst_ref=dst, send_sem=self.send_sems.at[len(self.begun)], recv_sem=recv_sem,
+            device_id=device, device_id_type=MESH,
+        )
+        self.begun.append((when, copy))
+        if when is None:
+            copy.start()
+        else:
+            pl.when(when)(copy.start)
+
+    def wait_sent(self):
+        for when, copy in self.begun:
+            if when is None:
+                copy.wait_send()
+            else:
+                pl.when(when)(copy.wait_send)
+
+
+def arrived(dst, recv_sem, when=None):
+    copy = pltpu.make_async_copy(dst, dst, recv_sem)
+    if when is None:
+        copy.wait()
+    else:
+        pl.when(when)(copy.wait)
+
+
+class Gather:
+    def __init__(self, spot, copies, src, dst, recv_sems, own_sem):
+        self.spot, self.copies, self.src, self.dst, self.recv_sems, self.own_sem = spot, copies, src, dst, recv_sems, own_sem
+        self.width = dst.shape[-1]
+
+    def columns(self, z):
+        return self.src.at[:, pl.ds(pl.multiple_of(z * self.width, self.width), self.width)]
+
+    def push(self):
+        spot, me = self.spot, self.spot.dp
+        for offset in range(1, NZ):
+            z = spot.z_at(offset)
+            self.copies.send(self.columns(z), self.dst.at[me], self.recv_sems.at[me], spot.on_line(z))
+        self.own = pltpu.make_async_copy(self.columns(spot.z), self.dst.at[me], self.own_sem)
+        self.own.start()
+
+    def pass_on(self, origin, device):
+        self.copies.send(self.dst.at[origin], self.dst.at[origin], self.recv_sems.at[origin], device)
+
+    def first(self):
+        spot = self.spot
+        for offset in range(NZ):
+            origin = place(spot.z_at(-offset), spot.x, spot.c)
+            if offset == 0:
+                self.own.wait()
+            else:
+                arrived(self.dst.at[origin], self.recv_sems.at[origin])
+            self.pass_on(origin, spot.x_mate)
+            self.pass_on(origin, spot.c_mate)
+
+    def second(self):
+        spot = self.spot
+        for offset in range(NZ):
+            origin = place(spot.z_at(-offset), 1 - spot.x, spot.c)
+            arrived(self.dst.at[origin], self.recv_sems.at[origin])
+            self.pass_on(origin, spot.c_mate)
+
+    def last(self):
+        spot = self.spot
+        for x in range(2):
+            for offset in range(NZ):
+                origin = place(spot.z_at(-offset), x, 1 - spot.c)
+                arrived(self.dst.at[origin], self.recv_sems.at[origin])
+
+
+class LineSum:
+    def __init__(self, spot, copies, part, landing, total, part_sems, total_sems):
+        self.spot, self.copies, self.part, self.landing, self.total = spot, copies, part, landing, total
+        self.part_sems, self.total_sems = part_sems, total_sems
+        self.offsets = [(dz, dy) for dz in range(NZ) for dy in range(2) if dz + dy > 0]
+
+    def there(self, dz, dy):
+        return self.spot.z_at(dz), lax.rem(self.spot.y + dy, 2)
+
+    def push(self):
+        for dz, dy in self.offsets:
+            z, y = self.there(dz, dy)
+            slot = dz * 2 + dy
+            self.copies.send(self.part.at[z, y], self.landing.at[slot], self.part_sems.at[slot], self.spot.on_line(z, y))
+
+    def middle(self):
+        own_z, own_y = self.spot.z, self.spot.y
+        summed = self.part[own_z, own_y]
+        for dz, dy in self.offsets:
+            slot = dz * 2 + dy
+            arrived(self.landing.at[slot], self.part_sems.at[slot])
+            summed = summed + self.landing[slot]
+        self.total[own_z, own_y] = summed
+        own = self.total.at[own_z, own_y]
+        for dz, dy in self.offsets:
+            z, y = self.there(dz, dy)
+            self.copies.send(own, own, self.total_sems.at[own_z, own_y], self.spot.on_line(z, y))
+
+    def last(self):
+        for dz, dy in self.offsets:
+            z, y = self.there(dz, dy)
+            arrived(self.total.at[z, y], self.total_sems.at[z, y])
+
+
+def column_masks(tile):
+    return jnp.concatenate([tile] * 16, axis=0).T
+
+
+class Share:
+    def __init__(self, spot, copies, dst, recv_sems):
+        self.spot, self.copies, self.dst, self.recv_sems = spot, copies, dst, recv_sems
+
+    def send(self, z, device, when=None):
+        y = self.spot.y
+        self.copies.send(self.dst.at[z, y], self.dst.at[z, y], self.recv_sems.at[z, y], device, when)
+
+    def push(self):
+        spot = self.spot
+        self.send(spot.z, spot.on_line(spot.z_at(1)), spot.z < NZ - 1)
+        self.send(spot.z, spot.on_line(spot.z_at(-1)), spot.z > 0)
+        self.send(spot.z, spot.y_mate)
+
+    def first(self, far):
+        spot = self.spot
+        for way in (1, -1):
+            origin = spot.z_at(-way * far)
+            comes = spot.z >= far if way == 1 else spot.z < NZ - far
+            goes = comes & (spot.z < NZ - 1 if way == 1 else spot.z > 0)
+            arrived(self.dst.at[origin, spot.y], self.recv_sems.at[origin, spot.y], comes)
+            if far < NZ - 1:
+                self.send(origin, spot.on_line(spot.z_at(way)), goes)
+            self.send(origin, spot.y_mate, comes)
+
+    def last(self):
+        spot = self.spot
+        for offset in range(NZ):
+            z = spot.z_at(-offset)
+            arrived(self.dst.at[z, 1 - spot.y], self.recv_sems.at[z, 1 - spot.y])
+
+
+class Scan:
+    def __init__(self, maps, a_s, stepd_s, drive_s, gs_s, read_s, q_s, r_s, state_s, pulled_s, alog_s, spread_s, sum_s, gmap_s):
+        self.maps, self.a_s, self.stepd_s, self.drive_s, self.gs_s = maps, a_s, stepd_s, drive_s, gs_s
+        self.read_s, self.q_s, self.r_s, self.state_s = read_s, q_s, r_s, state_s
+        self.pulled_s, self.alog_s, self.spread_s, self.sum_s, self.gmap_s = pulled_s, alog_s, spread_s, sum_s, gmap_s
+        sub = lax.broadcasted_iota(jnp.int32, (8, 128), 0)
+        self.masks = [(sub & shift) == 0 for shift in (1, 2, 4)]
+        self.lane = lax.broadcasted_iota(jnp.int32, (N, 128), 1)
+        self.blocks = [slice(b * 128, (b + 1) * 128) for b in range(a_s.shape[1] // 128)]
+
+    def place(self, i):
+        base = pl.multiple_of(i * 8, 8)
+        tile = pl.ds(pl.multiple_of((base // 128) * 128, 128), 128)
+        return base, tile, lax.rem(base, 128)
+
+    def spread(self, tile, first):
+        back = lax.rem(128 - first, 128)
+        for k in range(2):
+            moved = pltpu.roll(self.maps[k * N : (k + 1) * N, tile], back, 1)
+            for j in range(8):
+                self.spread_s[k, j] = jnp.broadcast_to(moved[:, j : j + 1], (N, 128))
+
+    def forward(self, start, stop):
+        def chunk(i, none):
+            base, tile, first = self.place(i)
+            self.spread(tile, first)
+            for lanes in self.blocks:
+                state = self.state_s[i, :, lanes]
+                a = self.a_s[:, lanes]
+                stepd, drive = self.stepd_s[pl.ds(base, 8), lanes], self.drive_s[pl.ds(base, 8), lanes]
+                sums = RowSums(self.masks)
+                for j in range(8):
+                    state = jnp.exp(stepd[j : j + 1] * a) * state + drive[j : j + 1] * self.spread_s[0, j]
+                    read = state * self.spread_s[1, j]
+                    sums.add(j, read[:8] + read[8:])
+                self.state_s[i + 1, :, lanes] = state
+                self.read_s[pl.ds(base, 8), lanes] = sums.result
+            return none
+
+        lax.fori_loop(start, stop, chunk, 0)
+
+    def backward(self, start, stop):
+        def chunk(step, none):
+            i = start + stop - 1 - step
+            base, tile, first = self.place(i)
+            self.spread(tile, first)
+            for b, lanes in enumerate(self.blocks):
+                a = self.a_s[:, lanes]
+                stepd, drive = self.stepd_s[pl.ds(base, 8), lanes], self.drive_s[pl.ds(base, 8), lanes]
+                gs = self.gs_s[pl.ds(base, 8), lanes]
+                states, decays = [self.state_s[i, :, lanes]], []
+                for j in range(8):
+                    decays.append(jnp.exp(stepd[j : j + 1] * a))
+                    states.append(decays[j] * states[j] + drive[j : j + 1] * self.spread_s[0, j])
+                pulled, alog = self.pulled_s[:, lanes], self.alog_s[:, lanes]
+                q_sums, r_sums = RowSums(self.masks), RowSums(self.masks)
+                for j in reversed(range(8)):
+                    adjoint = pulled + self.spread_s[1, j] * gs[j : j + 1]
+                    g_in, g_out = adjoint * drive[j : j + 1], states[j + 1] * gs[j : j + 1]
+                    if b > 0:
+                        g_in, g_out = g_in + self.sum_s[0, j], g_out + self.sum_s[1, j]
+                    self.sum_s[0, j], self.sum_s[1, j] = g_in, g_out
+                    q_t = adjoint * self.spread_s[0, j]
+                    q_sums.add(j, q_t[:8] + q_t[8:])
+                    pulled = decays[j] * adjoint
+                    past = pulled * states[j]
+                    r_t = past * a
+                    r_sums.add(j, r_t[:8] + r_t[8:])
+                    alog = alog + past * stepd[j : j + 1]
+                self.pulled_s[:, lanes], self.alog_s[:, lanes] = pulled, alog
+                self.q_s[pl.ds(base, 8), lanes] = q_sums.result
+                self.r_s[pl.ds(base, 8), lanes] = r_sums.result
+            for k in range(2):
+                row = self.gmap_s[k * N : (k + 1) * N, tile]
+                for j in range(8):
+                    row = jnp.where(self.lane == first + j, jnp.sum(self.sum_s[k, j], axis=1, keepdims=True), row)
+                self.gmap_s[k * N : (k + 1) * N, tile] = row
+            return none
+
+        lax.fori_loop(start, stop, chunk, 0)
+
+
+class TokenSum:
+    def __init__(self, spot, copies, part, y_land, z_land, y_sems, z_sems):
+        self.spot, self.copies, self.part, self.y_land, self.z_land = spot, copies, part, y_land, z_land
+        self.y_sems, self.z_sems = y_sems, z_sems
+
+    def push(self):
+        spot = self.spot
+        for offset in (1, 2, 3, 0):
+            z = spot.z_at(offset)
+            self.copies.send(self.part.at[z, 1 - spot.y], self.y_land.at[z], self.y_sems.at[z], spot.y_mate)
+
+    def middle(self):
+        spot = self.spot
+        for offset in (1, 2, 3):
+            z = spot.z_at(offset)
+            arrived(self.y_land.at[z], self.y_sems.at[z])
+            self.part[z, spot.y] = (self.part[z, spot.y].astype(F32) + self.y_land[z].astype(F32)).astype(BF16)
+            self.copies.send(self.part.at[z, spot.y], self.z_land.at[offset - 1], self.z_sems.at[offset - 1], spot.on_line(z))
+
+    def last(self):
+        spot = self.spot
+        arrived(self.y_land.at[spot.z], self.y_sems.at[spot.z])
+        summed = self.part[spot.z, spot.y].astype(F32) + self.y_land[spot.z].astype(F32)
+        for k in range(NZ - 1):
+            arrived(self.z_land.at[k], self.z_sems.at[k])
+            summed = summed + self.z_land[k].astype(F32)
+        return summed
+
+
+class RowSum:
+    def __init__(self, spot, copies, part, c_land, x_land, z_land, c_sems, x_sems, z_sems):
+        self.spot, self.copies, self.part = spot, copies, part
+        self.c_land, self.x_land, self.z_land = c_land, x_land, z_land
+        self.c_sems, self.x_sems, self.z_sems = c_sems, x_sems, z_sems
+
+    def push(self):
+        spot = self.spot
+        for offset in (1, 2, 3, 0):
+            z = spot.z_at(offset)
+            for x in (1 - spot.x, spot.x):
+                self.copies.send(self.part.at[z, x, 1 - spot.c], self.c_land.at[z, x], self.c_sems.at[z, x], spot.c_mate)
+
+    def add(self, z, x, landed):
+        part = self.part
+        part[z, x, self.spot.c] = (part[z, x, self.spot.c].astype(F32) + landed.astype(F32)).astype(part.dtype)
+
+    def second(self):
+        spot = self.spot
+        for offset in (1, 2, 3, 0):
+            z = spot.z_at(offset)
+            for x in (1 - spot.x, spot.x):
+                arrived(self.c_land.at[z, x], self.c_sems.at[z, x])
+                self.add(z, x, self.c_land[z, x])
+            self.copies.send(self.part.at[z, 1 - spot.x, spot.c], self.x_land.at[z], self.x_sems.at[z], spot.x_mate)
+
+    def third(self):
+        spot = self.spot
+        for offset in (1, 2, 3, 0):
+            z = spot.z_at(offset)
+            arrived(self.x_land.at[z], self.x_sems.at[z])
+            self.add(z, spot.x, self.x_land[z])
+            if offset:
+                self.copies.send(
+                    self.part.at[z, spot.x, spot.c], self.z_land.at[spot.z], self.z_sems.at[spot.z], spot.on_line(z)
+                )
+        self.z_land[spot.z] = self.part[spot.z, spot.x, spot.c]
+
+    def last(self):
+        spot = self.spot
+        for offset in (1, 2, 3):
+            z = spot.z_at(-offset)
+            arrived(self.z_land.at[z], self.z_sems.at[z])
+
+
+class ChannelSum:
+    def __init__(self, spot, copies, part, c_land, x_land, full, c_sem, x_sem, full_sems):
+        self.spot, self.copies, self.part, self.full, self.full_sems = spot, copies, part, full, full_sems
+        self.c_land, self.x_land, self.c_sem, self.x_sem = c_land, x_land, c_sem, x_sem
+
+    def push(self):
+        self.copies.send(self.part.at[1 - self.spot.c], self.c_land, self.c_sem, self.spot.c_mate)
+
+    def second(self):
+        spot = self.spot
+        arrived(self.c_land, self.c_sem)
+        self.part[spot.c] = self.part[spot.c] + self.c_land[...]
+        self.copies.send(self.part.at[spot.c, 1 - spot.x], self.x_land, self.x_sem, spot.x_mate)
+
+    def spread(self, origin, device):
+        self.copies.send(self.full.at[origin], self.full.at[origin], self.full_sems.at[origin], device)
+
+    def third(self):
+        spot = self.spot
+        arrived(self.x_land, self.x_sem)
+        self.full[spot.dp] = self.part[spot.c, spot.x] + self.x_land[...]
+        for offset in (1, 2, 3):
+            self.spread(spot.dp, spot.on_line(spot.z_at(offset)))
+        self.spread(spot.dp, spot.x_mate)
+        self.spread(spot.dp, spot.c_mate)
+
+    def fourth(self):
+        spot = self.spot
+        for offset in (1, 2, 3):
+            origin = place(spot.z_at(-offset), spot.x, spot.c)
+            arrived(self.full.at[origin], self.full_sems.at[origin])
+            self.spread(origin, spot.x_mate)
+            self.spread(origin, spot.c_mate)
+
+    def fifth(self):
+        spot = self.spot
+        for offset in range(NZ):
+            origin = place(spot.z_at(-offset), 1 - spot.x, spot.c)
+            arrived(self.full.at[origin], self.full_sems.at[origin])
+            self.spread(origin, spot.c_mate)
+
+    def last(self):
+        spot = self.spot
+        for x in range(2):
+            for offset in range(NZ):
+                origin = place(spot.z_at(-offset), x, 1 - spot.c)
+                arrived(self.full.at[origin], self.full_sems.at[origin])
+
+
+class Held:
+    def __init__(self, names, refs):
+        for name, ref in zip(names, refs, strict=True):
+            setattr(self, name, ref)
+
+
+def block_scratch(half, feats, rows, chans, step_rows, width):
+    tokens, n_dp, length = 2 * half * NZ, 4 * NZ, 2 * half
+    vmem, dma = pltpu.VMEM, pltpu.SemaphoreType.DMA
+    owners, steps = (NZ, 2, 2, rows, chans), (NZ, 2, 2, step_rows, chans)
+    part = (NZ, 2, width // 2, length)
+    small = (width + 32) // 4
+    held = {
+        "w": vmem((3, n_dp, rows, chans), BF16),
+        "acts": vmem((2, NZ, 2, half, feats), BF16),
+        "dtp_own": vmem((step_rows, chans * NZ), F32),
+        "dtp": vmem((n_dp, step_rows, chans), F32),
+        "info": vmem((n_dp, 8, 128), F32),
+        "mask": vmem((NZ, length, 128), F32),
+        "low": vmem((tokens, chans), BF16),
+        "gated": vmem((tokens, chans), BF16),
+        "ggate": vmem((tokens, chans), BF16),
+    }
+    for name in ("x_in", "pre", "gate", "gg", "raw", "stepd", "drive", "gs", "read", "r"):
+        held[name] = vmem((tokens, chans), F32)
+    held |= {
+        "a": vmem((N, chans), F32),
+        "state": vmem((tokens // 8 + 1, N, chans), F32),
+        "pulled": vmem((N, chans), F32),
+        "alog": vmem((N, chans), F32),
+        "spread": vmem((2, 8, N, 128), F32),
+        "sum": vmem((2, 8, N, 128), F32),
+        "gmap": vmem((2 * N, tokens), F32),
+        "dbl": vmem((width, tokens), F32),
+        "part": vmem(part, F32),
+        "landing": vmem((2 * NZ,) + part[2:], F32),
+        "total": vmem(part, F32),
+        "gpart": vmem(part, F32),
+        "glanding": vmem((2 * NZ,) + part[2:], F32),
+        "gtotal": vmem(part, F32),
+        "mixed": vmem((NZ, 2, half, feats), BF16),
+        "normed": vmem((NZ, 2, half, feats), BF16),
+        "outw": vmem(owners, BF16),
+        "ginz": vmem(owners, BF16),
+        "ginx": vmem(owners, BF16),
+        "gdtp": vmem(steps, F32),
+        "chan": vmem((2, 2, small, chans), F32),
+        "y_land": vmem((2, NZ, half, feats), BF16),
+        "z_land": vmem((2, NZ - 1, half, feats), BF16),
+        "wc_land": vmem((3, NZ, 2, rows, chans), BF16),
+        "wx_land": vmem((3, NZ, rows, chans), BF16),
+        "dc_land": vmem((NZ, 2, step_rows, chans), F32),
+        "dx_land": vmem((NZ, step_rows, chans), F32),
+        "fc_land": vmem((2, small, chans), F32),
+        "fx_land": vmem((small, chans), F32),
+        "tile": vmem((4, 8, 128), F32),
+        "gain": vmem((3, n_dp, 8, 128), F32),
+        "gain_land": vmem((n_dp - 1, 8, 128), F32),
+        "send_sems": dma((288,)),
+        "own_sems": dma((4,)),
+        "w_sems": dma((4, n_dp)),
+        "act_sems": dma((2, NZ, 2)),
+        "info_sems": dma((n_dp,)),
+        "part_sems": dma((2, 2 * NZ)),
+        "total_sems": dma((2, NZ, 2)),
+        "y_sems": dma((2, NZ)),
+        "z_sems": dma((2, NZ - 1)),
+        "wc_sems": dma((4, NZ, 2)),
+        "wx_sems": dma((4, NZ)),
+        "wz_sems": dma((4, NZ)),
+        "f_sems": dma((2,)),
+        "full_sems": dma((n_dp,)),
+        "tile_sems": dma((2,)),
+        "gain_sems": dma((n_dp,)),
+    }
+    return held
+
+
+def block_kernel(names, *refs):
+    (
+        inx_ref, inz_ref, outp_ref, resid_ref, cot_ref, gain_ref, ids_ref, dtp_ref, xproj_ref, convw_ref, convb_ref, dtb_ref,
+        alog_ref, skip_ref,
+        block_ref, gresid_ref, ggain_ref, ginx_ref, ginz_ref, goutp_ref, gdtp_ref, full_ref, square_ref, msquare_ref,
+    ) = refs[:24]
+    s = Held(names, refs[24:])
+    spot = Spot()
+    plane = [lax.rem(spot.dp + offset, 4 * NZ) for offset in range(1, 4 * NZ)]
+    greet([(dp, spot.y) for dp in plane] + [spot.on_line(spot.z_at(dz), 1 - spot.y) for dz in range(NZ)])
+    copies = Copies(s.send_sems)
+    tokens, chans = s.x_in.shape
+    half, feats = resid_ref.shape
+    length = 2 * half
+    columns = pl.ds(pl.multiple_of(spot.z * chans, chans), chans)
+    sequences = [slice(k * length, (k + 1) * length) for k in range(NZ)]
+
+    s.dtp_own[...] = dtp_ref[...].astype(F32)
+    inx, inz, outp, dtp = (
+        Gather(spot, copies, src, dst, s.w_sems.at[k], s.own_sems.at[k])
+        for k, (src, dst) in enumerate(((inx_ref, s.w.at[0]), (inz_ref, s.w.at[1]), (outp_ref, s.w.at[2]), (s.dtp_own, s.dtp)))
+    )
+    normed, cot = (Share(spot, copies, s.acts.at[k], s.act_sems.at[k]) for k in range(2))
+
+    ids = jnp.broadcast_to(ids_ref[...], (8, length))
+    lane = lax.broadcasted_iota(jnp.int32, (8, length), 1)
+    sub = lax.broadcasted_iota(jnp.int32, (8, length), 0)
+    info = jnp.broadcast_to(gain_ref[...].astype(F32), (8, length))
+    for back in range(1, 4):
+        same = jnp.where((pltpu.roll(ids, back, 1) == ids) & (lane >= back), 1.0, 0.0)
+        info = jnp.where(sub == back, same, info)
+    s.info[spot.dp] = info
+    for dp in plane:
+        copies.send(s.info.at[spot.dp], s.info.at[spot.dp], s.info_sems.at[spot.dp], (dp, spot.y))
+    inx.push()
+
+    resid = resid_ref[...]
+    row_square = jnp.sum(resid * resid, axis=1, keepdims=True)
+    scaled = resid * lax.rsqrt(row_square / feats + eps_norm)
+    s.tile[0] = jnp.broadcast_to(jnp.sum(row_square, axis=0, keepdims=True), (8, 128))
+    copies.send(s.tile.at[0], s.tile.at[1], s.tile_sems.at[0], spot.y_mate)
+    for dp in plane:
+        arrived(s.info.at[dp], s.info_sems.at[dp])
+    for k in range(4 * NZ):
+        cols = slice(k * 128, (k + 1) * 128)
+        s.acts[0, spot.z, spot.y, :, cols] = (scaled[:, cols] * s.info[k, 0:1, :]).astype(BF16)
+    normed.push()
+    dtp.push()
+    s.acts[1, spot.z, spot.y] = cot_ref[...].astype(BF16)
+    for k in range(NZ):
+        s.mask[k] = column_masks(s.info[place(k, spot.x, spot.c)])
+    inx.first()
+    inz.push()
+    normed.first(1)
+    inx.second()
+    cot.push()
+    normed.first(2)
+    dtp.first()
+    dtp.second()
+    normed.first(3)
+    inz.first()
+    outp.push()
+    normed.last()
+    inx.last()
+
+    tokens_x = s.acts.at[0], s.acts.at[1]
+    all_normed = s.acts[0].reshape(tokens, feats)
+    s.x_in[...] = dot(all_normed, s.w[0].reshape(-1, chans))
+    taps = convw_ref[:, columns]
+    bias = convb_ref[:, columns]
+    for k, rows in enumerate(sequences):
+        one = s.x_in[rows]
+        pre = bias + taps[3:4] * one
+        for back in range(1, 4):
+            pre = pre + taps[3 - back : 4 - back] * (pltpu.roll(one, back, 0) * s.mask[k, :, back : back + 1])
+        s.pre[rows] = pre
+        s.low[rows] = (pre * sigmoid(pre)).astype(BF16)
+    x_proj = xproj_ref[:, columns]
+    dbl = dot(x_proj, s.low[...], NT)
+    blocks = [(k, y) for k in range(NZ) for y in range(2)]
+    width = dbl.shape[0] // 2
+    for k, y in blocks:
+        s.part[k, y] = dbl[y * width : (y + 1) * width, sequences[k]]
+    x_dbl = LineSum(spot, copies, s.part, s.landing, s.total, s.part_sems.at[0], s.total_sems.at[0])
+    x_dbl.push()
+    cot.first(1)
+    inz.second()
+    x_dbl.middle()
+    cot.first(2)
+    outp.first()
+    dtp.last()
+    x_dbl.last()
+
+    for k, y in blocks:
+        s.dbl[y * width : (y + 1) * width, sequences[k]] = s.total[k, y]
+    step_w = s.dtp[...].reshape(R, chans).astype(BF16)
+    s.raw[...] = split_dot(s.dbl[:R], step_w, TN) + dtb_ref[:, columns]
+    for k, rows in enumerate(sequences):
+        step = softplus(s.raw[rows])
+        s.stepd[rows] = jnp.where(s.mask[k, :, 1:2] > 0.0, step, 1e30)
+        s.drive[rows] = step * s.low[rows].astype(F32)
+    s.a[...] = -jnp.exp(alog_ref[:, columns])
+    s.state[0] = jnp.zeros((N, chans), F32)
+    scan = Scan(
+        s.dbl.at[R : R + 2 * N], s.a, s.stepd, s.drive, s.gs, s.read, s.read, s.r, s.state, s.pulled, s.alog, s.spread, s.sum, s.gmap
+    )
+    steps = tokens // 8
+    scan.forward(0, steps // 4)
+    cot.first(3)
+    outp.second()
+    scan.forward(steps // 4, steps)
+    inz.last()
+    s.gate[...] = dot(s.acts[0].reshape(tokens, feats), s.w[1].reshape(-1, chans))
+    cot.last()
+    outp.last()
+    s.gg[...] = dot(s.acts[1].reshape(tokens, feats), s.w[2].reshape(-1, chans))
+    skip = skip_ref[:, columns]
+    for rows in sequences:
+        gate, gg = s.gate[rows], s.gg[rows]
+        sig = sigmoid(gate)
+        scanned = s.read[rows] + skip * s.low[rows].astype(F32)
+        s.gs[rows] = gg * gate * sig
+        s.gated[rows] = (scanned * gate * sig).astype(BF16)
+        s.ggate[rows] = (gg * scanned * sig * (1.0 + gate * (1.0 - sig))).astype(BF16)
+
+    mixed_sum, normed_sum = (
+        TokenSum(spot, copies, part, s.y_land.at[k], s.z_land.at[k], s.y_sems.at[k], s.z_sems.at[k])
+        for k, part in enumerate((s.mixed, s.normed))
+    )
+    outw_sum, ginz_sum, ginx_sum, gdtp_sum = (
+        RowSum(spot, copies, part, c_land, x_land, out, s.wc_sems.at[k], s.wx_sems.at[k], s.wz_sems.at[k])
+        for k, (part, c_land, x_land, out) in enumerate((
+            (s.outw, s.wc_land.at[0], s.wx_land.at[0], goutp_ref),
+            (s.ginz, s.wc_land.at[1], s.wx_land.at[1], ginz_ref),
+            (s.ginx, s.wc_land.at[2], s.wx_land.at[2], ginx_ref),
+            (s.gdtp, s.dc_land, s.dx_land, gdtp_ref),
+        ))
+    )
+    s.mixed[...] = dot(s.gated[...], s.w[2].reshape(-1, chans), NT).astype(BF16).reshape(s.mixed.shape)
+    mixed_sum.push()
+    s.outw[...] = dot(s.acts[1].reshape(tokens, feats), s.gated[...], TN).astype(BF16).reshape(s.outw.shape)
+    outw_sum.push()
+    s.ginz[...] = dot(s.acts[0].reshape(tokens, feats), s.ggate[...], TN).astype(BF16).reshape(s.ginz.shape)
+    ginz_sum.push()
+
+    s.pulled[...] = jnp.zeros_like(s.pulled)
+    s.alog[...] = jnp.zeros_like(s.alog)
+    outw_sum.second()
+    scan.backward(steps - steps // 4, steps)
+    ginz_sum.second()
+    mixed_sum.middle()
+    scan.backward(steps // 2, steps - steps // 4)
+    outw_sum.third()
+    scan.backward(steps // 4, steps // 2)
+    ginz_sum.third()
+    scan.backward(0, steps // 4)
+
+    grad_bias = jnp.zeros((1, chans), F32)
+    grad_skip = jnp.zeros((1, chans), F32)
+    raw_rows = []
+    for rows in sequences:
+        conv, raw, gs, q = s.low[rows].astype(F32), s.raw[rows], s.gs[rows], s.read[rows]
+        grad_raw = (conv * q + s.r[rows]) * sigmoid(raw)
+        s.gg[rows] = softplus(raw) * q + skip * gs
+        grad_bias = grad_bias + jnp.sum(grad_raw, axis=0, keepdims=True)
+        grad_skip = grad_skip + jnp.sum(gs * conv, axis=0, keepdims=True)
+        raw_rows.append(grad_raw.astype(BF16))
+    raw_low = jnp.concatenate(raw_rows, axis=0)
+    dbl = jnp.concatenate([dot(step_w, raw_low, NT), s.gmap[...]], axis=0)
+    for k, y in blocks:
+        s.gpart[k, y] = dbl[y * width : (y + 1) * width, sequences[k]]
+    grad_dbl_sum = LineSum(spot, copies, s.gpart, s.glanding, s.gtotal, s.part_sems.at[1], s.total_sems.at[1])
+    grad_dbl_sum.push()
+    s.gdtp[...] = dot(s.dbl[:R].astype(BF16), raw_low).reshape(s.gdtp.shape)
+    gdtp_sum.push()
+    grad_dbl_sum.middle()
+    gdtp_sum.second()
+    grad_dbl_sum.last()
+
+    grad_dbl = jnp.concatenate(
+        [jnp.concatenate([s.gtotal[k, y] for k in range(NZ)], axis=1) for y in range(2)], axis=0
+    ).astype(BF16)
+    s.gg[...] += dot(grad_dbl, x_proj, TN)
+    sums = [jnp.zeros((1, chans), F32) for _ in range(5)]
+    low_rows = []
+    for k, rows in enumerate(sequences):
+        pre, x_one = s.pre[rows], s.x_in[rows]
+        sig = sigmoid(pre)
+        one = s.gg[rows] * sig * (1.0 + pre * (1.0 - sig))
+        sums[3] = sums[3] + jnp.sum(one * x_one, axis=0, keepdims=True)
+        sums[4] = sums[4] + jnp.sum(one, axis=0, keepdims=True)
+        grad_x = taps[3:4] * one
+        for back in range(1, 4):
+            masked = one * s.mask[k, :, back : back + 1]
+            sums[3 - back] = sums[3 - back] + jnp.sum(masked * pltpu.roll(x_one, back, 0), axis=0, keepdims=True)
+            grad_x = grad_x + taps[3 - back : 4 - back] * pltpu.roll(masked, length - back, 0)
+        low_rows.append(grad_x.astype(BF16))
+    grad_xin = jnp.concatenate(low_rows, axis=0)
+    s.normed[...] = (
+        dot(grad_xin, s.w[0].reshape(-1, chans), NT) + dot(s.ggate[...], s.w[1].reshape(-1, chans), NT)
+    ).astype(BF16).reshape(s.normed.shape)
+    normed_sum.push()
+    s.ginx[...] = dot(s.acts[0].reshape(tokens, feats), grad_xin, TN).astype(BF16).reshape(s.ginx.shape)
+    ginx_sum.push()
+    s.chan[...] = jnp.concatenate(
+        [dot(grad_dbl, s.low[...]), s.alog[...] * s.a[...], grad_bias, grad_skip, jnp.zeros((6, chans), F32)]
+        + sums + [jnp.zeros((3, chans), F32)], axis=0
+    ).reshape(s.chan.shape)
+    small_sum = ChannelSum(
+        spot, copies, s.chan, s.fc_land, s.fx_land, full_ref, s.f_sems.at[0], s.f_sems.at[1], s.full_sems
+    )
+    small_sum.push()
+    ginx_sum.second()
+    gdtp_sum.third()
+    small_sum.second()
+    normed_sum.middle()
+    small_sum.third()
+    ginx_sum.third()
+
+    mixed = mixed_sum.last()
+    resid = resid_ref[...]
+    block_ref[...] = resid + mixed
+    s.tile[2] = jnp.broadcast_to(jnp.sum(jnp.sum(mixed * mixed, axis=1, keepdims=True), axis=0, keepdims=True), (8, 128))
+    copies.send(s.tile.at[2], s.tile.at[3], s.tile_sems.at[1], spot.y_mate)
+    small_sum.fourth()
+    outw_sum.last()
+    ginz_sum.last()
+    gdtp_sum.last()
+    small_sum.fifth()
+
+    grad_rows = normed_sum.last()
+    inv = lax.rsqrt(jnp.sum(resid * resid, axis=1, keepdims=True) / feats + eps_norm)
+    scaled = resid * inv
+    gain_part = jnp.sum(grad_rows * scaled, axis=0, keepdims=True)
+    for k in range(4 * NZ):
+        s.gain[0, k] = jnp.broadcast_to(gain_part[:, k * 128 : (k + 1) * 128], (8, 128))
+    copies.send(s.gain.at[0], s.gain.at[1], s.gain_sems.at[4 * NZ - 1], spot.y_mate)
+    gain = jnp.concatenate([s.info[k, 0:1] for k in range(4 * NZ)], axis=1)
+    grad_scaled = grad_rows * gain
+    mean = jnp.sum(grad_scaled * scaled, axis=1, keepdims=True) / feats
+    gresid_ref[...] = cot_ref[...] + inv * (grad_scaled - scaled * mean)
+    arrived(s.gain.at[1], s.gain_sems.at[4 * NZ - 1])
+    s.gain[2] = s.gain[0] + s.gain[1]
+    for offset, dp in enumerate(plane):
+        copies.send(s.gain.at[2, dp], s.gain_land.at[offset], s.gain_sems.at[offset], (dp, spot.y))
+    arrived(s.tile.at[1], s.tile_sems.at[0])
+    square_ref[...] = s.tile[0] + s.tile[1]
+    arrived(s.tile.at[3], s.tile_sems.at[1])
+    msquare_ref[...] = s.tile[2] + s.tile[3]
+    ginx_sum.last()
+    small_sum.last()
+    total = s.gain[2, spot.dp]
+    for offset in range(4 * NZ - 1):
+        arrived(s.gain_land.at[offset], s.gain_sems.at[offset])
+        total = total + s.gain_land[offset]
+    ggain_ref[...] = total
+    copies.wait_sent()
+
+
+def block_call(in_x, in_z, out_p, residual, cotangent, gain, ids, dt_p, x_proj, conv_w, conv_b, dt_b, a_log, d_skip):
+    half, feats = residual.shape
+    rows, wide = in_x.shape
+    n_dp, chans = 4 * NZ, wide // NZ
+    held = block_scratch(half, feats, rows, chans, dt_p.shape[0], x_proj.shape[0])
+    shape = jax.ShapeDtypeStruct
+    outs = [
+        shape((half, feats), F32), shape((half, feats), F32), shape((8, 128), F32),
+        shape((NZ, rows, chans), BF16), shape((NZ, rows, chans), BF16), shape((NZ, rows, chans), BF16),
+        shape((NZ, dt_p.shape[0], chans), F32), shape((n_dp, (x_proj.shape[0] + 32) // 4, chans), F32),
+        shape((8, 128), F32), shape((8, 128), F32),
+    ]
+    in_any = pl.BlockSpec(memory_space=pl.ANY)
+    in_vmem = pl.BlockSpec(memory_space=pltpu.VMEM)
+    return pl.pallas_call(
+        functools.partial(block_kernel, list(held)),
+        out_shape=outs,
+        in_specs=[in_any] * 3 + [in_vmem] * 11,
+        out_specs=[in_vmem] * len(outs),
+        scratch_shapes=list(held.values()),
+        name="block",
+        compiler_params=pltpu.CompilerParams(collective_id=1, has_side_effects=True, vmem_limit_bytes=62 << 20),
+    )(in_x, in_z, out_p, residual, cotangent, gain, ids, dt_p, x_proj, conv_w, conv_b, dt_b, a_log, d_skip)
+
+
+def finish_kernel(
+    block_in, gresid_in, ginx_in, ginz_in, goutp_in, gdtp_in, full_in,
+    block_ref, gresid_ref, ginx_ref, ginz_ref, goutp_ref, gdtp_ref, xproj_ref, alog_ref, dtb_ref, skip_ref, convw_ref, convb_ref,
+):
+    block_ref[...] = block_in[...]
+    gresid_ref[...] = gresid_in[...]
+    chans = ginx_in.shape[2]
+    for z in range(NZ):
+        cols = slice(z * chans, (z + 1) * chans)
+        for given, ref in ((ginx_in, ginx_ref), (ginz_in, ginz_ref), (goutp_in, goutp_ref), (gdtp_in, gdtp_ref)):
+            ref[:, cols] = given[z].astype(F32)
+        rows = full_in.shape[1]
+        for k in range(4):
+            origin = place(z, k % 2, k // 2)
+            upto = min(rows, xproj_ref.shape[0] - k * rows)
+            xproj_ref[k * rows : k * rows + upto, cols] = full_in[origin, :upto]
+        last = place(z, 1, 1)
+        alog_ref[:, cols] = full_in[last, upto : upto + N]
+        dtb_ref[:, cols] = full_in[last, upto + N : upto + N + 1]
+        skip_ref[:, cols] = full_in[last, upto + N + 1 : upto + N + 2]
+        convw_ref[:, cols] = full_in[last, upto + 24 : upto + 28]
+        convb_ref[:, cols] = full_in[last, upto + 28 : upto + 29]
+
+
+def finish_call(block, gresid, ginx, ginz, goutp, gdtp, full, width):
+    rows, wide = ginx.shape[1], ginx.shape[2] * NZ
+    shape = lambda count: jax.ShapeDtypeStruct((count, wide), F32)
+    outs = [
+        jax.ShapeDtypeStruct(block.shape, F32), jax.ShapeDtypeStruct(gresid.shape, F32), shape(rows), shape(rows), shape(rows),
+        shape(gdtp.shape[1]), shape(width), shape(N), shape(1), shape(1), shape(4), shape(1),
+    ]
+    spec = pl.BlockSpec(memory_space=pltpu.VMEM)
+    return pl.pallas_call(
+        finish_kernel, out_shape=outs, in_specs=[spec] * 7, out_specs=[spec] * len(outs), name="finish",
+        compiler_params=pltpu.CompilerParams(vmem_limit_bytes=40 << 20),
+    )(block, gresid, ginx, ginz, goutp, gdtp, full)
+
+
+def per_device_split(
+    residual,
+    norm_gain,
+    in_proj_x,
+    in_proj_z,
+    x_proj,
+    dt_proj,
+    dt_bias,
+    conv_weight,
+    conv_bias,
+    a_log,
+    d_skip,
+    out_proj,
+    doc_ids,
+    cotangent,
+):
+    block, gresid, grad_gain, ginx, ginz, goutp, gdtp, full, resid_square, mixed_square = block_call(
+        in_proj_x, in_proj_z, out_proj, residual, cotangent, norm_gain[None], doc_ids[None], dt_proj, x_proj, conv_weight,
+        conv_bias[None], dt_bias[None], a_log, d_skip[None],
+    )
+    block, gresid, ginx, ginz, goutp, gdtp, g_xproj, g_alog, g_dtb, g_skip, g_convw, g_convb = finish_call(
+        block, gresid, ginx, ginz, goutp, gdtp, full, x_proj.shape[0]
+    )
+    rms_resid, rms_mixed = (jnp.sqrt(v[0, :1] / (doc_ids.shape[0] * D)) for v in (resid_square, mixed_square))
+    return (
+        block,
+        gresid,
+        grad_gain[0],
+        ginx,
+        ginz,
+        g_xproj,
+        gdtp,
+        g_dtb[0],
+        g_convw,
+        g_convb[0],
+        g_alog,
+        g_skip[0],
+        goutp,
+        rms_resid,
+        rms_mixed,
+    )
 
 
 def norm_rows(values, gain_val):
@@ -279,7 +1121,7 @@
     grad_out_w = lax.dot_general(
         cot_all, gated_low, (((0,), (0,)), ((), ())), preferred_element_type=jnp.float32
     )
-    grad_dbl = lax.psum(grad_dbl_part, "tensor")
+    grad_dbl = lax.psum(grad_dbl_part.T, "tensor")
     grad_dbl_low = grad_dbl.astype(jnp.bfloat16)
     grad_conv = grad_conv + jnp.dot(grad_dbl_low, x_proj, preferred_element_type=jnp.float32)
     grad_xproj = lax.dot_general(
@@ -305,8 +1147,6 @@
     grad_rows_x, grad_gain_part = norm_back(grad_normed)
     grad_residual = cotangent + grad_rows_x
     grad_gain = lax.psum(grad_gain_part, "tensor")
-    if lax.axis_size("dp") <= 16:
-        grad_inx, grad_inz, grad_out_w = (v.astype(jnp.bfloat16) for v in (grad_inx, grad_inz, grad_out_w))
     gain_shard, inx_shard, inz_shard, step_shard, out_shard = (
         lax.psum_scatter(grad_gain, "dp", scatter_dimension=0, tiled=True),
         lax.psum_scatter(grad_inx, "dp", scatter_dimension=0, tiled=True),
@@ -314,7 +1154,6 @@
         lax.psum_scatter(grad_step_w, "dp", scatter_dimension=0, tiled=True),
         lax.psum_scatter(grad_out_w, "dp", scatter_dimension=0, tiled=True),
     )
-    inx_shard, inz_shard, out_shard = (v.astype(jnp.float32) for v in (inx_shard, inz_shard, out_shard))
     small_sums = lax.psum(
         (grad_xproj, grad_bias, grad_convw, grad_convb, grad_alog, grad_skip), "dp"
     )
@@ -356,7 +1195,7 @@
         P(("dp", "tensor"), None),
     )
     return jax.shard_map(
-        per_device,
+        per_device_split if mesh.shape["dp"] == 4 * NZ else per_device,
         mesh=mesh,
         in_specs=placed,
         out_specs=(

time: 965 us -> 265 us (0.27)
  waiting for transfers between devices: 735 us -> 0 us
  Pallas kernels: 24.3 us -> 249 us
  blocking collectives: 77.4 us -> 0 us
  matrix products: 56.3 us -> 0 us
  other arithmetic: 20.9 us -> 0 us
  local copies, waits for them, and re-layouts: 29.8 us -> 11 us
  between operations: 18.8 us -> 4.32 us
    reduce_scatter x5 -> x0, waiting for transfers between devices: 288 us -> none  [the longest x1 107 us: per_device(): lax.psum_scatter(grad_inz, 'dp', scatter_dimension=0, tiled=True)]
    pallas_call x1 -> x2, Pallas kernels: 24.3 us -> 249 us  [the longest x1 246 us: block_call(): pl.pallas_call(functools.partial(block_kernel, list(held)), out_shape=out...]
    unnamed x14 -> x0, waiting for transfers between devices: 183 us -> none
    all_gather x3 -> x0, waiting for transfers between devices: 150 us -> none  [the longest x1 69.7 us: per_device(): lax.all_gather(out_proj, 'dp', axis=0, tiled=True)]
    psum x2 -> x0, waiting for transfers between devices: 114 us -> none  [the longest x1 97.6 us: per_device(): lax.psum((grad_xproj, grad_bias, grad_convw, grad_convb, grad_alog, grad_...]
    all_gather x4 -> x0, blocking collectives: 63.1 us -> none  [the longest x1 23.2 us: per_device(): lax.all_gather(norm_gain, 'dp', axis=0, tiled=True)]
    dot_general x12 -> x0, matrix products: 56.3 us -> none  [the longest x1 7.28 us: per_device(): lax.dot_general(gated_low, out_all, (((1,), (1,)), ((), ())), preferred_e...]
    unnamed x49 -> x14, local copies, waits for them, and re-layouts: 23.8 us -> 7.45 us
  transfers between devices with their start and end apart: 12 -> 0, of which waited for: 11 -> 0; matrix products, arithmetic and copies ran while one was open for 8% -> 0% of each run, Pallas kernels for 0% -> 0%
where the time goes in v3:
time: 265 us; the launch traced here: 264 us
  Pallas kernels  249 us (94%)
  local copies, waits for them, and re-layouts  11 us (4%)
  between operations  4.32 us (2%)
    pallas_call x1, Pallas kernels, block_call(): pl.pallas_call(functools.partial(block_kernel, list(held)), out_shape=out...  246 us
    unnamed x14, local copies, waits for them, and re-layouts  7.45 us

profile of v3, /device:TPU:0, one launch (start us, length us, event | category | flops | bytes accessed | tf_op | source)
XLA Modules:
  0.0 264.2 jit_solution(7946394197956161494)
XLA Ops:
  0.7 246.1 %block.1 = (f32[64,2048]{1,0:T(8,128)}, f32[64,2048]{1,0:T(8,128)}, f32[8,128]{1,0:T(8,128)}, bf16[4,128,512]{2,1,0:T(8,128)(2,1)}, bf16[4,128,512]{2,1,0:T(8,12...) custom-call(bf16[128,2048]{1,0:T(8,128)(2,1)} %refs_0_.1, ...), custom_call_target="tpu_custom_call" | custom-call | tf_op jit(solution)/shard_map/block/pallas_call | solution.py:953
  246.7 1.2 slice.11
  248.6 1.2 slice.10
  250.5 1.2 slice_bitcast_fusion
  251.7 0.0 copy-start
  251.7 1.4 copy-done
  253.1 0.0 copy-start.1
  253.1 1.0 copy-done.1
  254.1 0.0 copy-start.2
  254.1 1.0 copy-done.2
  255.2 0.0 copy-start.3
  255.2 1.0 copy-done.3
  256.2 0.0 copy-start.4
  256.2 1.0 copy-done.4
  257.2 0.0 copy-start.5
  257.2 1.0 copy-done.5
  258.3 0.0 copy-start.6
  258.3 0.8 copy-done.6
  259.1 2.9 %finish.1 = (f32[64,2048]{1,0:T(8,128)}, f32[64,2048]{1,0:T(8,128)}, f32[128,2048]{1,0:T(8,128)}, f32[128,2048]{1,0:T(8,128)}, f32[128,2048]{1,0:T(8,128)}, /*in...) custom-call(f32[64,2048]{1,0:T(8,128)S(1)} %copy-done.1, ...), custom_call_target="tpu_custom_call" | custom-call | tf_op jit(solution)/shard_map/finish/pallas_call | solution.py:996
Async XLA Ops:
  251.7 1.4 copy-start
  253.1 1.0 copy-start.1
  254.1 1.0 copy-start.2
  255.2 1.0 copy-start.3
  256.2 1.0 copy-start.4
  257.2 1.0 copy-start.5
  258.3 0.8 copy-start.6

commit v4 on v3

--- a/solution.py
+++ b/solution.py
@@ -248,27 +248,44 @@
 
 
 class Copies:
-    def __init__(self, send_sems):
-        self.send_sems = send_sems
-        self.begun = []
-
-    def send(self, src, dst, recv_sem, device, when=None):
+    def __init__(self, send_sems, own_sems):
+        self.send_sems, self.own_sems = send_sems, own_sems
+        self.used, self.begun, self.kept = 0, [], []
+
+    def new_sem(self):
+        self.used += 1
+        return self.send_sems.at[self.used - 1]
+
+    def group(self, whole):
+        sem = self.new_sem()
+        self.begun.append((None, pltpu.make_async_copy(whole, whole, sem).wait))
+        return sem
+
+    def send(self, src, dst, recv_sem, device, when=None, group=None):
         copy = pltpu.make_async_remote_copy(
-            src_ref=src, dst_ref=dst, send_sem=self.send_sems.at[len(self.begun)], recv_sem=recv_sem,
+            src_ref=src, dst_ref=dst, send_sem=self.new_sem() if group is None else group, recv_sem=recv_sem,
             device_id=device, device_id_type=MESH,
         )
-        self.begun.append((when, copy))
+        if group is None:
+            self.begun.append((when, copy.wait_send))
         if when is None:
             copy.start()
         else:
             pl.when(when)(copy.start)
 
+    def keep(self, src, dst):
+        copy = pltpu.make_async_copy(src, dst, self.own_sems.at[len(self.kept)])
+        copy.start()
+        self.kept.append(copy)
+
     def wait_sent(self):
-        for when, copy in self.begun:
+        for when, wait in self.begun:
             if when is None:
-                copy.wait_send()
+                wait()
             else:
-                pl.when(when)(copy.wait_send)
+                pl.when(when)(wait)
+        for copy in self.kept:
+            copy.wait()
 
 
 def arrived(dst, recv_sem, when=None):
@@ -283,6 +300,7 @@
     def __init__(self, spot, copies, src, dst, recv_sems, own_sem):
         self.spot, self.copies, self.src, self.dst, self.recv_sems, self.own_sem = spot, copies, src, dst, recv_sems, own_sem
         self.width = dst.shape[-1]
+        self.group = copies.group(dst.at[pl.ds(0, 4 * NZ - 1)])
 
     def columns(self, z):
         return self.src.at[:, pl.ds(pl.multiple_of(z * self.width, self.width), self.width)]
@@ -291,12 +309,13 @@
         spot, me = self.spot, self.spot.dp
         for offset in range(1, NZ):
             z = spot.z_at(offset)
-            self.copies.send(self.columns(z), self.dst.at[me], self.recv_sems.at[me], spot.on_line(z))
+            self.copies.send(self.columns(z), self.dst.at[me], self.recv_sems.at[me], spot.on_line(z), group=self.group)
         self.own = pltpu.make_async_copy(self.columns(spot.z), self.dst.at[me], self.own_sem)
         self.own.start()
 
     def pass_on(self, origin, device):
-        self.copies.send(self.dst.at[origin], self.dst.at[origin], self.recv_sems.at[origin], device)
+        sem = self.recv_sems.at[4 * NZ if device is self.spot.c_mate else origin]
+        self.copies.send(self.dst.at[origin], self.dst.at[origin], sem, device, group=self.group)
 
     def first(self):
         spot = self.spot
@@ -317,45 +336,37 @@
             self.pass_on(origin, spot.c_mate)
 
     def last(self):
-        spot = self.spot
-        for x in range(2):
-            for offset in range(NZ):
-                origin = place(spot.z_at(-offset), x, 1 - spot.c)
-                arrived(self.dst.at[origin], self.recv_sems.at[origin])
+        arrived(self.dst.at[pl.ds(0, 2 * NZ)], self.recv_sems.at[4 * NZ])
 
 
 class LineSum:
-    def __init__(self, spot, copies, part, landing, total, part_sems, total_sems):
-        self.spot, self.copies, self.part, self.landing, self.total = spot, copies, part, landing, total
-        self.part_sems, self.total_sems = part_sems, total_sems
+    def __init__(self, spot, copies, part, landing, total, sems):
+        self.spot, self.copies, self.part, self.landing, self.total, self.sems = spot, copies, part, landing, total, sems
         self.offsets = [(dz, dy) for dz in range(NZ) for dy in range(2) if dz + dy > 0]
+        self.all_others = landing.at[pl.ds(0, len(self.offsets))]
+        self.groups = [copies.group(self.all_others) for _ in range(2)]
 
     def there(self, dz, dy):
         return self.spot.z_at(dz), lax.rem(self.spot.y + dy, 2)
 
     def push(self):
-        for dz, dy in self.offsets:
+        for k, (dz, dy) in enumerate(self.offsets):
             z, y = self.there(dz, dy)
-            slot = dz * 2 + dy
-            self.copies.send(self.part.at[z, y], self.landing.at[slot], self.part_sems.at[slot], self.spot.on_line(z, y))
+            self.copies.send(self.part.at[z, y], self.landing.at[k], self.sems.at[0], self.spot.on_line(z, y), group=self.groups[0])
 
     def middle(self):
         own_z, own_y = self.spot.z, self.spot.y
-        summed = self.part[own_z, own_y]
-        for dz, dy in self.offsets:
-            slot = dz * 2 + dy
-            arrived(self.landing.at[slot], self.part_sems.at[slot])
-            summed = summed + self.landing[slot]
-        self.total[own_z, own_y] = summed
+        arrived(self.all_others, self.sems.at[0])
+        summed = self.part[own_z, own_y].astype(F32)
+        for k in range(len(self.offsets)):
+            summed = summed + self.landing[k].astype(F32)
+        self.total[own_z, own_y] = summed.astype(BF16)
         own = self.total.at[own_z, own_y]
         for dz, dy in self.offsets:
-            z, y = self.there(dz, dy)
-            self.copies.send(own, own, self.total_sems.at[own_z, own_y], self.spot.on_line(z, y))
+            self.copies.send(own, own, self.sems.at[1], self.spot.on_line(*self.there(dz, dy)), group=self.groups[1])
 
     def last(self):
-        for dz, dy in self.offsets:
-            z, y = self.there(dz, dy)
-            arrived(self.total.at[z, y], self.total_sems.at[z, y])
+        arrived(self.all_others, self.sems.at[1])
 
 
 def column_masks(tile):
@@ -365,16 +376,21 @@
 class Share:
     def __init__(self, spot, copies, dst, recv_sems):
         self.spot, self.copies, self.dst, self.recv_sems = spot, copies, dst, recv_sems
+        self.over_y = copies.group(dst.at[pl.ds(0, NZ // 2)])
 
     def send(self, z, device, when=None):
-        y = self.spot.y
-        self.copies.send(self.dst.at[z, y], self.dst.at[z, y], self.recv_sems.at[z, y], device, when)
+        own = self.dst.at[z, self.spot.y]
+        self.copies.send(own, own, self.recv_sems.at[z], device, when)
+
+    def send_y(self, z, when=None):
+        own = self.dst.at[z, self.spot.y]
+        self.copies.send(own, own, self.recv_sems.at[NZ], self.spot.y_mate, when, self.over_y)
 
     def push(self):
         spot = self.spot
         self.send(spot.z, spot.on_line(spot.z_at(1)), spot.z < NZ - 1)
         self.send(spot.z, spot.on_line(spot.z_at(-1)), spot.z > 0)
-        self.send(spot.z, spot.y_mate)
+        self.send_y(spot.z)
 
     def first(self, far):
         spot = self.spot
@@ -382,16 +398,13 @@
             origin = spot.z_at(-way * far)
             comes = spot.z >= far if way == 1 else spot.z < NZ - far
             goes = comes & (spot.z < NZ - 1 if way == 1 else spot.z > 0)
-            arrived(self.dst.at[origin, spot.y], self.recv_sems.at[origin, spot.y], comes)
+            arrived(self.dst.at[origin, spot.y], self.recv_sems.at[origin], comes)
             if far < NZ - 1:
                 self.send(origin, spot.on_line(spot.z_at(way)), goes)
-            self.send(origin, spot.y_mate, comes)
+            self.send_y(origin, comes)
 
     def last(self):
-        spot = self.spot
-        for offset in range(NZ):
-            z = spot.z_at(-offset)
-            arrived(self.dst.at[z, 1 - spot.y], self.recv_sems.at[z, 1 - spot.y])
+        arrived(self.dst.at[pl.ds(0, NZ // 2)], self.recv_sems.at[NZ])
 
 
 class Scan:
@@ -480,43 +493,77 @@
     def __init__(self, spot, copies, part, y_land, z_land, y_sems, z_sems):
         self.spot, self.copies, self.part, self.y_land, self.z_land = spot, copies, part, y_land, z_land
         self.y_sems, self.z_sems = y_sems, z_sems
+        self.group = copies.group(y_land)
+
+    def push(self):
+        spot = self.spot
+        for far in (3, 2, 1):
+            for way in (1, -1):
+                self.over_y(spot.z_at(way * far), self.within(way, far))
+        self.over_y(spot.z, None)
+
+    def within(self, way, far):
+        return self.spot.z < NZ - far if way == 1 else self.spot.z >= far
+
+    def over_y(self, z, when):
+        self.copies.send(self.part.at[z, 1 - self.spot.y], self.y_land.at[z], self.y_sems.at[z], self.spot.y_mate, when, self.group)
+
+    def add(self, z, landed):
+        part, y = self.part, self.spot.y
+        part[z, y] = (part[z, y].astype(F32) + landed[...].astype(F32)).astype(BF16)
+
+    def stage(self, far):
+        spot = self.spot
+        for side, way in enumerate((1, -1)):
+            z = spot.z_at(way * far)
+            goes = self.within(way, far)
+            grown = goes & self.within(-way, 1)
+            land, sem = self.z_land.at[side, z], self.z_sems.at[side, z]
+
+            @pl.when(goes)
+            def _(z=z):
+                arrived(self.y_land.at[z], self.y_sems.at[z])
+                self.add(z, self.y_land.at[z])
+
+            if far < NZ - 1:
+
+                @pl.when(grown)
+                def _(z=z, land=land, sem=sem):
+                    arrived(land, sem)
+                    self.add(z, land)
+
+            self.copies.send(self.part.at[z, spot.y], land, sem, spot.on_line(spot.z_at(way)), goes)
+
+    def last(self):
+        spot = self.spot
+        z = spot.z
+        arrived(self.y_land.at[z], self.y_sems.at[z])
+        self.add(z, self.y_land.at[z])
+        for side, way in enumerate((1, -1)):
+
+            @pl.when(self.within(-way, 1))
+            def _(land=self.z_land.at[side, z], sem=self.z_sems.at[side, z]):
+                arrived(land, sem)
+                self.add(z, land)
+
+        return self.part[z, spot.y].astype(F32)
+
+
+class RowSum:
+    def __init__(self, spot, copies, part, c_land, x_land, z_land, c_sems, x_sems, z_sem):
+        self.spot, self.copies, self.part = spot, copies, part
+        self.c_land, self.x_land, self.z_land = c_land, x_land, z_land
+        self.c_sems, self.x_sems, self.z_sem = c_sems, x_sems, z_sem
+        self.groups = [copies.group(whole) for whole in (c_land, x_land, z_land.at[pl.ds(0, NZ - 1)])]
 
     def push(self):
         spot = self.spot
         for offset in (1, 2, 3, 0):
             z = spot.z_at(offset)
-            self.copies.send(self.part.at[z, 1 - spot.y], self.y_land.at[z], self.y_sems.at[z], spot.y_mate)
-
-    def middle(self):
-        spot = self.spot
-        for offset in (1, 2, 3):
-            z = spot.z_at(offset)
-            arrived(self.y_land.at[z], self.y_sems.at[z])
-            self.part[z, spot.y] = (self.part[z, spot.y].astype(F32) + self.y_land[z].astype(F32)).astype(BF16)
-            self.copies.send(self.part.at[z, spot.y], self.z_land.at[offset - 1], self.z_sems.at[offset - 1], spot.on_line(z))
-
-    def last(self):
-        spot = self.spot
-        arrived(self.y_land.at[spot.z], self.y_sems.at[spot.z])
-        summed = self.part[spot.z, spot.y].astype(F32) + self.y_land[spot.z].astype(F32)
-        for k in range(NZ - 1):
-            arrived(self.z_land.at[k], self.z_sems.at[k])
-            summed = summed + self.z_land[k].astype(F32)
-        return summed
-
-
-class RowSum:
-    def __init__(self, spot, copies, part, c_land, x_land, z_land, c_sems, x_sems, z_sems):
-        self.spot, self.copies, self.part = spot, copies, part
-        self.c_land, self.x_land, self.z_land = c_land, x_land, z_land
-        self.c_sems, self.x_sems, self.z_sems = c_sems, x_sems, z_sems
-
-    def push(self):
-        spot = self.spot
-        for offset in (1, 2, 3, 0):
-            z = spot.z_at(offset)
-            for x in (1 - spot.x, spot.x):
-                self.copies.send(self.part.at[z, x, 1 - spot.c], self.c_land.at[z, x], self.c_sems.at[z, x], spot.c_mate)
+            for x in range(2):
+                self.copies.send(
+                    self.part.at[z, x, 1 - spot.c], self.c_land.at[z, x], self.c_sems.at[z], spot.c_mate, group=self.groups[0]
+                )
 
     def add(self, z, x, landed):
         part = self.part
@@ -526,34 +573,34 @@
         spot = self.spot
         for offset in (1, 2, 3, 0):
             z = spot.z_at(offset)
-            for x in (1 - spot.x, spot.x):
-                arrived(self.c_land.at[z, x], self.c_sems.at[z, x])
+            arrived(self.c_land.at[z], self.c_sems.at[z])
+            for x in range(2):
                 self.add(z, x, self.c_land[z, x])
-            self.copies.send(self.part.at[z, 1 - spot.x, spot.c], self.x_land.at[z], self.x_sems.at[z], spot.x_mate)
-
-    def third(self):
-        spot = self.spot
-        for offset in (1, 2, 3, 0):
+            self.copies.send(
+                self.part.at[z, 1 - spot.x, spot.c], self.x_land.at[z], self.x_sems.at[z], spot.x_mate, group=self.groups[1]
+            )
+
+    def third(self, offsets=(1, 2, 3, 0)):
+        spot = self.spot
+        for offset in offsets:
             z = spot.z_at(offset)
             arrived(self.x_land.at[z], self.x_sems.at[z])
             self.add(z, spot.x, self.x_land[z])
+            own = self.part.at[z, spot.x, spot.c]
             if offset:
-                self.copies.send(
-                    self.part.at[z, spot.x, spot.c], self.z_land.at[spot.z], self.z_sems.at[spot.z], spot.on_line(z)
-                )
-        self.z_land[spot.z] = self.part[spot.z, spot.x, spot.c]
+                self.copies.send(own, self.z_land.at[spot.z], self.z_sem, spot.on_line(z), group=self.groups[2])
+            else:
+                self.copies.keep(own, self.z_land.at[z])
 
     def last(self):
-        spot = self.spot
-        for offset in (1, 2, 3):
-            z = spot.z_at(-offset)
-            arrived(self.z_land.at[z], self.z_sems.at[z])
+        arrived(self.z_land.at[pl.ds(0, NZ - 1)], self.z_sem)
 
 
 class ChannelSum:
-    def __init__(self, spot, copies, part, c_land, x_land, full, c_sem, x_sem, full_sems):
-        self.spot, self.copies, self.part, self.full, self.full_sems = spot, copies, part, full, full_sems
+    def __init__(self, spot, copies, part, c_land, x_land, own, full, c_sem, x_sem, full_sems):
+        self.spot, self.copies, self.part, self.own, self.full, self.full_sems = spot, copies, part, own, full, full_sems
         self.c_land, self.x_land, self.c_sem, self.x_sem = c_land, x_land, c_sem, x_sem
+        self.group = copies.group(full.at[pl.ds(0, 4 * NZ - 1)])
 
     def push(self):
         self.copies.send(self.part.at[1 - self.spot.c], self.c_land, self.c_sem, self.spot.c_mate)
@@ -564,17 +611,18 @@
         self.part[spot.c] = self.part[spot.c] + self.c_land[...]
         self.copies.send(self.part.at[spot.c, 1 - spot.x], self.x_land, self.x_sem, spot.x_mate)
 
-    def spread(self, origin, device):
-        self.copies.send(self.full.at[origin], self.full.at[origin], self.full_sems.at[origin], device)
+    def spread(self, origin, device, src=None):
+        src = self.full.at[origin] if src is None else src
+        sem = self.full_sems.at[4 * NZ if device is self.spot.c_mate else origin]
+        self.copies.send(src, self.full.at[origin], sem, device, group=self.group)
 
     def third(self):
         spot = self.spot
         arrived(self.x_land, self.x_sem)
-        self.full[spot.dp] = self.part[spot.c, spot.x] + self.x_land[...]
-        for offset in (1, 2, 3):
-            self.spread(spot.dp, spot.on_line(spot.z_at(offset)))
-        self.spread(spot.dp, spot.x_mate)
-        self.spread(spot.dp, spot.c_mate)
+        self.own[...] = (self.part[spot.c, spot.x] + self.x_land[...]).astype(BF16)
+        for device in [spot.on_line(spot.z_at(offset)) for offset in (1, 2, 3)] + [spot.x_mate, spot.c_mate]:
+            self.spread(spot.dp, device, self.own)
+        self.copies.keep(self.own, self.full.at[spot.dp])
 
     def fourth(self):
         spot = self.spot
@@ -592,11 +640,7 @@
             self.spread(origin, spot.c_mate)
 
     def last(self):
-        spot = self.spot
-        for x in range(2):
-            for offset in range(NZ):
-                origin = place(spot.z_at(-offset), x, 1 - spot.c)
-                arrived(self.full.at[origin], self.full_sems.at[origin])
+        arrived(self.full.at[pl.ds(0, 2 * NZ)], self.full_sems.at[4 * NZ])
 
 
 class Held:
@@ -633,12 +677,9 @@
         "sum": vmem((2, 8, N, 128), F32),
         "gmap": vmem((2 * N, tokens), F32),
         "dbl": vmem((width, tokens), F32),
-        "part": vmem(part, F32),
-        "landing": vmem((2 * NZ,) + part[2:], F32),
-        "total": vmem(part, F32),
-        "gpart": vmem(part, F32),
-        "glanding": vmem((2 * NZ,) + part[2:], F32),
-        "gtotal": vmem(part, F32),
+        "part": vmem((2,) + part, BF16),
+        "landing": vmem((2, 2 * NZ) + part[2:], BF16),
+        "total": vmem((2,) + part, BF16),
         "mixed": vmem((NZ, 2, half, feats), BF16),
         "normed": vmem((NZ, 2, half, feats), BF16),
         "outw": vmem(owners, BF16),
@@ -647,32 +688,35 @@
         "gdtp": vmem(steps, F32),
         "chan": vmem((2, 2, small, chans), F32),
         "y_land": vmem((2, NZ, half, feats), BF16),
-        "z_land": vmem((2, NZ - 1, half, feats), BF16),
+        "z_land": vmem((2, 2, NZ, half, feats), BF16),
         "wc_land": vmem((3, NZ, 2, rows, chans), BF16),
         "wx_land": vmem((3, NZ, rows, chans), BF16),
         "dc_land": vmem((NZ, 2, step_rows, chans), F32),
         "dx_land": vmem((NZ, step_rows, chans), F32),
         "fc_land": vmem((2, small, chans), F32),
         "fx_land": vmem((small, chans), F32),
+        "f_own": vmem((small, chans), BF16),
+        "block": vmem((half, feats), F32),
+        "gresid": vmem((half, feats), F32),
         "tile": vmem((4, 8, 128), F32),
         "gain": vmem((3, n_dp, 8, 128), F32),
         "gain_land": vmem((n_dp - 1, 8, 128), F32),
-        "send_sems": dma((288,)),
+        "send_sems": dma((56,)),
+        "keep_sems": dma((7,)),
         "own_sems": dma((4,)),
-        "w_sems": dma((4, n_dp)),
-        "act_sems": dma((2, NZ, 2)),
-        "info_sems": dma((n_dp,)),
-        "part_sems": dma((2, 2 * NZ)),
-        "total_sems": dma((2, NZ, 2)),
+        "w_sems": dma((4, n_dp + 1)),
+        "act_sems": dma((2, NZ + 1)),
+        "info_sem": dma(()),
+        "dbl_sems": dma((2, 2)),
         "y_sems": dma((2, NZ)),
-        "z_sems": dma((2, NZ - 1)),
-        "wc_sems": dma((4, NZ, 2)),
+        "z_sems": dma((2, 2, NZ)),
+        "wc_sems": dma((4, NZ)),
         "wx_sems": dma((4, NZ)),
-        "wz_sems": dma((4, NZ)),
+        "wz_sems": dma((4,)),
         "f_sems": dma((2,)),
-        "full_sems": dma((n_dp,)),
+        "full_sems": dma((n_dp + 1,)),
         "tile_sems": dma((2,)),
-        "gain_sems": dma((n_dp,)),
+        "gain_sems": dma((2,)),
     }
     return held
 
@@ -687,7 +731,7 @@
     spot = Spot()
     plane = [lax.rem(spot.dp + offset, 4 * NZ) for offset in range(1, 4 * NZ)]
     greet([(dp, spot.y) for dp in plane] + [spot.on_line(spot.z_at(dz), 1 - spot.y) for dz in range(NZ)])
-    copies = Copies(s.send_sems)
+    copies = Copies(s.send_sems, s.keep_sems)
     tokens, chans = s.x_in.shape
     half, feats = resid_ref.shape
     length = 2 * half
@@ -709,8 +753,10 @@
         same = jnp.where((pltpu.roll(ids, back, 1) == ids) & (lane >= back), 1.0, 0.0)
         info = jnp.where(sub == back, same, info)
     s.info[spot.dp] = info
+    other_info = s.info.at[pl.ds(0, 4 * NZ - 1)]
+    info_group = copies.group(other_info)
     for dp in plane:
-        copies.send(s.info.at[spot.dp], s.info.at[spot.dp], s.info_sems.at[spot.dp], (dp, spot.y))
+        copies.send(s.info.at[spot.dp], s.info.at[spot.dp], s.info_sem, (dp, spot.y), group=info_group)
     inx.push()
 
     resid = resid_ref[...]
@@ -718,8 +764,7 @@
     scaled = resid * lax.rsqrt(row_square / feats + eps_norm)
     s.tile[0] = jnp.broadcast_to(jnp.sum(row_square, axis=0, keepdims=True), (8, 128))
     copies.send(s.tile.at[0], s.tile.at[1], s.tile_sems.at[0], spot.y_mate)
-    for dp in plane:
-        arrived(s.info.at[dp], s.info_sems.at[dp])
+    arrived(other_info, s.info_sem)
     for k in range(4 * NZ):
         cols = slice(k * 128, (k + 1) * 128)
         s.acts[0, spot.z, spot.y, :, cols] = (scaled[:, cols] * s.info[k, 0:1, :]).astype(BF16)
@@ -729,16 +774,14 @@
     for k in range(NZ):
         s.mask[k] = column_masks(s.info[place(k, spot.x, spot.c)])
     inx.first()
-    inz.push()
     normed.first(1)
     inx.second()
-    cot.push()
+    inz.push()
     normed.first(2)
     dtp.first()
     dtp.second()
+    cot.push()
     normed.first(3)
-    inz.first()
-    outp.push()
     normed.last()
     inx.last()
 
@@ -759,21 +802,23 @@
     blocks = [(k, y) for k in range(NZ) for y in range(2)]
     width = dbl.shape[0] // 2
     for k, y in blocks:
-        s.part[k, y] = dbl[y * width : (y + 1) * width, sequences[k]]
-    x_dbl = LineSum(spot, copies, s.part, s.landing, s.total, s.part_sems.at[0], s.total_sems.at[0])
+        s.part[0, k, y] = dbl[y * width : (y + 1) * width, sequences[k]].astype(BF16)
+    x_dbl = LineSum(
+        spot, copies, s.part.at[0], s.landing.at[0], s.total.at[0], s.dbl_sems.at[0]
+    )
     x_dbl.push()
+    outp.push()
     cot.first(1)
-    inz.second()
     x_dbl.middle()
+    inz.first()
     cot.first(2)
-    outp.first()
+    x_dbl.last()
+
     dtp.last()
-    x_dbl.last()
-
     for k, y in blocks:
-        s.dbl[y * width : (y + 1) * width, sequences[k]] = s.total[k, y]
+        s.dbl[y * width : (y + 1) * width, sequences[k]] = s.total[0, k, y].astype(F32)
     step_w = s.dtp[...].reshape(R, chans).astype(BF16)
-    s.raw[...] = split_dot(s.dbl[:R], step_w, TN) + dtb_ref[:, columns]
+    s.raw[...] = dot(s.dbl[:R].astype(BF16), step_w, TN) + dtb_ref[:, columns]
     for k, rows in enumerate(sequences):
         step = softplus(s.raw[rows])
         s.stepd[rows] = jnp.where(s.mask[k, :, 1:2] > 0.0, step, 1e30)
@@ -785,9 +830,13 @@
     )
     steps = tokens // 8
     scan.forward(0, steps // 4)
+    inz.second()
+    scan.forward(steps // 4, steps // 2)
     cot.first(3)
+    scan.forward(steps // 2, 3 * steps // 4)
+    outp.first()
+    scan.forward(3 * steps // 4, steps)
     outp.second()
-    scan.forward(steps // 4, steps)
     inz.last()
     s.gate[...] = dot(s.acts[0].reshape(tokens, feats), s.w[1].reshape(-1, chans))
     cot.last()
@@ -827,11 +876,11 @@
     outw_sum.second()
     scan.backward(steps - steps // 4, steps)
     ginz_sum.second()
-    mixed_sum.middle()
+    mixed_sum.stage(3)
     scan.backward(steps // 2, steps - steps // 4)
     outw_sum.third()
+    mixed_sum.stage(2)
     scan.backward(steps // 4, steps // 2)
-    ginz_sum.third()
     scan.backward(0, steps // 4)
 
     grad_bias = jnp.zeros((1, chans), F32)
@@ -847,18 +896,22 @@
     raw_low = jnp.concatenate(raw_rows, axis=0)
     dbl = jnp.concatenate([dot(step_w, raw_low, NT), s.gmap[...]], axis=0)
     for k, y in blocks:
-        s.gpart[k, y] = dbl[y * width : (y + 1) * width, sequences[k]]
-    grad_dbl_sum = LineSum(spot, copies, s.gpart, s.glanding, s.gtotal, s.part_sems.at[1], s.total_sems.at[1])
+        s.part[1, k, y] = dbl[y * width : (y + 1) * width, sequences[k]].astype(BF16)
+    grad_dbl_sum = LineSum(
+        spot, copies, s.part.at[1], s.landing.at[1], s.total.at[1], s.dbl_sems.at[1]
+    )
     grad_dbl_sum.push()
     s.gdtp[...] = dot(s.dbl[:R].astype(BF16), raw_low).reshape(s.gdtp.shape)
     gdtp_sum.push()
     grad_dbl_sum.middle()
+    mixed_sum.stage(1)
+    ginz_sum.third()
     gdtp_sum.second()
     grad_dbl_sum.last()
 
     grad_dbl = jnp.concatenate(
-        [jnp.concatenate([s.gtotal[k, y] for k in range(NZ)], axis=1) for y in range(2)], axis=0
-    ).astype(BF16)
+        [jnp.concatenate([s.total[1, k, y] for k in range(NZ)], axis=1) for y in range(2)], axis=0
+    )
     s.gg[...] += dot(grad_dbl, x_proj, TN)
     sums = [jnp.zeros((1, chans), F32) for _ in range(5)]
     low_rows = []
@@ -875,65 +928,71 @@
             grad_x = grad_x + taps[3 - back : 4 - back] * pltpu.roll(masked, length - back, 0)
         low_rows.append(grad_x.astype(BF16))
     grad_xin = jnp.concatenate(low_rows, axis=0)
-    s.normed[...] = (
-        dot(grad_xin, s.w[0].reshape(-1, chans), NT) + dot(s.ggate[...], s.w[1].reshape(-1, chans), NT)
-    ).astype(BF16).reshape(s.normed.shape)
+    grad_normed = dot(grad_xin, s.w[0].reshape(-1, chans), NT) + dot(s.ggate[...], s.w[1].reshape(-1, chans), NT)
+    s.normed[...] = grad_normed.astype(BF16).reshape(s.normed.shape)
     normed_sum.push()
-    s.ginx[...] = dot(s.acts[0].reshape(tokens, feats), grad_xin, TN).astype(BF16).reshape(s.ginx.shape)
-    ginx_sum.push()
     s.chan[...] = jnp.concatenate(
         [dot(grad_dbl, s.low[...]), s.alog[...] * s.a[...], grad_bias, grad_skip, jnp.zeros((6, chans), F32)]
         + sums + [jnp.zeros((3, chans), F32)], axis=0
     ).reshape(s.chan.shape)
     small_sum = ChannelSum(
-        spot, copies, s.chan, s.fc_land, s.fx_land, full_ref, s.f_sems.at[0], s.f_sems.at[1], s.full_sems
+        spot, copies, s.chan, s.fc_land, s.fx_land, s.f_own, full_ref, s.f_sems.at[0], s.f_sems.at[1], s.full_sems
     )
     small_sum.push()
+    s.ginx[...] = dot(s.acts[0].reshape(tokens, feats), grad_xin, TN).astype(BF16).reshape(s.ginx.shape)
+    ginx_sum.push()
+    small_sum.second()
+    gain_part = jnp.sum(grad_normed * s.acts[0].reshape(tokens, feats).astype(F32), axis=0, keepdims=True)
+    for k in range(4 * NZ):
+        s.gain[0, k] = jnp.broadcast_to(gain_part[:, k * 128 : (k + 1) * 128], (8, 128)) / s.info[k, 0:1]
+    copies.send(s.gain.at[0], s.gain.at[1], s.gain_sems.at[0], spot.y_mate)
     ginx_sum.second()
     gdtp_sum.third()
-    small_sum.second()
-    normed_sum.middle()
+    normed_sum.stage(3)
     small_sum.third()
-    ginx_sum.third()
+    normed_sum.stage(2)
+    ginx_sum.third((1, 2))
+    arrived(s.gain.at[1], s.gain_sems.at[0])
+    s.gain[2] = s.gain[0] + s.gain[1]
+    gain_group = copies.group(s.gain_land)
+    for offset, dp in enumerate(plane):
+        copies.send(s.gain.at[2, dp], s.gain_land.at[offset], s.gain_sems.at[1], (dp, spot.y), group=gain_group)
+    normed_sum.stage(1)
+    ginx_sum.third((3, 0))
+    small_sum.fourth()
 
     mixed = mixed_sum.last()
     resid = resid_ref[...]
-    block_ref[...] = resid + mixed
+    s.block[...] = resid + mixed
+    copies.keep(s.block, block_ref)
     s.tile[2] = jnp.broadcast_to(jnp.sum(jnp.sum(mixed * mixed, axis=1, keepdims=True), axis=0, keepdims=True), (8, 128))
     copies.send(s.tile.at[2], s.tile.at[3], s.tile_sems.at[1], spot.y_mate)
-    small_sum.fourth()
+    arrived(s.gain_land, s.gain_sems.at[1])
+    total = s.gain[2, spot.dp]
+    for offset in range(4 * NZ - 1):
+        total = total + s.gain_land[offset]
+    ggain_ref[...] = total
+    small_sum.fifth()
     outw_sum.last()
     ginz_sum.last()
     gdtp_sum.last()
-    small_sum.fifth()
-
-    grad_rows = normed_sum.last()
-    inv = lax.rsqrt(jnp.sum(resid * resid, axis=1, keepdims=True) / feats + eps_norm)
-    scaled = resid * inv
-    gain_part = jnp.sum(grad_rows * scaled, axis=0, keepdims=True)
-    for k in range(4 * NZ):
-        s.gain[0, k] = jnp.broadcast_to(gain_part[:, k * 128 : (k + 1) * 128], (8, 128))
-    copies.send(s.gain.at[0], s.gain.at[1], s.gain_sems.at[4 * NZ - 1], spot.y_mate)
-    gain = jnp.concatenate([s.info[k, 0:1] for k in range(4 * NZ)], axis=1)
-    grad_scaled = grad_rows * gain
-    mean = jnp.sum(grad_scaled * scaled, axis=1, keepdims=True) / feats
-    gresid_ref[...] = cot_ref[...] + inv * (grad_scaled - scaled * mean)
-    arrived(s.gain.at[1], s.gain_sems.at[4 * NZ - 1])
-    s.gain[2] = s.gain[0] + s.gain[1]
-    for offset, dp in enumerate(plane):
-        copies.send(s.gain.at[2, dp], s.gain_land.at[offset], s.gain_sems.at[offset], (dp, spot.y))
     arrived(s.tile.at[1], s.tile_sems.at[0])
     square_ref[...] = s.tile[0] + s.tile[1]
     arrived(s.tile.at[3], s.tile_sems.at[1])
     msquare_ref[...] = s.tile[2] + s.tile[3]
+
+    grad_rows = normed_sum.last()
+    inv = lax.rsqrt(jnp.sum(resid * resid, axis=1, keepdims=True) / feats + eps_norm)
+    scaled = resid * inv
+    gain = jnp.concatenate([s.info[k, 0:1] for k in range(4 * NZ)], axis=1)
+    grad_scaled = grad_rows * gain
+    mean = jnp.sum(grad_scaled * scaled, axis=1, keepdims=True) / feats
+    s.gresid[...] = cot_ref[...] + inv * (grad_scaled - scaled * mean)
+    copies.keep(s.gresid, gresid_ref)
     ginx_sum.last()
     small_sum.last()
-    total = s.gain[2, spot.dp]
-    for offset in range(4 * NZ - 1):
-        arrived(s.gain_land.at[offset], s.gain_sems.at[offset])
-        total = total + s.gain_land[offset]
-    ggain_ref[...] = total
     copies.wait_sent()
+    assert copies.used == s.send_sems.shape[0], copies.used
 
 
 def block_call(in_x, in_z, out_p, residual, cotangent, gain, ids, dt_p, x_proj, conv_w, conv_b, dt_b, a_log, d_skip):
@@ -945,7 +1004,7 @@
     outs = [
         shape((half, feats), F32), shape((half, feats), F32), shape((8, 128), F32),
         shape((NZ, rows, chans), BF16), shape((NZ, rows, chans), BF16), shape((NZ, rows, chans), BF16),
-        shape((NZ, dt_p.shape[0], chans), F32), shape((n_dp, (x_proj.shape[0] + 32) // 4, chans), F32),
+        shape((NZ, dt_p.shape[0], chans), F32), shape((n_dp, (x_proj.shape[0] + 32) // 4, chans), BF16),
         shape((8, 128), F32), shape((8, 128), F32),
     ]
     in_any = pl.BlockSpec(memory_space=pl.ANY)
@@ -954,7 +1013,7 @@
         functools.partial(block_kernel, list(held)),
         out_shape=outs,
         in_specs=[in_any] * 3 + [in_vmem] * 11,
-        out_specs=[in_vmem] * len(outs),
+        out_specs=[in_any] * 2 + [in_vmem] + [in_any] * 5 + [in_vmem] * 2,
         scratch_shapes=list(held.values()),
         name="block",
         compiler_params=pltpu.CompilerParams(collective_id=1, has_side_effects=True, vmem_limit_bytes=62 << 20),
@@ -962,11 +1021,15 @@
 
 
 def finish_kernel(
-    block_in, gresid_in, ginx_in, ginz_in, goutp_in, gdtp_in, full_in,
+    scale, block_in, gresid_in, ginx_in, ginz_in, goutp_in, gdtp_in, full_in, ggain_in, square_in, msquare_in,
     block_ref, gresid_ref, ginx_ref, ginz_ref, goutp_ref, gdtp_ref, xproj_ref, alog_ref, dtb_ref, skip_ref, convw_ref, convb_ref,
+    ggain_ref, rms_ref, mrms_ref,
 ):
     block_ref[...] = block_in[...]
     gresid_ref[...] = gresid_in[...]
+    ggain_ref[...] = ggain_in[0:1]
+    rms_ref[...] = jnp.sqrt(square_in[0:1, 0:1] * scale)
+    mrms_ref[...] = jnp.sqrt(msquare_in[0:1, 0:1] * scale)
     chans = ginx_in.shape[2]
     for z in range(NZ):
         cols = slice(z * chans, (z + 1) * chans)
@@ -974,29 +1037,29 @@
             ref[:, cols] = given[z].astype(F32)
         rows = full_in.shape[1]
         for k in range(4):
-            origin = place(z, k % 2, k // 2)
+            found = full_in[place(z, k % 2, k // 2)].astype(F32)
             upto = min(rows, xproj_ref.shape[0] - k * rows)
-            xproj_ref[k * rows : k * rows + upto, cols] = full_in[origin, :upto]
-        last = place(z, 1, 1)
-        alog_ref[:, cols] = full_in[last, upto : upto + N]
-        dtb_ref[:, cols] = full_in[last, upto + N : upto + N + 1]
-        skip_ref[:, cols] = full_in[last, upto + N + 1 : upto + N + 2]
-        convw_ref[:, cols] = full_in[last, upto + 24 : upto + 28]
-        convb_ref[:, cols] = full_in[last, upto + 28 : upto + 29]
-
-
-def finish_call(block, gresid, ginx, ginz, goutp, gdtp, full, width):
+            xproj_ref[k * rows : k * rows + upto, cols] = found[:upto]
+        alog_ref[:, cols] = found[upto : upto + N]
+        dtb_ref[:, cols] = found[upto + N : upto + N + 1]
+        skip_ref[:, cols] = found[upto + N + 1 : upto + N + 2]
+        convw_ref[:, cols] = found[upto + 24 : upto + 28]
+        convb_ref[:, cols] = found[upto + 28 : upto + 29]
+
+
+def finish_call(block, gresid, ginx, ginz, goutp, gdtp, full, ggain, square, msquare, width):
     rows, wide = ginx.shape[1], ginx.shape[2] * NZ
-    shape = lambda count: jax.ShapeDtypeStruct((count, wide), F32)
+    shape = lambda count, columns=wide: jax.ShapeDtypeStruct((count, columns), F32)
     outs = [
-        jax.ShapeDtypeStruct(block.shape, F32), jax.ShapeDtypeStruct(gresid.shape, F32), shape(rows), shape(rows), shape(rows),
-        shape(gdtp.shape[1]), shape(width), shape(N), shape(1), shape(1), shape(4), shape(1),
+        shape(*block.shape), shape(*gresid.shape), shape(rows), shape(rows), shape(rows),
+        shape(gdtp.shape[1]), shape(width), shape(N), shape(1), shape(1), shape(4), shape(1), shape(1, 128), shape(1, 1), shape(1, 1),
     ]
     spec = pl.BlockSpec(memory_space=pltpu.VMEM)
     return pl.pallas_call(
-        finish_kernel, out_shape=outs, in_specs=[spec] * 7, out_specs=[spec] * len(outs), name="finish",
-        compiler_params=pltpu.CompilerParams(vmem_limit_bytes=40 << 20),
-    )(block, gresid, ginx, ginz, goutp, gdtp, full)
+        functools.partial(finish_kernel, 1.0 / (2 * block.shape[0] * block.shape[1])),
+        out_shape=outs, in_specs=[spec] * 10, out_specs=[spec] * len(outs), name="finish",
+        compiler_params=pltpu.CompilerParams(vmem_limit_bytes=60 << 20),
+    )(block, gresid, ginx, ginz, goutp, gdtp, full, ggain, square, msquare)
 
 
 def per_device_split(
@@ -1015,18 +1078,18 @@
     doc_ids,
     cotangent,
 ):
-    block, gresid, grad_gain, ginx, ginz, goutp, gdtp, full, resid_square, mixed_square = block_call(
+    parts = block_call(
         in_proj_x, in_proj_z, out_proj, residual, cotangent, norm_gain[None], doc_ids[None], dt_proj, x_proj, conv_weight,
         conv_bias[None], dt_bias[None], a_log, d_skip[None],
     )
-    block, gresid, ginx, ginz, goutp, gdtp, g_xproj, g_alog, g_dtb, g_skip, g_convw, g_convb = finish_call(
-        block, gresid, ginx, ginz, goutp, gdtp, full, x_proj.shape[0]
-    )
-    rms_resid, rms_mixed = (jnp.sqrt(v[0, :1] / (doc_ids.shape[0] * D)) for v in (resid_square, mixed_square))
+    block, gresid, ggain, ginx, ginz, goutp, gdtp, full, square, msquare = parts
+    block, gresid, ginx, ginz, goutp, gdtp, g_xproj, g_alog, g_dtb, g_skip, g_convw, g_convb, ggain, rms, mrms = finish_call(
+        block, gresid, ginx, ginz, goutp, gdtp, full, ggain, square, msquare, x_proj.shape[0]
+    )
     return (
         block,
         gresid,
-        grad_gain[0],
+        ggain[0],
         ginx,
         ginz,
         g_xproj,
@@ -1037,8 +1100,8 @@
         g_alog,
         g_skip[0],
         goutp,
-        rms_resid,
-        rms_mixed,
+        rms[0],
+        mrms[0],
     )
 
 

time: 265 us -> 200 us (0.75)
  Pallas kernels: 249 us -> 198 us
  local copies, waits for them, and re-layouts: 11 us -> 0 us
  between operations: 4.32 us -> 0.82 us
    pallas_call x1, Pallas kernels: 246 us -> 193 us  [block_call(): pl.pallas_call(functools.partial(block_kernel, list(held)), out_shape=out...]
    unnamed x14 -> x0, local copies, waits for them, and re-layouts: 7.45 us -> none
where the time goes in v4:
time: 200 us; the launch traced here: 199 us
  Pallas kernels  198 us (99%)
    pallas_call x1, Pallas kernels, block_call(): pl.pallas_call(functools.partial(block_kernel, list(held)), out_shape=out...  193 us
    pallas_call x1, Pallas kernels, finish_call(): pl.pallas_call(functools.partial(finish_kernel, 1.0 / (2 * block.shape[0]...  4.54 us

profile of v4, /device:TPU:0, one launch (start us, length us, event | category | flops | bytes accessed | tf_op | source)
XLA Modules:
  0.0 198.7 jit_solution(5625817546700001579)
XLA Ops:
  0.7 193.3 %block.1 = (f32[64,2048]{1,0:T(8,128)}, f32[64,2048]{1,0:T(8,128)}, f32[8,128]{1,0:T(8,128)}, bf16[4,128,512]{2,1,0:T(8,128)(2,1)}, bf16[4,128,512]{2,1,0:T(8,12...) custom-call(bf16[128,2048]{1,0:T(8,128)(2,1)} %refs_0_.1, ...), custom_call_target="tpu_custom_call" | custom-call | tf_op jit(solution)/shard_map/block/pallas_call | solution.py:1012
  194.0 4.5 %finish.1 = (f32[64,2048]{1,0:T(8,128)}, f32[64,2048]{1,0:T(8,128)}, f32[128,2048]{1,0:T(8,128)}, f32[128,2048]{1,0:T(8,128)}, f32[128,2048]{1,0:T(8,128)}, /*in...) custom-call(f32[64,2048]{1,0:T(8,128)} %get-tuple-element.40.block_i, ...), custom_call_target="tpu_custom_call" | custom-call | tf_op jit(solution)/shard_map/finish/pallas_call | solution.py:1058

commit v5 on v4

--- a/solution.py
+++ b/solution.py
@@ -236,6 +236,11 @@
     def z_at(self, offset):
         return lax.rem(self.z + offset + NZ, NZ)
 
+    def slot(self, origin, device):
+        if device is self.c_mate:
+            return 2 * NZ
+        return origin // 4 + (NZ if device is self.x_mate else 0)
+
     def on_line(self, z, y=None):
         return (place(z, self.x, self.c), self.y if y is None else y)
 
@@ -250,7 +255,7 @@
 class Copies:
     def __init__(self, send_sems, own_sems):
         self.send_sems, self.own_sems = send_sems, own_sems
-        self.used, self.begun, self.kept = 0, [], []
+        self.used, self.groups, self.begun, self.kept = 0, [], [], []
 
     def new_sem(self):
         self.used += 1
@@ -258,8 +263,14 @@
 
     def group(self, whole):
         sem = self.new_sem()
-        self.begun.append((None, pltpu.make_async_copy(whole, whole, sem).wait))
+        self.groups.append((sem, pltpu.make_async_copy(whole, whole, sem).wait))
         return sem
+
+    def settle(self, *sems):
+        for sem, wait in self.groups:
+            if any(sem is one for one in sems):
+                wait()
+        self.groups = [(sem, wait) for sem, wait in self.groups if all(sem is not one for one in sems)]
 
     def send(self, src, dst, recv_sem, device, when=None, group=None):
         copy = pltpu.make_async_remote_copy(
@@ -279,13 +290,18 @@
         self.kept.append(copy)
 
     def wait_sent(self):
-        for when, wait in self.begun:
+        self.settle(*[sem for sem, _ in self.groups])
+        self.settle_alone(self.begun)
+        for copy in self.kept:
+            copy.wait()
+
+    def settle_alone(self, begun):
+        for when, wait in begun:
             if when is None:
                 wait()
             else:
                 pl.when(when)(wait)
-        for copy in self.kept:
-            copy.wait()
+        self.begun = [one for one in self.begun if all(one is not done for done in begun)]
 
 
 def arrived(dst, recv_sem, when=None):
@@ -305,38 +321,47 @@
     def columns(self, z):
         return self.src.at[:, pl.ds(pl.multiple_of(z * self.width, self.width), self.width)]
 
-    def push(self):
+    def push(self, offsets=(1, 2, 3, 0)):
         spot, me = self.spot, self.spot.dp
-        for offset in range(1, NZ):
+        for offset in offsets:
+            if offset == 0:
+                self.push_own()
+                continue
             z = spot.z_at(offset)
-            self.copies.send(self.columns(z), self.dst.at[me], self.recv_sems.at[me], spot.on_line(z), group=self.group)
+            self.copies.send(self.columns(z), self.dst.at[me], self.recv_sems.at[spot.z], spot.on_line(z), group=self.group)
+
+    def push_own(self):
+        spot, me = self.spot, self.spot.dp
         self.own = pltpu.make_async_copy(self.columns(spot.z), self.dst.at[me], self.own_sem)
         self.own.start()
-
-    def pass_on(self, origin, device):
-        sem = self.recv_sems.at[4 * NZ if device is self.spot.c_mate else origin]
-        self.copies.send(self.dst.at[origin], self.dst.at[origin], sem, device, group=self.group)
+        self.pass_on(me, spot.x_mate, self.columns(spot.z))
+        self.pass_on(me, spot.c_mate, self.columns(spot.z))
+
+    def pass_on(self, origin, device, src=None):
+        sem = self.recv_sems.at[self.spot.slot(origin, device)]
+        src = self.dst.at[origin] if src is None else src
+        self.copies.send(src, self.dst.at[origin], sem, device, group=self.group)
 
     def first(self):
         spot = self.spot
-        for offset in range(NZ):
-            origin = place(spot.z_at(-offset), spot.x, spot.c)
-            if offset == 0:
-                self.own.wait()
-            else:
-                arrived(self.dst.at[origin], self.recv_sems.at[origin])
+        for offset in range(1, NZ):
+            z = spot.z_at(-offset)
+            origin = place(z, spot.x, spot.c)
+            arrived(self.dst.at[origin], self.recv_sems.at[z])
             self.pass_on(origin, spot.x_mate)
             self.pass_on(origin, spot.c_mate)
 
     def second(self):
         spot = self.spot
         for offset in range(NZ):
-            origin = place(spot.z_at(-offset), 1 - spot.x, spot.c)
-            arrived(self.dst.at[origin], self.recv_sems.at[origin])
+            z = spot.z_at(-offset)
+            origin = place(z, 1 - spot.x, spot.c)
+            arrived(self.dst.at[origin], self.recv_sems.at[NZ + z])
             self.pass_on(origin, spot.c_mate)
 
     def last(self):
-        arrived(self.dst.at[pl.ds(0, 2 * NZ)], self.recv_sems.at[4 * NZ])
+        self.own.wait()
+        arrived(self.dst.at[pl.ds(0, 2 * NZ)], self.recv_sems.at[2 * NZ])
 
 
 class LineSum:
@@ -376,11 +401,16 @@
 class Share:
     def __init__(self, spot, copies, dst, recv_sems):
         self.spot, self.copies, self.dst, self.recv_sems = spot, copies, dst, recv_sems
-        self.over_y = copies.group(dst.at[pl.ds(0, NZ // 2)])
+        self.over_y, self.alone = copies.group(dst.at[pl.ds(0, NZ // 2)]), []
 
     def send(self, z, device, when=None):
         own = self.dst.at[z, self.spot.y]
         self.copies.send(own, own, self.recv_sems.at[z], device, when)
+        self.alone.append(self.copies.begun[-1])
+
+    def settle(self):
+        self.copies.settle(self.over_y)
+        self.copies.settle_alone(self.alone)
 
     def send_y(self, z, when=None):
         own = self.dst.at[z, self.spot.y]
@@ -408,8 +438,8 @@
 
 
 class Scan:
-    def __init__(self, maps, a_s, stepd_s, drive_s, gs_s, read_s, q_s, r_s, state_s, pulled_s, alog_s, spread_s, sum_s, gmap_s):
-        self.maps, self.a_s, self.stepd_s, self.drive_s, self.gs_s = maps, a_s, stepd_s, drive_s, gs_s
+    def __init__(self, a_s, stepd_s, drive_s, gs_s, read_s, q_s, r_s, state_s, pulled_s, alog_s, spread_s, sum_s, gmap_s):
+        self.a_s, self.stepd_s, self.drive_s, self.gs_s = a_s, stepd_s, drive_s, gs_s
         self.read_s, self.q_s, self.r_s, self.state_s = read_s, q_s, r_s, state_s
         self.pulled_s, self.alog_s, self.spread_s, self.sum_s, self.gmap_s = pulled_s, alog_s, spread_s, sum_s, gmap_s
         sub = lax.broadcasted_iota(jnp.int32, (8, 128), 0)
@@ -422,25 +452,32 @@
         tile = pl.ds(pl.multiple_of((base // 128) * 128, 128), 128)
         return base, tile, lax.rem(base, 128)
 
-    def spread(self, tile, first):
-        back = lax.rem(128 - first, 128)
-        for k in range(2):
-            moved = pltpu.roll(self.maps[k * N : (k + 1) * N, tile], back, 1)
-            for j in range(8):
-                self.spread_s[k, j] = jnp.broadcast_to(moved[:, j : j + 1], (N, 128))
+    def spread(self, maps, shifted_s):
+        rows = maps.shape[0]
+        for i in range(maps.shape[1] // 8):
+            tile, first = maps[:, i // 16 * 128 : (i // 16 + 1) * 128], i % 16 * 8
+            shifted_s[i * rows : (i + 1) * rows] = pltpu.roll(tile, (128 - first) % 128, 1).astype(BF16)
+        row = lax.broadcasted_iota(jnp.int32, (128, 8 * 128), 0)
+        column = lax.broadcasted_iota(jnp.int32, (128, 8 * 128), 1)
+        chosen = jnp.where(row == column // 128, 1.0, 0.0).astype(BF16)
+        self.spread_s[...] = dot(shifted_s[...], chosen).reshape(self.spread_s.shape)
+
+    def maps_at(self, i, j):
+        lanes = slice(j * 128, (j + 1) * 128)
+        return self.spread_s[i, :N, lanes], self.spread_s[i, N:, lanes]
 
     def forward(self, start, stop):
         def chunk(i, none):
-            base, tile, first = self.place(i)
-            self.spread(tile, first)
+            base = pl.multiple_of(i * 8, 8)
             for lanes in self.blocks:
                 state = self.state_s[i, :, lanes]
                 a = self.a_s[:, lanes]
                 stepd, drive = self.stepd_s[pl.ds(base, 8), lanes], self.drive_s[pl.ds(base, 8), lanes]
                 sums = RowSums(self.masks)
                 for j in range(8):
-                    state = jnp.exp(stepd[j : j + 1] * a) * state + drive[j : j + 1] * self.spread_s[0, j]
-                    read = state * self.spread_s[1, j]
+                    in_map, out_map = self.maps_at(i, j)
+                    state = jnp.exp(stepd[j : j + 1] * a) * state + drive[j : j + 1] * in_map
+                    read = state * out_map
                     sums.add(j, read[:8] + read[8:])
                 self.state_s[i + 1, :, lanes] = state
                 self.read_s[pl.ds(base, 8), lanes] = sums.result
@@ -452,7 +489,6 @@
         def chunk(step, none):
             i = start + stop - 1 - step
             base, tile, first = self.place(i)
-            self.spread(tile, first)
             for b, lanes in enumerate(self.blocks):
                 a = self.a_s[:, lanes]
                 stepd, drive = self.stepd_s[pl.ds(base, 8), lanes], self.drive_s[pl.ds(base, 8), lanes]
@@ -460,16 +496,17 @@
                 states, decays = [self.state_s[i, :, lanes]], []
                 for j in range(8):
                     decays.append(jnp.exp(stepd[j : j + 1] * a))
-                    states.append(decays[j] * states[j] + drive[j : j + 1] * self.spread_s[0, j])
+                    states.append(decays[j] * states[j] + drive[j : j + 1] * self.maps_at(i, j)[0])
                 pulled, alog = self.pulled_s[:, lanes], self.alog_s[:, lanes]
                 q_sums, r_sums = RowSums(self.masks), RowSums(self.masks)
                 for j in reversed(range(8)):
-                    adjoint = pulled + self.spread_s[1, j] * gs[j : j + 1]
+                    in_map, out_map = self.maps_at(i, j)
+                    adjoint = pulled + out_map * gs[j : j + 1]
                     g_in, g_out = adjoint * drive[j : j + 1], states[j + 1] * gs[j : j + 1]
                     if b > 0:
                         g_in, g_out = g_in + self.sum_s[0, j], g_out + self.sum_s[1, j]
                     self.sum_s[0, j], self.sum_s[1, j] = g_in, g_out
-                    q_t = adjoint * self.spread_s[0, j]
+                    q_t = adjoint * in_map
                     q_sums.add(j, q_t[:8] + q_t[8:])
                     pulled = decays[j] * adjoint
                     past = pulled * states[j]
@@ -562,12 +599,12 @@
             z = spot.z_at(offset)
             for x in range(2):
                 self.copies.send(
-                    self.part.at[z, x, 1 - spot.c], self.c_land.at[z, x], self.c_sems.at[z], spot.c_mate, group=self.groups[0]
+                    self.part.at[place(z, x, 1 - spot.c)], self.c_land.at[z, x], self.c_sems.at[z], spot.c_mate, group=self.groups[0]
                 )
 
     def add(self, z, x, landed):
-        part = self.part
-        part[z, x, self.spot.c] = (part[z, x, self.spot.c].astype(F32) + landed.astype(F32)).astype(part.dtype)
+        part, owner = self.part, place(z, x, self.spot.c)
+        part[owner] = (part[owner].astype(F32) + landed.astype(F32)).astype(part.dtype)
 
     def second(self):
         spot = self.spot
@@ -577,7 +614,7 @@
             for x in range(2):
                 self.add(z, x, self.c_land[z, x])
             self.copies.send(
-                self.part.at[z, 1 - spot.x, spot.c], self.x_land.at[z], self.x_sems.at[z], spot.x_mate, group=self.groups[1]
+                self.part.at[place(z, 1 - spot.x, spot.c)], self.x_land.at[z], self.x_sems.at[z], spot.x_mate, group=self.groups[1]
             )
 
     def third(self, offsets=(1, 2, 3, 0)):
@@ -586,7 +623,7 @@
             z = spot.z_at(offset)
             arrived(self.x_land.at[z], self.x_sems.at[z])
             self.add(z, spot.x, self.x_land[z])
-            own = self.part.at[z, spot.x, spot.c]
+            own = self.part.at[place(z, spot.x, spot.c)]
             if offset:
                 self.copies.send(own, self.z_land.at[spot.z], self.z_sem, spot.on_line(z), group=self.groups[2])
             else:
@@ -613,7 +650,7 @@
 
     def spread(self, origin, device, src=None):
         src = self.full.at[origin] if src is None else src
-        sem = self.full_sems.at[4 * NZ if device is self.spot.c_mate else origin]
+        sem = self.full_sems.at[self.spot.slot(origin, device)]
         self.copies.send(src, self.full.at[origin], sem, device, group=self.group)
 
     def third(self):
@@ -627,20 +664,22 @@
     def fourth(self):
         spot = self.spot
         for offset in (1, 2, 3):
-            origin = place(spot.z_at(-offset), spot.x, spot.c)
-            arrived(self.full.at[origin], self.full_sems.at[origin])
+            z = spot.z_at(-offset)
+            origin = place(z, spot.x, spot.c)
+            arrived(self.full.at[origin], self.full_sems.at[z])
             self.spread(origin, spot.x_mate)
             self.spread(origin, spot.c_mate)
 
     def fifth(self):
         spot = self.spot
         for offset in range(NZ):
-            origin = place(spot.z_at(-offset), 1 - spot.x, spot.c)
-            arrived(self.full.at[origin], self.full_sems.at[origin])
+            z = spot.z_at(-offset)
+            origin = place(z, 1 - spot.x, spot.c)
+            arrived(self.full.at[origin], self.full_sems.at[NZ + z])
             self.spread(origin, spot.c_mate)
 
     def last(self):
-        arrived(self.full.at[pl.ds(0, 2 * NZ)], self.full_sems.at[4 * NZ])
+        arrived(self.full.at[pl.ds(0, 2 * NZ)], self.full_sems.at[2 * NZ])
 
 
 class Held:
@@ -652,7 +691,7 @@
 def block_scratch(half, feats, rows, chans, step_rows, width):
     tokens, n_dp, length = 2 * half * NZ, 4 * NZ, 2 * half
     vmem, dma = pltpu.VMEM, pltpu.SemaphoreType.DMA
-    owners, steps = (NZ, 2, 2, rows, chans), (NZ, 2, 2, step_rows, chans)
+    owners, steps = (n_dp, rows, chans), (n_dp, step_rows, chans)
     part = (NZ, 2, width // 2, length)
     small = (width + 32) // 4
     held = {
@@ -666,14 +705,15 @@
         "gated": vmem((tokens, chans), BF16),
         "ggate": vmem((tokens, chans), BF16),
     }
-    for name in ("x_in", "pre", "gate", "gg", "raw", "stepd", "drive", "gs", "read", "r"):
+    for name in ("x_in", "pre", "gate", "gg", "raw", "stepd", "drive", "gs", "read"):
         held[name] = vmem((tokens, chans), F32)
     held |= {
         "a": vmem((N, chans), F32),
         "state": vmem((tokens // 8 + 1, N, chans), F32),
         "pulled": vmem((N, chans), F32),
         "alog": vmem((N, chans), F32),
-        "spread": vmem((2, 8, N, 128), F32),
+        "spread": vmem((tokens // 8, 2 * N, 8 * 128), F32),
+        "shifted": vmem((tokens // 8 * 2 * N, 128), BF16),
         "sum": vmem((2, 8, N, 128), F32),
         "gmap": vmem((2 * N, tokens), F32),
         "dbl": vmem((width, tokens), F32),
@@ -681,10 +721,8 @@
         "landing": vmem((2, 2 * NZ) + part[2:], BF16),
         "total": vmem((2,) + part, BF16),
         "mixed": vmem((NZ, 2, half, feats), BF16),
-        "normed": vmem((NZ, 2, half, feats), BF16),
         "outw": vmem(owners, BF16),
         "ginz": vmem(owners, BF16),
-        "ginx": vmem(owners, BF16),
         "gdtp": vmem(steps, F32),
         "chan": vmem((2, 2, small, chans), F32),
         "y_land": vmem((2, NZ, half, feats), BF16),
@@ -699,12 +737,19 @@
         "block": vmem((half, feats), F32),
         "gresid": vmem((half, feats), F32),
         "tile": vmem((4, 8, 128), F32),
-        "gain": vmem((3, n_dp, 8, 128), F32),
+        "gain_part": vmem((2, n_dp, 128), F32),
+        "gain": vmem((n_dp, 8, 128), F32),
+        "gain_total": vmem((8, 128), F32),
+        "squares": vmem((2, 8, 128), F32),
         "gain_land": vmem((n_dp - 1, 8, 128), F32),
+        "resid": vmem((half, feats), F32),
+        "cot": vmem((half, feats), F32),
+        "xproj": vmem((width, chans * NZ), BF16),
+        "load_sems": dma((3,)),
         "send_sems": dma((56,)),
-        "keep_sems": dma((7,)),
+        "keep_sems": dma((9,)),
         "own_sems": dma((4,)),
-        "w_sems": dma((4, n_dp + 1)),
+        "w_sems": dma((4, 2 * NZ + 1)),
         "act_sems": dma((2, NZ + 1)),
         "info_sem": dma(()),
         "dbl_sems": dma((2, 2)),
@@ -714,7 +759,7 @@
         "wx_sems": dma((4, NZ)),
         "wz_sems": dma((4,)),
         "f_sems": dma((2,)),
-        "full_sems": dma((n_dp + 1,)),
+        "full_sems": dma((2 * NZ + 1,)),
         "tile_sems": dma((2,)),
         "gain_sems": dma((2,)),
     }
@@ -723,12 +768,19 @@
 
 def block_kernel(names, *refs):
     (
-        inx_ref, inz_ref, outp_ref, resid_ref, cot_ref, gain_ref, ids_ref, dtp_ref, xproj_ref, convw_ref, convb_ref, dtb_ref,
+        inx_ref, inz_ref, outp_ref, resid_in, cot_in, xproj_in, gain_ref, ids_ref, dtp_ref, convw_ref, convb_ref, dtb_ref,
         alog_ref, skip_ref,
-        block_ref, gresid_ref, ggain_ref, ginx_ref, ginz_ref, goutp_ref, gdtp_ref, full_ref, square_ref, msquare_ref,
-    ) = refs[:24]
-    s = Held(names, refs[24:])
+        block_ref, gresid_ref, ggain_ref, ginx_ref, ginz_ref, goutp_ref, gdtp_ref, full_ref, squares_ref,
+    ) = refs[:23]
+    s = Held(names, refs[23:])
     spot = Spot()
+    resid_ref, cot_ref, xproj_ref = s.resid, s.cot, s.xproj
+    loads = [
+        pltpu.make_async_copy(src, dst, s.load_sems.at[k])
+        for k, (src, dst) in enumerate(((resid_in, s.resid), (cot_in, s.cot), (xproj_in, s.xproj)))
+    ]
+    for load in loads:
+        load.start()
     plane = [lax.rem(spot.dp + offset, 4 * NZ) for offset in range(1, 4 * NZ)]
     greet([(dp, spot.y) for dp in plane] + [spot.on_line(spot.z_at(dz), 1 - spot.y) for dz in range(NZ)])
     copies = Copies(s.send_sems, s.keep_sems)
@@ -736,6 +788,9 @@
     half, feats = resid_ref.shape
     length = 2 * half
     columns = pl.ds(pl.multiple_of(spot.z * chans, chans), chans)
+    quarters = [
+        (slice(k * feats // NZ, (k + 1) * feats // NZ), slice(k * NZ, (k + 1) * NZ)) for k in range(NZ)
+    ]
     sequences = [slice(k * length, (k + 1) * length) for k in range(NZ)]
 
     s.dtp_own[...] = dtp_ref[...].astype(F32)
@@ -759,6 +814,7 @@
         copies.send(s.info.at[spot.dp], s.info.at[spot.dp], s.info_sem, (dp, spot.y), group=info_group)
     inx.push()
 
+    loads[0].wait()
     resid = resid_ref[...]
     row_square = jnp.sum(resid * resid, axis=1, keepdims=True)
     scaled = resid * lax.rsqrt(row_square / feats + eps_norm)
@@ -770,22 +826,23 @@
         s.acts[0, spot.z, spot.y, :, cols] = (scaled[:, cols] * s.info[k, 0:1, :]).astype(BF16)
     normed.push()
     dtp.push()
+    loads[1].wait()
+    loads[2].wait()
     s.acts[1, spot.z, spot.y] = cot_ref[...].astype(BF16)
     for k in range(NZ):
         s.mask[k] = column_masks(s.info[place(k, spot.x, spot.c)])
     inx.first()
     normed.first(1)
     inx.second()
+    normed.first(2)
     inz.push()
-    normed.first(2)
     dtp.first()
     dtp.second()
+    normed.first(3)
     cot.push()
-    normed.first(3)
     normed.last()
     inx.last()
 
-    tokens_x = s.acts.at[0], s.acts.at[1]
     all_normed = s.acts[0].reshape(tokens, feats)
     s.x_in[...] = dot(all_normed, s.w[0].reshape(-1, chans))
     taps = convw_ref[:, columns]
@@ -807,10 +864,11 @@
         spot, copies, s.part.at[0], s.landing.at[0], s.total.at[0], s.dbl_sems.at[0]
     )
     x_dbl.push()
-    outp.push()
+    inz.first()
     cot.first(1)
+    outp.push((1, 0))
     x_dbl.middle()
-    inz.first()
+    outp.push((2, 3))
     cot.first(2)
     x_dbl.last()
 
@@ -826,69 +884,79 @@
     s.a[...] = -jnp.exp(alog_ref[:, columns])
     s.state[0] = jnp.zeros((N, chans), F32)
     scan = Scan(
-        s.dbl.at[R : R + 2 * N], s.a, s.stepd, s.drive, s.gs, s.read, s.read, s.r, s.state, s.pulled, s.alog, s.spread, s.sum, s.gmap
-    )
+        s.a, s.stepd, s.drive, s.gs, s.read, s.read, s.gate, s.state, s.pulled, s.alog, s.spread, s.sum, s.gmap
+    )
+    scan.spread(s.dbl[R : R + 2 * N], s.shifted)
     steps = tokens // 8
-    scan.forward(0, steps // 4)
+    eighth = steps // 8
     inz.second()
-    scan.forward(steps // 4, steps // 2)
+    scan.forward(0, 4 * eighth)
+    outp.first()
     cot.first(3)
-    scan.forward(steps // 2, 3 * steps // 4)
-    outp.first()
-    scan.forward(3 * steps // 4, steps)
-    outp.second()
+    scan.forward(4 * eighth, steps)
     inz.last()
     s.gate[...] = dot(s.acts[0].reshape(tokens, feats), s.w[1].reshape(-1, chans))
+    skip = skip_ref[:, columns]
+    for rows in sequences:
+        gate = s.gate[rows]
+        scanned = s.read[rows] + skip * s.low[rows].astype(F32)
+        s.gated[rows] = (scanned * gate * sigmoid(gate)).astype(BF16)
+
+    mixed_sum, normed_sum = (
+        TokenSum(spot, copies, part, s.y_land.at[k], s.z_land.at[k], s.y_sems.at[k], s.z_sems.at[k])
+        for k, part in enumerate((s.mixed, s.acts.at[1]))
+    )
+    outw_sum, ginz_sum, ginx_sum, gdtp_sum = (
+        RowSum(spot, copies, part, c_land, x_land, out, s.wc_sems.at[k], s.wx_sems.at[k], s.wz_sems.at[k])
+        for k, (part, c_land, x_land, out) in enumerate((
+            (s.outw, s.wc_land.at[0], s.wx_land.at[0], goutp_ref),
+            (s.ginz, s.wc_land.at[1], s.wx_land.at[1], ginz_ref),
+            (s.w.at[2], s.wc_land.at[2], s.wx_land.at[2], ginx_ref),
+            (s.gdtp, s.dc_land, s.dx_land, gdtp_ref),
+        ))
+    )
+    outp.second()
     cot.last()
+    for cols, owners in quarters:
+        given = s.acts[1, :, :, :, cols].reshape(tokens, -1)
+        s.outw[owners] = dot(given, s.gated[...], TN).astype(BF16).reshape(-1, *s.outw.shape[1:])
+    outw_sum.push()
     outp.last()
     s.gg[...] = dot(s.acts[1].reshape(tokens, feats), s.w[2].reshape(-1, chans))
-    skip = skip_ref[:, columns]
+    outw_sum.second()
+    for cols, owners in quarters:
+        part = dot(s.gated[...], s.w[2, owners].reshape(-1, chans), NT)
+        s.mixed[:, :, :, cols] = part.astype(BF16).reshape(*s.mixed.shape[:3], -1)
+    mixed_sum.push()
     for rows in sequences:
         gate, gg = s.gate[rows], s.gg[rows]
         sig = sigmoid(gate)
         scanned = s.read[rows] + skip * s.low[rows].astype(F32)
         s.gs[rows] = gg * gate * sig
-        s.gated[rows] = (scanned * gate * sig).astype(BF16)
         s.ggate[rows] = (gg * scanned * sig * (1.0 + gate * (1.0 - sig))).astype(BF16)
-
-    mixed_sum, normed_sum = (
-        TokenSum(spot, copies, part, s.y_land.at[k], s.z_land.at[k], s.y_sems.at[k], s.z_sems.at[k])
-        for k, part in enumerate((s.mixed, s.normed))
-    )
-    outw_sum, ginz_sum, ginx_sum, gdtp_sum = (
-        RowSum(spot, copies, part, c_land, x_land, out, s.wc_sems.at[k], s.wx_sems.at[k], s.wz_sems.at[k])
-        for k, (part, c_land, x_land, out) in enumerate((
-            (s.outw, s.wc_land.at[0], s.wx_land.at[0], goutp_ref),
-            (s.ginz, s.wc_land.at[1], s.wx_land.at[1], ginz_ref),
-            (s.ginx, s.wc_land.at[2], s.wx_land.at[2], ginx_ref),
-            (s.gdtp, s.dc_land, s.dx_land, gdtp_ref),
-        ))
-    )
-    s.mixed[...] = dot(s.gated[...], s.w[2].reshape(-1, chans), NT).astype(BF16).reshape(s.mixed.shape)
-    mixed_sum.push()
-    s.outw[...] = dot(s.acts[1].reshape(tokens, feats), s.gated[...], TN).astype(BF16).reshape(s.outw.shape)
-    outw_sum.push()
-    s.ginz[...] = dot(s.acts[0].reshape(tokens, feats), s.ggate[...], TN).astype(BF16).reshape(s.ginz.shape)
+    outw_sum.third((1,))
+    for cols, owners in quarters:
+        given = s.acts[0, :, :, :, cols].reshape(tokens, -1)
+        s.ginz[owners] = dot(given, s.ggate[...], TN).astype(BF16).reshape(-1, *s.ginz.shape[1:])
     ginz_sum.push()
 
     s.pulled[...] = jnp.zeros_like(s.pulled)
     s.alog[...] = jnp.zeros_like(s.alog)
-    outw_sum.second()
-    scan.backward(steps - steps // 4, steps)
+    scan.backward(7 * eighth, steps)
+    outw_sum.third((2,))
     ginz_sum.second()
+    scan.backward(6 * eighth, 7 * eighth)
+    outw_sum.third((3, 0))
+    scan.backward(3 * eighth, 6 * eighth)
+    ginz_sum.third((1,))
     mixed_sum.stage(3)
-    scan.backward(steps // 2, steps - steps // 4)
-    outw_sum.third()
-    mixed_sum.stage(2)
-    scan.backward(steps // 4, steps // 2)
-    scan.backward(0, steps // 4)
-
+    scan.backward(0, 3 * eighth)
     grad_bias = jnp.zeros((1, chans), F32)
     grad_skip = jnp.zeros((1, chans), F32)
     raw_rows = []
     for rows in sequences:
         conv, raw, gs, q = s.low[rows].astype(F32), s.raw[rows], s.gs[rows], s.read[rows]
-        grad_raw = (conv * q + s.r[rows]) * sigmoid(raw)
+        grad_raw = (conv * q + s.gate[rows]) * sigmoid(raw)
         s.gg[rows] = softplus(raw) * q + skip * gs
         grad_bias = grad_bias + jnp.sum(grad_raw, axis=0, keepdims=True)
         grad_skip = grad_skip + jnp.sum(gs * conv, axis=0, keepdims=True)
@@ -904,8 +972,8 @@
     s.gdtp[...] = dot(s.dbl[:R].astype(BF16), raw_low).reshape(s.gdtp.shape)
     gdtp_sum.push()
     grad_dbl_sum.middle()
-    mixed_sum.stage(1)
-    ginz_sum.third()
+    ginz_sum.third((2, 3, 0))
+    mixed_sum.stage(2)
     gdtp_sum.second()
     grad_dbl_sum.last()
 
@@ -928,8 +996,15 @@
             grad_x = grad_x + taps[3 - back : 4 - back] * pltpu.roll(masked, length - back, 0)
         low_rows.append(grad_x.astype(BF16))
     grad_xin = jnp.concatenate(low_rows, axis=0)
-    grad_normed = dot(grad_xin, s.w[0].reshape(-1, chans), NT) + dot(s.ggate[...], s.w[1].reshape(-1, chans), NT)
-    s.normed[...] = grad_normed.astype(BF16).reshape(s.normed.shape)
+    cot.settle()
+    for cols, owners in quarters:
+        part = dot(grad_xin, s.w[0, owners].reshape(-1, chans), NT) + dot(s.ggate[...], s.w[1, owners].reshape(-1, chans), NT)
+        s.acts[1, :, :, :, cols] = part.astype(BF16).reshape(*s.mixed.shape[:3], -1)
+        gain_part = jnp.sum(part * s.acts[0, :, :, :, cols].reshape(tokens, -1).astype(F32), axis=0, keepdims=True)
+        for k in range(NZ):
+            owner = owners.start + k
+            s.gain_part[0, owner : owner + 1] = gain_part[:, k * 128 : (k + 1) * 128] / s.info[owner, 0:1]
+    copies.send(s.gain_part.at[0], s.gain_part.at[1], s.gain_sems.at[0], spot.y_mate)
     normed_sum.push()
     s.chan[...] = jnp.concatenate(
         [dot(grad_dbl, s.low[...]), s.alog[...] * s.a[...], grad_bias, grad_skip, jnp.zeros((6, chans), F32)]
@@ -939,24 +1014,25 @@
         spot, copies, s.chan, s.fc_land, s.fx_land, s.f_own, full_ref, s.f_sems.at[0], s.f_sems.at[1], s.full_sems
     )
     small_sum.push()
-    s.ginx[...] = dot(s.acts[0].reshape(tokens, feats), grad_xin, TN).astype(BF16).reshape(s.ginx.shape)
+    copies.settle(outp.group)
+    for cols, owners in quarters:
+        given = s.acts[0, :, :, :, cols].reshape(tokens, -1)
+        s.w[2, owners] = dot(given, grad_xin, TN).astype(BF16).reshape(-1, *s.outw.shape[1:])
     ginx_sum.push()
     small_sum.second()
-    gain_part = jnp.sum(grad_normed * s.acts[0].reshape(tokens, feats).astype(F32), axis=0, keepdims=True)
-    for k in range(4 * NZ):
-        s.gain[0, k] = jnp.broadcast_to(gain_part[:, k * 128 : (k + 1) * 128], (8, 128)) / s.info[k, 0:1]
-    copies.send(s.gain.at[0], s.gain.at[1], s.gain_sems.at[0], spot.y_mate)
+    mixed_sum.stage(1)
+    normed_sum.stage(3)
     ginx_sum.second()
     gdtp_sum.third()
-    normed_sum.stage(3)
+    arrived(s.gain_part.at[1], s.gain_sems.at[0])
+    for k in range(4 * NZ):
+        s.gain[k] = jnp.broadcast_to(s.gain_part[0, k : k + 1] + s.gain_part[1, k : k + 1], (8, 128))
+    gain_group = copies.group(s.gain_land)
+    for offset, dp in enumerate(plane):
+        copies.send(s.gain.at[dp], s.gain_land.at[offset], s.gain_sems.at[1], (dp, spot.y), group=gain_group)
     small_sum.third()
     normed_sum.stage(2)
     ginx_sum.third((1, 2))
-    arrived(s.gain.at[1], s.gain_sems.at[0])
-    s.gain[2] = s.gain[0] + s.gain[1]
-    gain_group = copies.group(s.gain_land)
-    for offset, dp in enumerate(plane):
-        copies.send(s.gain.at[2, dp], s.gain_land.at[offset], s.gain_sems.at[1], (dp, spot.y), group=gain_group)
     normed_sum.stage(1)
     ginx_sum.third((3, 0))
     small_sum.fourth()
@@ -967,19 +1043,15 @@
     copies.keep(s.block, block_ref)
     s.tile[2] = jnp.broadcast_to(jnp.sum(jnp.sum(mixed * mixed, axis=1, keepdims=True), axis=0, keepdims=True), (8, 128))
     copies.send(s.tile.at[2], s.tile.at[3], s.tile_sems.at[1], spot.y_mate)
-    arrived(s.gain_land, s.gain_sems.at[1])
-    total = s.gain[2, spot.dp]
-    for offset in range(4 * NZ - 1):
-        total = total + s.gain_land[offset]
-    ggain_ref[...] = total
     small_sum.fifth()
     outw_sum.last()
     ginz_sum.last()
     gdtp_sum.last()
     arrived(s.tile.at[1], s.tile_sems.at[0])
-    square_ref[...] = s.tile[0] + s.tile[1]
+    s.squares[0] = s.tile[0] + s.tile[1]
     arrived(s.tile.at[3], s.tile_sems.at[1])
-    msquare_ref[...] = s.tile[2] + s.tile[3]
+    s.squares[1] = s.tile[2] + s.tile[3]
+    copies.keep(s.squares, squares_ref)
 
     grad_rows = normed_sum.last()
     inv = lax.rsqrt(jnp.sum(resid * resid, axis=1, keepdims=True) / feats + eps_norm)
@@ -989,6 +1061,12 @@
     mean = jnp.sum(grad_scaled * scaled, axis=1, keepdims=True) / feats
     s.gresid[...] = cot_ref[...] + inv * (grad_scaled - scaled * mean)
     copies.keep(s.gresid, gresid_ref)
+    arrived(s.gain_land, s.gain_sems.at[1])
+    total = s.gain[spot.dp]
+    for offset in range(4 * NZ - 1):
+        total = total + s.gain_land[offset]
+    s.gain_total[...] = total
+    copies.keep(s.gain_total, ggain_ref)
     ginx_sum.last()
     small_sum.last()
     copies.wait_sent()
@@ -1005,61 +1083,99 @@
         shape((half, feats), F32), shape((half, feats), F32), shape((8, 128), F32),
         shape((NZ, rows, chans), BF16), shape((NZ, rows, chans), BF16), shape((NZ, rows, chans), BF16),
         shape((NZ, dt_p.shape[0], chans), F32), shape((n_dp, (x_proj.shape[0] + 32) // 4, chans), BF16),
-        shape((8, 128), F32), shape((8, 128), F32),
+        shape((2, 8, 128), F32),
     ]
     in_any = pl.BlockSpec(memory_space=pl.ANY)
     in_vmem = pl.BlockSpec(memory_space=pltpu.VMEM)
     return pl.pallas_call(
         functools.partial(block_kernel, list(held)),
         out_shape=outs,
-        in_specs=[in_any] * 3 + [in_vmem] * 11,
-        out_specs=[in_any] * 2 + [in_vmem] + [in_any] * 5 + [in_vmem] * 2,
+        in_specs=[in_any] * 6 + [in_vmem] * 8,
+        out_specs=[in_any] * len(outs),
         scratch_shapes=list(held.values()),
         name="block",
         compiler_params=pltpu.CompilerParams(collective_id=1, has_side_effects=True, vmem_limit_bytes=62 << 20),
-    )(in_x, in_z, out_p, residual, cotangent, gain, ids, dt_p, x_proj, conv_w, conv_b, dt_b, a_log, d_skip)
+    )(in_x, in_z, out_p, residual, cotangent, x_proj, gain, ids, dt_p, conv_w, conv_b, dt_b, a_log, d_skip)
 
 
 def finish_kernel(
-    scale, block_in, gresid_in, ginx_in, ginz_in, goutp_in, gdtp_in, full_in, ggain_in, square_in, msquare_in,
+    scale, block_in, gresid_in, ginx_in, ginz_in, goutp_in, gdtp_in, full_in, ggain_in, squares_in,
     block_ref, gresid_ref, ginx_ref, ginz_ref, goutp_ref, gdtp_ref, xproj_ref, alog_ref, dtb_ref, skip_ref, convw_ref, convb_ref,
     ggain_ref, rms_ref, mrms_ref,
+    token_s, low_s, wide_s, step_s, full_s, xproj_s, in_sems, out_sems,
 ):
-    block_ref[...] = block_in[...]
-    gresid_ref[...] = gresid_in[...]
+    begun = []
+
+    def out(src, dst):
+        copy = pltpu.make_async_copy(src, dst, out_sems.at[len(begun)])
+        copy.start()
+        begun.append(copy)
+
+    reads = [
+        pltpu.make_async_copy(src, dst, in_sems.at[k])
+        for k, (src, dst) in enumerate(
+            (
+                (block_in, token_s.at[0]), (gresid_in, token_s.at[1]),
+                (ginx_in, low_s.at[0]), (ginz_in, low_s.at[1]), (goutp_in, low_s.at[2]), (full_in, full_s), (gdtp_in, step_s),
+            )
+        )
+    ]
+    for read in reads:
+        read.start()
+    for k, ref in enumerate((block_ref, gresid_ref)):
+        reads[k].wait()
+        out(token_s.at[k], ref)
     ggain_ref[...] = ggain_in[0:1]
-    rms_ref[...] = jnp.sqrt(square_in[0:1, 0:1] * scale)
-    mrms_ref[...] = jnp.sqrt(msquare_in[0:1, 0:1] * scale)
-    chans = ginx_in.shape[2]
-    for z in range(NZ):
-        cols = slice(z * chans, (z + 1) * chans)
-        for given, ref in ((ginx_in, ginx_ref), (ginz_in, ginz_ref), (goutp_in, goutp_ref), (gdtp_in, gdtp_ref)):
-            ref[:, cols] = given[z].astype(F32)
-        rows = full_in.shape[1]
+    rms_ref[...] = jnp.sqrt(squares_in[0, 0:1, 0:1] * scale)
+    mrms_ref[...] = jnp.sqrt(squares_in[1, 0:1, 0:1] * scale)
+    chans = low_s.shape[3]
+    columns = [slice(z * chans, (z + 1) * chans) for z in range(NZ)]
+    for k, ref in enumerate((ginx_ref, ginz_ref, goutp_ref)):
+        reads[k + 2].wait()
+        for z, cols in enumerate(columns):
+            wide_s[k, :, cols] = low_s[k, z].astype(F32)
+        out(wide_s.at[k], ref)
+    reads[5].wait()
+    rows, width = full_s.shape[1], xproj_s.shape[0]
+    for z, cols in enumerate(columns):
         for k in range(4):
-            found = full_in[place(z, k % 2, k // 2)].astype(F32)
-            upto = min(rows, xproj_ref.shape[0] - k * rows)
-            xproj_ref[k * rows : k * rows + upto, cols] = found[:upto]
+            found = full_s[place(z, k % 2, k // 2)].astype(F32)
+            upto = min(rows, width - k * rows)
+            xproj_s[k * rows : k * rows + upto, cols] = found[:upto]
         alog_ref[:, cols] = found[upto : upto + N]
         dtb_ref[:, cols] = found[upto + N : upto + N + 1]
         skip_ref[:, cols] = found[upto + N + 1 : upto + N + 2]
         convw_ref[:, cols] = found[upto + 24 : upto + 28]
         convb_ref[:, cols] = found[upto + 28 : upto + 29]
-
-
-def finish_call(block, gresid, ginx, ginz, goutp, gdtp, full, ggain, square, msquare, width):
-    rows, wide = ginx.shape[1], ginx.shape[2] * NZ
+    out(xproj_s, xproj_ref)
+    reads[6].wait()
+    for z, cols in enumerate(columns):
+        gdtp_ref[:, cols] = step_s[z]
+    for copy in begun:
+        copy.wait()
+
+
+def finish_call(block, gresid, ginx, ginz, goutp, gdtp, full, ggain, squares, width):
+    rows, chans = ginx.shape[1:]
+    wide = chans * NZ
     shape = lambda count, columns=wide: jax.ShapeDtypeStruct((count, columns), F32)
-    outs = [
-        shape(*block.shape), shape(*gresid.shape), shape(rows), shape(rows), shape(rows),
-        shape(gdtp.shape[1]), shape(width), shape(N), shape(1), shape(1), shape(4), shape(1), shape(1, 128), shape(1, 1), shape(1, 1),
-    ]
-    spec = pl.BlockSpec(memory_space=pltpu.VMEM)
+    vmem, dma = pltpu.VMEM, pltpu.SemaphoreType.DMA
+    in_any, in_vmem = pl.BlockSpec(memory_space=pl.ANY), pl.BlockSpec(memory_space=vmem)
     return pl.pallas_call(
         functools.partial(finish_kernel, 1.0 / (2 * block.shape[0] * block.shape[1])),
-        out_shape=outs, in_specs=[spec] * 10, out_specs=[spec] * len(outs), name="finish",
+        out_shape=[
+            shape(*block.shape), shape(*gresid.shape), shape(rows), shape(rows), shape(rows), shape(gdtp.shape[1]), shape(width),
+            shape(N), shape(1), shape(1), shape(4), shape(1), shape(1, 128), shape(1, 1), shape(1, 1),
+        ],
+        in_specs=[in_any] * 7 + [in_vmem] * 2,
+        out_specs=[in_any] * 5 + [in_vmem] + [in_any] + [in_vmem] * 8,
+        scratch_shapes=[
+            vmem((2,) + block.shape, F32), vmem((3,) + ginx.shape, BF16), vmem((3, rows, wide), F32), vmem(gdtp.shape, F32), vmem(full.shape, BF16),
+            vmem((width, wide), F32), dma((7,)), dma((6,)),
+        ],
+        name="finish",
         compiler_params=pltpu.CompilerParams(vmem_limit_bytes=60 << 20),
-    )(block, gresid, ginx, ginz, goutp, gdtp, full, ggain, square, msquare)
+    )(block, gresid, ginx, ginz, goutp, gdtp, full, ggain, squares)
 
 
 def per_device_split(
@@ -1082,9 +1198,9 @@
         in_proj_x, in_proj_z, out_proj, residual, cotangent, norm_gain[None], doc_ids[None], dt_proj, x_proj, conv_weight,
         conv_bias[None], dt_bias[None], a_log, d_skip[None],
     )
-    block, gresid, ggain, ginx, ginz, goutp, gdtp, full, square, msquare = parts
+    block, gresid, ggain, ginx, ginz, goutp, gdtp, full, squares = parts
     block, gresid, ginx, ginz, goutp, gdtp, g_xproj, g_alog, g_dtb, g_skip, g_convw, g_convb, ggain, rms, mrms = finish_call(
-        block, gresid, ginx, ginz, goutp, gdtp, full, ggain, square, msquare, x_proj.shape[0]
+        block, gresid, ginx, ginz, goutp, gdtp, full, ggain, squares, x_proj.shape[0]
     )
     return (
         block,

time: 200 us -> 186 us (0.930)
  Pallas kernels: 198 us -> 184 us
    pallas_call x1, Pallas kernels: 193 us -> 179 us  [block_call(): pl.pallas_call(functools.partial(block_kernel, list(held)), out_shape=out...]
where the time goes in v5:
time: 186 us; the launch traced here: 185 us
  Pallas kernels  184 us (99%)
    pallas_call x1, Pallas kernels, block_call(): pl.pallas_call(functools.partial(block_kernel, list(held)), out_shape=out...  179 us
    pallas_call x1, Pallas kernels, finish_call(): pl.pallas_call(functools.partial(finish_kernel, 1.0 / (2 * block.shape[0]...  5.04 us

profile of v5, /device:TPU:0, one launch (start us, length us, event | category | flops | bytes accessed | tf_op | source)
XLA Modules:
  0.0 184.8 jit_solution(15758904824629305581)
XLA Ops:
  0.7 179.0 %block.1 = (f32[64,2048]{1,0:T(8,128)}, f32[64,2048]{1,0:T(8,128)}, f32[8,128]{1,0:T(8,128)}, bf16[4,128,512]{2,1,0:T(8,128)(2,1)}, bf16[4,128,512]{2,1,0:T(8,12...) custom-call(bf16[128,2048]{1,0:T(8,128)(2,1)} %refs_0_.1, ...), custom_call_target="tpu_custom_call" | custom-call | tf_op jit(solution)/shard_map/block/pallas_call | solution.py:1090
  179.6 5.0 %finish.1 = (f32[64,2048]{1,0:T(8,128)}, f32[64,2048]{1,0:T(8,128)}, f32[128,2048]{1,0:T(8,128)}, f32[128,2048]{1,0:T(8,128)}, f32[128,2048]{1,0:T(8,128)}, /*in...) custom-call(f32[64,2048]{1,0:T(8,128)} %get-tuple-element.39.block_i, ...), custom_call_target="tpu_custom_call" | custom-call | tf_op jit(solution)/shard_map/finish/pallas_call | solution.py:1164

commit v6 on v5

--- a/solution.py
+++ b/solution.py
@@ -233,6 +233,12 @@
         self.c_mate = (place(self.z, self.x, 1 - self.c), self.y)
         self.y_mate = (self.dp, 1 - self.y)
 
+        far, near = jnp.where(self.z < 2, 3, 0), 1 + self.z % 2
+        self.others = [far, 6 - self.z - far - near, near]
+
+    def turn(self, k):
+        return self.others[k - 1] if k else self.z
+
     def z_at(self, offset):
         return lax.rem(self.z + offset + NZ, NZ)
 
@@ -327,7 +333,7 @@
             if offset == 0:
                 self.push_own()
                 continue
-            z = spot.z_at(offset)
+            z = spot.turn(offset)
             self.copies.send(self.columns(z), self.dst.at[me], self.recv_sems.at[spot.z], spot.on_line(z), group=self.group)
 
     def push_own(self):
@@ -345,7 +351,7 @@
     def first(self):
         spot = self.spot
         for offset in range(1, NZ):
-            z = spot.z_at(-offset)
+            z = spot.turn(offset)
             origin = place(z, spot.x, spot.c)
             arrived(self.dst.at[origin], self.recv_sems.at[z])
             self.pass_on(origin, spot.x_mate)
@@ -354,7 +360,7 @@
     def second(self):
         spot = self.spot
         for offset in range(NZ):
-            z = spot.z_at(-offset)
+            z = spot.turn(offset)
             origin = place(z, 1 - spot.x, spot.c)
             arrived(self.dst.at[origin], self.recv_sems.at[NZ + z])
             self.pass_on(origin, spot.c_mate)
@@ -596,7 +602,7 @@
     def push(self):
         spot = self.spot
         for offset in (1, 2, 3, 0):
-            z = spot.z_at(offset)
+            z = spot.turn(offset)
             for x in range(2):
                 self.copies.send(
                     self.part.at[place(z, x, 1 - spot.c)], self.c_land.at[z, x], self.c_sems.at[z], spot.c_mate, group=self.groups[0]
@@ -609,7 +615,7 @@
     def second(self):
         spot = self.spot
         for offset in (1, 2, 3, 0):
-            z = spot.z_at(offset)
+            z = spot.turn(offset)
             arrived(self.c_land.at[z], self.c_sems.at[z])
             for x in range(2):
                 self.add(z, x, self.c_land[z, x])
@@ -620,7 +626,7 @@
     def third(self, offsets=(1, 2, 3, 0)):
         spot = self.spot
         for offset in offsets:
-            z = spot.z_at(offset)
+            z = spot.turn(offset)
             arrived(self.x_land.at[z], self.x_sems.at[z])
             self.add(z, spot.x, self.x_land[z])
             own = self.part.at[place(z, spot.x, spot.c)]
@@ -866,11 +872,11 @@
     x_dbl.push()
     inz.first()
     cot.first(1)
+    x_dbl.middle()
     outp.push((1, 0))
-    x_dbl.middle()
-    outp.push((2, 3))
     cot.first(2)
     x_dbl.last()
+    outp.push((2, 3))
 
     dtp.last()
     for k, y in blocks:
@@ -891,8 +897,8 @@
     eighth = steps // 8
     inz.second()
     scan.forward(0, 4 * eighth)
+    cot.first(3)
     outp.first()
-    cot.first(3)
     scan.forward(4 * eighth, steps)
     inz.last()
     s.gate[...] = dot(s.acts[0].reshape(tokens, feats), s.w[1].reshape(-1, chans))
@@ -915,15 +921,16 @@
             (s.gdtp, s.dc_land, s.dx_land, gdtp_ref),
         ))
     )
-    outp.second()
     cot.last()
     for cols, owners in quarters:
         given = s.acts[1, :, :, :, cols].reshape(tokens, -1)
         s.outw[owners] = dot(given, s.gated[...], TN).astype(BF16).reshape(-1, *s.outw.shape[1:])
     outw_sum.push()
+    outp.second()
+    outw_sum.second()
     outp.last()
     s.gg[...] = dot(s.acts[1].reshape(tokens, feats), s.w[2].reshape(-1, chans))
-    outw_sum.second()
+    outw_sum.third((1,))
     for cols, owners in quarters:
         part = dot(s.gated[...], s.w[2, owners].reshape(-1, chans), NT)
         s.mixed[:, :, :, cols] = part.astype(BF16).reshape(*s.mixed.shape[:3], -1)
@@ -934,7 +941,6 @@
         scanned = s.read[rows] + skip * s.low[rows].astype(F32)
         s.gs[rows] = gg * gate * sig
         s.ggate[rows] = (gg * scanned * sig * (1.0 + gate * (1.0 - sig))).astype(BF16)
-    outw_sum.third((1,))
     for cols, owners in quarters:
         given = s.acts[0, :, :, :, cols].reshape(tokens, -1)
         s.ginz[owners] = dot(given, s.ggate[...], TN).astype(BF16).reshape(-1, *s.ginz.shape[1:])
@@ -947,10 +953,12 @@
     ginz_sum.second()
     scan.backward(6 * eighth, 7 * eighth)
     outw_sum.third((3, 0))
-    scan.backward(3 * eighth, 6 * eighth)
+    mixed_sum.stage(3)
+    scan.backward(4 * eighth, 6 * eighth)
     ginz_sum.third((1,))
-    mixed_sum.stage(3)
-    scan.backward(0, 3 * eighth)
+    scan.backward(2 * eighth, 4 * eighth)
+    ginz_sum.third((2,))
+    scan.backward(0, 2 * eighth)
     grad_bias = jnp.zeros((1, chans), F32)
     grad_skip = jnp.zeros((1, chans), F32)
     raw_rows = []
@@ -972,7 +980,7 @@
     s.gdtp[...] = dot(s.dbl[:R].astype(BF16), raw_low).reshape(s.gdtp.shape)
     gdtp_sum.push()
     grad_dbl_sum.middle()
-    ginz_sum.third((2, 3, 0))
+    ginz_sum.third((3, 0))
     mixed_sum.stage(2)
     gdtp_sum.second()
     grad_dbl_sum.last()
@@ -996,6 +1004,11 @@
             grad_x = grad_x + taps[3 - back : 4 - back] * pltpu.roll(masked, length - back, 0)
         low_rows.append(grad_x.astype(BF16))
     grad_xin = jnp.concatenate(low_rows, axis=0)
+    copies.settle(outp.group)
+    for cols, owners in quarters:
+        given = s.acts[0, :, :, :, cols].reshape(tokens, -1)
+        s.w[2, owners] = dot(given, grad_xin, TN).astype(BF16).reshape(-1, *s.outw.shape[1:])
+    ginx_sum.push()
     cot.settle()
     for cols, owners in quarters:
         part = dot(grad_xin, s.w[0, owners].reshape(-1, chans), NT) + dot(s.ggate[...], s.w[1, owners].reshape(-1, chans), NT)
@@ -1006,6 +1019,7 @@
             s.gain_part[0, owner : owner + 1] = gain_part[:, k * 128 : (k + 1) * 128] / s.info[owner, 0:1]
     copies.send(s.gain_part.at[0], s.gain_part.at[1], s.gain_sems.at[0], spot.y_mate)
     normed_sum.push()
+    mixed_sum.stage(1)
     s.chan[...] = jnp.concatenate(
         [dot(grad_dbl, s.low[...]), s.alog[...] * s.a[...], grad_bias, grad_skip, jnp.zeros((6, chans), F32)]
         + sums + [jnp.zeros((3, chans), F32)], axis=0
@@ -1014,27 +1028,22 @@
         spot, copies, s.chan, s.fc_land, s.fx_land, s.f_own, full_ref, s.f_sems.at[0], s.f_sems.at[1], s.full_sems
     )
     small_sum.push()
-    copies.settle(outp.group)
-    for cols, owners in quarters:
-        given = s.acts[0, :, :, :, cols].reshape(tokens, -1)
-        s.w[2, owners] = dot(given, grad_xin, TN).astype(BF16).reshape(-1, *s.outw.shape[1:])
-    ginx_sum.push()
-    small_sum.second()
-    mixed_sum.stage(1)
-    normed_sum.stage(3)
     ginx_sum.second()
     gdtp_sum.third()
+    ginx_sum.third((1,))
+    normed_sum.stage(3)
+    small_sum.second()
+    ginx_sum.third((2,))
     arrived(s.gain_part.at[1], s.gain_sems.at[0])
     for k in range(4 * NZ):
         s.gain[k] = jnp.broadcast_to(s.gain_part[0, k : k + 1] + s.gain_part[1, k : k + 1], (8, 128))
     gain_group = copies.group(s.gain_land)
     for offset, dp in enumerate(plane):
         copies.send(s.gain.at[dp], s.gain_land.at[offset], s.gain_sems.at[1], (dp, spot.y), group=gain_group)
+    normed_sum.stage(2)
+    ginx_sum.third((3, 0))
     small_sum.third()
-    normed_sum.stage(2)
-    ginx_sum.third((1, 2))
     normed_sum.stage(1)
-    ginx_sum.third((3, 0))
     small_sum.fourth()
 
     mixed = mixed_sum.last()

time: 186 us -> 180 us (0.968)
  Pallas kernels: 184 us -> 179 us
    pallas_call x1, Pallas kernels: 179 us -> 174 us  [block_call(): pl.pallas_call(functools.partial(block_kernel, list(held)), out_shape=out...]
where the time goes in v6:
time: 180 us
  Pallas kernels  179 us (99%)
    pallas_call x1, Pallas kernels, block_call(): pl.pallas_call(functools.partial(block_kernel, list(held)), out_shape=out...  174 us
    pallas_call x1, Pallas kernels, finish_call(): pl.pallas_call(functools.partial(finish_kernel, 1.0 / (2 * block.shape[0]...  5.04 us

profile of v6, /device:TPU:0, one launch (start us, length us, event | category | flops | bytes accessed | tf_op | source)
XLA Modules:
  0.0 179.9 jit_solution(14272095501748624539)
XLA Ops:
  0.7 174.1 %block.1 = (f32[64,2048]{1,0:T(8,128)}, f32[64,2048]{1,0:T(8,128)}, f32[8,128]{1,0:T(8,128)}, bf16[4,128,512]{2,1,0:T(8,128)(2,1)}, bf16[4,128,512]{2,1,0:T(8,12...) custom-call(bf16[128,2048]{1,0:T(8,128)(2,1)} %refs_0_.1, ...), custom_call_target="tpu_custom_call" | custom-call | tf_op jit(solution)/shard_map/block/pallas_call | solution.py:1099
  174.7 5.0 %finish.1 = (f32[64,2048]{1,0:T(8,128)}, f32[64,2048]{1,0:T(8,128)}, f32[128,2048]{1,0:T(8,128)}, f32[128,2048]{1,0:T(8,128)}, f32[128,2048]{1,0:T(8,128)}, /*in...) custom-call(f32[64,2048]{1,0:T(8,128)} %get-tuple-element.39.block_i, ...), custom_call_target="tpu_custom_call" | custom-call | tf_op jit(solution)/shard_map/finish/pallas_call | solution.py:1173

commit v7 on v6

--- a/solution.py
+++ b/solution.py
@@ -370,6 +370,21 @@
         arrived(self.dst.at[pl.ds(0, 2 * NZ)], self.recv_sems.at[2 * NZ])
 
 
+class BlockGather(Gather):
+    def columns(self, z):
+        return self.src.at[z]
+
+
+def fold_columns(values):
+    half = values.shape[-1] // 2
+    return jnp.concatenate([values[..., :half], values[..., half:]], axis=-2)
+
+
+def unfold_columns(values):
+    rows = values.shape[-2] // 2
+    return jnp.concatenate([values[..., :rows, :], values[..., rows:, :]], axis=-1)
+
+
 class LineSum:
     def __init__(self, spot, copies, part, landing, total, sems):
         self.spot, self.copies, self.part, self.landing, self.total, self.sems = spot, copies, part, landing, total, sems
@@ -422,11 +437,12 @@
         own = self.dst.at[z, self.spot.y]
         self.copies.send(own, own, self.recv_sems.at[NZ], self.spot.y_mate, when, self.over_y)
 
-    def push(self):
+    def push(self, over_y=True):
         spot = self.spot
         self.send(spot.z, spot.on_line(spot.z_at(1)), spot.z < NZ - 1)
         self.send(spot.z, spot.on_line(spot.z_at(-1)), spot.z > 0)
-        self.send_y(spot.z)
+        if over_y:
+            self.send_y(spot.z)
 
     def first(self, far):
         spot = self.spot
@@ -697,14 +713,14 @@
 def block_scratch(half, feats, rows, chans, step_rows, width):
     tokens, n_dp, length = 2 * half * NZ, 4 * NZ, 2 * half
     vmem, dma = pltpu.VMEM, pltpu.SemaphoreType.DMA
-    owners, steps = (n_dp, rows, chans), (n_dp, step_rows, chans)
+    owners, steps = (n_dp, rows, chans), (n_dp, 2 * step_rows, chans // 2)
     part = (NZ, 2, width // 2, length)
     small = (width + 32) // 4
     held = {
         "w": vmem((3, n_dp, rows, chans), BF16),
         "acts": vmem((2, NZ, 2, half, feats), BF16),
-        "dtp_own": vmem((step_rows, chans * NZ), F32),
-        "dtp": vmem((n_dp, step_rows, chans), F32),
+        "dtp_own": vmem((NZ,) + steps[1:], BF16),
+        "dtp": vmem(steps, BF16),
         "info": vmem((n_dp, 8, 128), F32),
         "mask": vmem((NZ, length, 128), F32),
         "low": vmem((tokens, chans), BF16),
@@ -729,14 +745,14 @@
         "mixed": vmem((NZ, 2, half, feats), BF16),
         "outw": vmem(owners, BF16),
         "ginz": vmem(owners, BF16),
-        "gdtp": vmem(steps, F32),
+        "gdtp": vmem(steps, BF16),
         "chan": vmem((2, 2, small, chans), F32),
         "y_land": vmem((2, NZ, half, feats), BF16),
         "z_land": vmem((2, 2, NZ, half, feats), BF16),
         "wc_land": vmem((3, NZ, 2, rows, chans), BF16),
         "wx_land": vmem((3, NZ, rows, chans), BF16),
-        "dc_land": vmem((NZ, 2, step_rows, chans), F32),
-        "dx_land": vmem((NZ, step_rows, chans), F32),
+        "dc_land": vmem((NZ, 2) + steps[1:], BF16),
+        "dx_land": vmem((NZ,) + steps[1:], BF16),
         "fc_land": vmem((2, small, chans), F32),
         "fx_land": vmem((small, chans), F32),
         "f_own": vmem((small, chans), BF16),
@@ -751,7 +767,13 @@
         "resid": vmem((half, feats), F32),
         "cot": vmem((half, feats), F32),
         "xproj": vmem((width, chans * NZ), BF16),
-        "load_sems": dma((3,)),
+        "ids": vmem((1, length), jnp.int32),
+        "convw": vmem((4, chans * NZ), F32),
+        "convb": vmem((1, chans * NZ), F32),
+        "dtb": vmem((1, chans * NZ), F32),
+        "alog_in": vmem((N, chans * NZ), F32),
+        "skip": vmem((1, chans * NZ), F32),
+        "load_sems": dma((9,)),
         "send_sems": dma((56,)),
         "keep_sems": dma((9,)),
         "own_sems": dma((4,)),
@@ -774,16 +796,21 @@
 
 def block_kernel(names, *refs):
     (
-        inx_ref, inz_ref, outp_ref, resid_in, cot_in, xproj_in, gain_ref, ids_ref, dtp_ref, convw_ref, convb_ref, dtb_ref,
-        alog_ref, skip_ref,
+        inx_ref, inz_ref, outp_ref, resid_in, cot_in, xproj_in, ids_in, convw_in, convb_in, dtb_in, alog_in, skip_in, gain_ref, dtp_ref,
         block_ref, gresid_ref, ggain_ref, ginx_ref, ginz_ref, goutp_ref, gdtp_ref, full_ref, squares_ref,
     ) = refs[:23]
     s = Held(names, refs[23:])
     spot = Spot()
-    resid_ref, cot_ref, xproj_ref = s.resid, s.cot, s.xproj
+    resid_ref, cot_ref, xproj_ref, ids_ref = s.resid, s.cot, s.xproj, s.ids
+    convw_ref, convb_ref, dtb_ref, alog_ref, skip_ref = s.convw, s.convb, s.dtb, s.alog_in, s.skip
     loads = [
         pltpu.make_async_copy(src, dst, s.load_sems.at[k])
-        for k, (src, dst) in enumerate(((resid_in, s.resid), (cot_in, s.cot), (xproj_in, s.xproj)))
+        for k, (src, dst) in enumerate(
+            (
+                (ids_in, s.ids), (resid_in, s.resid), (cot_in, s.cot), (xproj_in, s.xproj), (convw_in, s.convw),
+                (convb_in, s.convb), (dtb_in, s.dtb), (alog_in, s.alog_in), (skip_in, s.skip),
+            )
+        )
     ]
     for load in loads:
         load.start()
@@ -799,13 +826,16 @@
     ]
     sequences = [slice(k * length, (k + 1) * length) for k in range(NZ)]
 
-    s.dtp_own[...] = dtp_ref[...].astype(F32)
-    inx, inz, outp, dtp = (
-        Gather(spot, copies, src, dst, s.w_sems.at[k], s.own_sems.at[k])
-        for k, (src, dst) in enumerate(((inx_ref, s.w.at[0]), (inz_ref, s.w.at[1]), (outp_ref, s.w.at[2]), (s.dtp_own, s.dtp)))
-    )
+    step_rows = dtp_ref[...].astype(F32)
+    for z in range(NZ):
+        s.dtp_own[z] = fold_columns(step_rows[:, z * chans : (z + 1) * chans]).astype(BF16)
+    inx, inz, outp = (
+        Gather(spot, copies, src, s.w.at[k], s.w_sems.at[k], s.own_sems.at[k]) for k, src in enumerate((inx_ref, inz_ref, outp_ref))
+    )
+    dtp = BlockGather(spot, copies, s.dtp_own, s.dtp, s.w_sems.at[3], s.own_sems.at[3])
     normed, cot = (Share(spot, copies, s.acts.at[k], s.act_sems.at[k]) for k in range(2))
 
+    loads[0].wait()
     ids = jnp.broadcast_to(ids_ref[...], (8, length))
     lane = lax.broadcasted_iota(jnp.int32, (8, length), 1)
     sub = lax.broadcasted_iota(jnp.int32, (8, length), 0)
@@ -820,7 +850,7 @@
         copies.send(s.info.at[spot.dp], s.info.at[spot.dp], s.info_sem, (dp, spot.y), group=info_group)
     inx.push()
 
-    loads[0].wait()
+    loads[1].wait()
     resid = resid_ref[...]
     row_square = jnp.sum(resid * resid, axis=1, keepdims=True)
     scaled = resid * lax.rsqrt(row_square / feats + eps_norm)
@@ -832,8 +862,8 @@
         s.acts[0, spot.z, spot.y, :, cols] = (scaled[:, cols] * s.info[k, 0:1, :]).astype(BF16)
     normed.push()
     dtp.push()
-    loads[1].wait()
-    loads[2].wait()
+    for load in loads[2:]:
+        load.wait()
     s.acts[1, spot.z, spot.y] = cot_ref[...].astype(BF16)
     for k in range(NZ):
         s.mask[k] = column_masks(s.info[place(k, spot.x, spot.c)])
@@ -841,12 +871,14 @@
     normed.first(1)
     inx.second()
     normed.first(2)
-    inz.push()
+    inz.push((3, 0))
     dtp.first()
     dtp.second()
     normed.first(3)
-    cot.push()
+    inz.push((1, 2))
+    cot.push(False)
     normed.last()
+    cot.send_y(spot.z)
     inx.last()
 
     all_normed = s.acts[0].reshape(tokens, feats)
@@ -881,7 +913,7 @@
     dtp.last()
     for k, y in blocks:
         s.dbl[y * width : (y + 1) * width, sequences[k]] = s.total[0, k, y].astype(F32)
-    step_w = s.dtp[...].reshape(R, chans).astype(BF16)
+    step_w = unfold_columns(s.dtp[...].astype(F32)).reshape(R, chans).astype(BF16)
     s.raw[...] = dot(s.dbl[:R].astype(BF16), step_w, TN) + dtb_ref[:, columns]
     for k, rows in enumerate(sequences):
         step = softplus(s.raw[rows])
@@ -977,7 +1009,8 @@
         spot, copies, s.part.at[1], s.landing.at[1], s.total.at[1], s.dbl_sems.at[1]
     )
     grad_dbl_sum.push()
-    s.gdtp[...] = dot(s.dbl[:R].astype(BF16), raw_low).reshape(s.gdtp.shape)
+    grad_step = dot(s.dbl[:R].astype(BF16), raw_low).reshape(4 * NZ, -1, chans)
+    s.gdtp[...] = fold_columns(grad_step).astype(BF16)
     gdtp_sum.push()
     grad_dbl_sum.middle()
     ginz_sum.third((3, 0))
@@ -1091,7 +1124,7 @@
     outs = [
         shape((half, feats), F32), shape((half, feats), F32), shape((8, 128), F32),
         shape((NZ, rows, chans), BF16), shape((NZ, rows, chans), BF16), shape((NZ, rows, chans), BF16),
-        shape((NZ, dt_p.shape[0], chans), F32), shape((n_dp, (x_proj.shape[0] + 32) // 4, chans), BF16),
+        shape((NZ, 2 * dt_p.shape[0], chans // 2), BF16), shape((n_dp, (x_proj.shape[0] + 32) // 4, chans), BF16),
         shape((2, 8, 128), F32),
     ]
     in_any = pl.BlockSpec(memory_space=pl.ANY)
@@ -1099,19 +1132,19 @@
     return pl.pallas_call(
         functools.partial(block_kernel, list(held)),
         out_shape=outs,
-        in_specs=[in_any] * 6 + [in_vmem] * 8,
+        in_specs=[in_any] * 12 + [in_vmem] * 2,
         out_specs=[in_any] * len(outs),
         scratch_shapes=list(held.values()),
         name="block",
         compiler_params=pltpu.CompilerParams(collective_id=1, has_side_effects=True, vmem_limit_bytes=62 << 20),
-    )(in_x, in_z, out_p, residual, cotangent, x_proj, gain, ids, dt_p, conv_w, conv_b, dt_b, a_log, d_skip)
+    )(in_x, in_z, out_p, residual, cotangent, x_proj, ids, conv_w, conv_b, dt_b, a_log, d_skip, gain, dt_p)
 
 
 def finish_kernel(
     scale, block_in, gresid_in, ginx_in, ginz_in, goutp_in, gdtp_in, full_in, ggain_in, squares_in,
     block_ref, gresid_ref, ginx_ref, ginz_ref, goutp_ref, gdtp_ref, xproj_ref, alog_ref, dtb_ref, skip_ref, convw_ref, convb_ref,
     ggain_ref, rms_ref, mrms_ref,
-    token_s, low_s, wide_s, step_s, full_s, xproj_s, in_sems, out_sems,
+    token_s, low_s, step_s, full_s, ggain_s, squares_s, wide_s, gdtp_s, xproj_s, rows_s, in_sems, out_sems,
 ):
     begun = []
 
@@ -1124,42 +1157,44 @@
         pltpu.make_async_copy(src, dst, in_sems.at[k])
         for k, (src, dst) in enumerate(
             (
-                (block_in, token_s.at[0]), (gresid_in, token_s.at[1]),
                 (ginx_in, low_s.at[0]), (ginz_in, low_s.at[1]), (goutp_in, low_s.at[2]), (full_in, full_s), (gdtp_in, step_s),
+                (block_in, token_s.at[0]), (gresid_in, token_s.at[1]), (ggain_in, ggain_s), (squares_in, squares_s),
             )
         )
     ]
     for read in reads:
         read.start()
-    for k, ref in enumerate((block_ref, gresid_ref)):
-        reads[k].wait()
-        out(token_s.at[k], ref)
-    ggain_ref[...] = ggain_in[0:1]
-    rms_ref[...] = jnp.sqrt(squares_in[0, 0:1, 0:1] * scale)
-    mrms_ref[...] = jnp.sqrt(squares_in[1, 0:1, 0:1] * scale)
     chans = low_s.shape[3]
     columns = [slice(z * chans, (z + 1) * chans) for z in range(NZ)]
     for k, ref in enumerate((ginx_ref, ginz_ref, goutp_ref)):
-        reads[k + 2].wait()
+        reads[k].wait()
         for z, cols in enumerate(columns):
             wide_s[k, :, cols] = low_s[k, z].astype(F32)
         out(wide_s.at[k], ref)
-    reads[5].wait()
+    reads[3].wait()
     rows, width = full_s.shape[1], xproj_s.shape[0]
     for z, cols in enumerate(columns):
         for k in range(4):
             found = full_s[place(z, k % 2, k // 2)].astype(F32)
             upto = min(rows, width - k * rows)
             xproj_s[k * rows : k * rows + upto, cols] = found[:upto]
-        alog_ref[:, cols] = found[upto : upto + N]
-        dtb_ref[:, cols] = found[upto + N : upto + N + 1]
-        skip_ref[:, cols] = found[upto + N + 1 : upto + N + 2]
-        convw_ref[:, cols] = found[upto + 24 : upto + 28]
-        convb_ref[:, cols] = found[upto + 28 : upto + 29]
+        rows_s[:, cols] = found[upto:]
     out(xproj_s, xproj_ref)
-    reads[6].wait()
+    out(rows_s.at[pl.ds(0, N)], alog_ref)
+    for at, ref in ((N, dtb_ref), (N + 1, skip_ref), (24, convw_ref), (28, convb_ref)):
+        out(rows_s.at[pl.ds(at, ref.shape[0])], ref)
+    reads[4].wait()
     for z, cols in enumerate(columns):
-        gdtp_ref[:, cols] = step_s[z]
+        gdtp_s[:, cols] = unfold_columns(step_s[z].astype(F32))
+    out(gdtp_s, gdtp_ref)
+    for k, ref in enumerate((block_ref, gresid_ref)):
+        reads[5 + k].wait()
+        out(token_s.at[k], ref)
+    reads[7].wait()
+    out(ggain_s.at[pl.ds(0, 1)], ggain_ref)
+    reads[8].wait()
+    for k, ref in enumerate((rms_ref, mrms_ref)):
+        ref[...] = jnp.sqrt(squares_s[k, 0:1, 0:1] * scale)
     for copy in begun:
         copy.wait()
 
@@ -1169,18 +1204,20 @@
     wide = chans * NZ
     shape = lambda count, columns=wide: jax.ShapeDtypeStruct((count, columns), F32)
     vmem, dma = pltpu.VMEM, pltpu.SemaphoreType.DMA
-    in_any, in_vmem = pl.BlockSpec(memory_space=pl.ANY), pl.BlockSpec(memory_space=vmem)
+    in_any = pl.BlockSpec(memory_space=pl.ANY)
+    outs = [
+        shape(*block.shape), shape(*gresid.shape), shape(rows), shape(rows), shape(rows), shape(gdtp.shape[1] // 2), shape(width),
+        shape(N), shape(1), shape(1), shape(4), shape(1), shape(1, 128), shape(1, 1), shape(1, 1),
+    ]
     return pl.pallas_call(
         functools.partial(finish_kernel, 1.0 / (2 * block.shape[0] * block.shape[1])),
-        out_shape=[
-            shape(*block.shape), shape(*gresid.shape), shape(rows), shape(rows), shape(rows), shape(gdtp.shape[1]), shape(width),
-            shape(N), shape(1), shape(1), shape(4), shape(1), shape(1, 128), shape(1, 1), shape(1, 1),
-        ],
-        in_specs=[in_any] * 7 + [in_vmem] * 2,
-        out_specs=[in_any] * 5 + [in_vmem] + [in_any] + [in_vmem] * 8,
+        out_shape=outs,
+        in_specs=[in_any] * 9,
+        out_specs=[in_any] * (len(outs) - 2) + [pl.BlockSpec(memory_space=vmem)] * 2,
         scratch_shapes=[
-            vmem((2,) + block.shape, F32), vmem((3,) + ginx.shape, BF16), vmem((3, rows, wide), F32), vmem(gdtp.shape, F32), vmem(full.shape, BF16),
-            vmem((width, wide), F32), dma((7,)), dma((6,)),
+            vmem((2,) + block.shape, F32), vmem((3,) + ginx.shape, BF16), vmem(gdtp.shape, BF16), vmem(full.shape, BF16),
+            vmem(ggain.shape, F32), vmem(squares.shape, F32), vmem((3, rows, wide), F32), vmem((gdtp.shape[1] // 2, wide), F32),
+            vmem((width, wide), F32), vmem((32, wide), F32), dma((9,)), dma((len(outs) - 2,)),
         ],
         name="finish",
         compiler_params=pltpu.CompilerParams(vmem_limit_bytes=60 << 20),

time: 180 us -> 177 us (0.983)
  Pallas kernels: 179 us -> 176 us
    pallas_call x1, Pallas kernels: 174 us -> 172 us  [block_call(): pl.pallas_call(functools.partial(block_kernel, list(held)), out_shape=out...]
where the time goes in v7:
time: 177 us
  Pallas kernels  176 us (99%)
    pallas_call x1, Pallas kernels, block_call(): pl.pallas_call(functools.partial(block_kernel, list(held)), out_shape=out...  172 us
    pallas_call x1, Pallas kernels, finish_call(): pl.pallas_call(functools.partial(finish_kernel, 1.0 / (2 * block.shape[0]...  4.33 us

profile of v7, /device:TPU:0, one launch (start us, length us, event | category | flops | bytes accessed | tf_op | source)
XLA Modules:
  0.0 177.0 jit_solution(1699697691845674408)
XLA Ops:
  0.7 171.8 %block.1 = (f32[64,2048]{1,0:T(8,128)}, f32[64,2048]{1,0:T(8,128)}, f32[8,128]{1,0:T(8,128)}, bf16[4,128,512]{2,1,0:T(8,128)(2,1)}, bf16[4,128,512]{2,1,0:T(8,12...) custom-call(bf16[128,2048]{1,0:T(8,128)(2,1)} %refs_0_.1, ...), custom_call_target="tpu_custom_call" | custom-call | tf_op jit(solution)/shard_map/block/pallas_call | solution.py:1132
  172.5 4.3 %finish.1 = (f32[64,2048]{1,0:T(8,128)}, f32[64,2048]{1,0:T(8,128)}, f32[128,2048]{1,0:T(8,128)}, f32[128,2048]{1,0:T(8,128)}, f32[128,2048]{1,0:T(8,128)}, /*in...) custom-call(f32[64,2048]{1,0:T(8,128)} %get-tuple-element.39.block_i, ...), custom_call_target="tpu_custom_call" | custom-call | tf_op jit(solution)/shard_map/finish/pallas_call | solution.py:1212

commit v8 on v7

--- a/solution.py
+++ b/solution.py
@@ -1013,8 +1013,8 @@
     s.gdtp[...] = fold_columns(grad_step).astype(BF16)
     gdtp_sum.push()
     grad_dbl_sum.middle()
+    mixed_sum.stage(2)
     ginz_sum.third((3, 0))
-    mixed_sum.stage(2)
     gdtp_sum.second()
     grad_dbl_sum.last()
 
@@ -1037,11 +1037,20 @@
             grad_x = grad_x + taps[3 - back : 4 - back] * pltpu.roll(masked, length - back, 0)
         low_rows.append(grad_x.astype(BF16))
     grad_xin = jnp.concatenate(low_rows, axis=0)
+    s.chan[...] = jnp.concatenate(
+        [dot(grad_dbl, s.low[...]), s.alog[...] * s.a[...], grad_bias, grad_skip, jnp.zeros((6, chans), F32)]
+        + sums + [jnp.zeros((3, chans), F32)], axis=0
+    ).reshape(s.chan.shape)
+    small_sum = ChannelSum(
+        spot, copies, s.chan, s.fc_land, s.fx_land, s.f_own, full_ref, s.f_sems.at[0], s.f_sems.at[1], s.full_sems
+    )
+    small_sum.push()
     copies.settle(outp.group)
     for cols, owners in quarters:
         given = s.acts[0, :, :, :, cols].reshape(tokens, -1)
         s.w[2, owners] = dot(given, grad_xin, TN).astype(BF16).reshape(-1, *s.outw.shape[1:])
     ginx_sum.push()
+    small_sum.second()
     cot.settle()
     for cols, owners in quarters:
         part = dot(grad_xin, s.w[0, owners].reshape(-1, chans), NT) + dot(s.ggate[...], s.w[1, owners].reshape(-1, chans), NT)
@@ -1053,19 +1062,11 @@
     copies.send(s.gain_part.at[0], s.gain_part.at[1], s.gain_sems.at[0], spot.y_mate)
     normed_sum.push()
     mixed_sum.stage(1)
-    s.chan[...] = jnp.concatenate(
-        [dot(grad_dbl, s.low[...]), s.alog[...] * s.a[...], grad_bias, grad_skip, jnp.zeros((6, chans), F32)]
-        + sums + [jnp.zeros((3, chans), F32)], axis=0
-    ).reshape(s.chan.shape)
-    small_sum = ChannelSum(
-        spot, copies, s.chan, s.fc_land, s.fx_land, s.f_own, full_ref, s.f_sems.at[0], s.f_sems.at[1], s.full_sems
-    )
-    small_sum.push()
     ginx_sum.second()
     gdtp_sum.third()
     ginx_sum.third((1,))
     normed_sum.stage(3)
-    small_sum.second()
+    small_sum.third()
     ginx_sum.third((2,))
     arrived(s.gain_part.at[1], s.gain_sems.at[0])
     for k in range(4 * NZ):
@@ -1075,7 +1076,6 @@
         copies.send(s.gain.at[dp], s.gain_land.at[offset], s.gain_sems.at[1], (dp, spot.y), group=gain_group)
     normed_sum.stage(2)
     ginx_sum.third((3, 0))
-    small_sum.third()
     normed_sum.stage(1)
     small_sum.fourth()
 

time: 177 us -> 175 us (0.989)
  Pallas kernels: 176 us -> 174 us
    pallas_call x1, Pallas kernels: 172 us -> 170 us  [block_call(): pl.pallas_call(functools.partial(block_kernel, list(held)), out_shape=out...]
where the time goes in v8:
time: 175 us
  Pallas kernels  174 us (99%)
    pallas_call x1, Pallas kernels, block_call(): pl.pallas_call(functools.partial(block_kernel, list(held)), out_shape=out...  170 us
    pallas_call x1, Pallas kernels, finish_call(): pl.pallas_call(functools.partial(finish_kernel, 1.0 / (2 * block.shape[0]...  4.33 us

profile of v8, /device:TPU:0, one launch (start us, length us, event | category | flops | bytes accessed | tf_op | source)
XLA Modules:
  0.0 174.9 jit_solution(14767531129410746756)
XLA Ops:
  0.7 169.8 %block.1 = (f32[64,2048]{1,0:T(8,128)}, f32[64,2048]{1,0:T(8,128)}, f32[8,128]{1,0:T(8,128)}, bf16[4,128,512]{2,1,0:T(8,128)(2,1)}, bf16[4,128,512]{2,1,0:T(8,12...) custom-call(bf16[128,2048]{1,0:T(8,128)(2,1)} %refs_0_.1, ...), custom_call_target="tpu_custom_call" | custom-call | tf_op jit(solution)/shard_map/block/pallas_call | solution.py:1132
  170.4 4.3 %finish.1 = (f32[64,2048]{1,0:T(8,128)}, f32[64,2048]{1,0:T(8,128)}, f32[128,2048]{1,0:T(8,128)}, f32[128,2048]{1,0:T(8,128)}, f32[128,2048]{1,0:T(8,128)}, /*in...) custom-call(f32[64,2048]{1,0:T(8,128)} %get-tuple-element.39.block_i, ...), custom_call_target="tpu_custom_call" | custom-call | tf_op jit(solution)/shard_map/finish/pallas_call | solution.py:1212

commit v9 on v8

--- a/solution.py
+++ b/solution.py
@@ -962,11 +962,11 @@
     outw_sum.second()
     outp.last()
     s.gg[...] = dot(s.acts[1].reshape(tokens, feats), s.w[2].reshape(-1, chans))
-    outw_sum.third((1,))
     for cols, owners in quarters:
         part = dot(s.gated[...], s.w[2, owners].reshape(-1, chans), NT)
         s.mixed[:, :, :, cols] = part.astype(BF16).reshape(*s.mixed.shape[:3], -1)
     mixed_sum.push()
+    outw_sum.third((1,))
     for rows in sequences:
         gate, gg = s.gate[rows], s.gg[rows]
         sig = sigmoid(gate)

time: 175 us -> 175 us (level)
  no operation moved by 1% of the time
where the time goes in v9:
time: 175 us; the launch traced here: 174 us
  Pallas kernels  174 us (99%)
    pallas_call x1, Pallas kernels, block_call(): pl.pallas_call(functools.partial(block_kernel, list(held)), out_shape=out...  169 us
    pallas_call x1, Pallas kernels, finish_call(): pl.pallas_call(functools.partial(finish_kernel, 1.0 / (2 * block.shape[0]...  4.33 us

profile of v9, /device:TPU:0, one launch (start us, length us, event | category | flops | bytes accessed | tf_op | source)
XLA Modules:
  0.0 174.4 jit_solution(3387348003744746040)
XLA Ops:
  0.7 169.2 %block.1 = (f32[64,2048]{1,0:T(8,128)}, f32[64,2048]{1,0:T(8,128)}, f32[8,128]{1,0:T(8,128)}, bf16[4,128,512]{2,1,0:T(8,128)(2,1)}, bf16[4,128,512]{2,1,0:T(8,12...) custom-call(bf16[128,2048]{1,0:T(8,128)(2,1)} %refs_0_.1, ...), custom_call_target="tpu_custom_call" | custom-call | tf_op jit(solution)/shard_map/block/pallas_call | solution.py:1132
  169.9 4.3 %finish.1 = (f32[64,2048]{1,0:T(8,128)}, f32[64,2048]{1,0:T(8,128)}, f32[128,2048]{1,0:T(8,128)}, f32[128,2048]{1,0:T(8,128)}, f32[128,2048]{1,0:T(8,128)}, /*in...) custom-call(f32[64,2048]{1,0:T(8,128)} %get-tuple-element.39.block_i, ...), custom_call_target="tpu_custom_call" | custom-call | tf_op jit(solution)/shard_map/finish/pallas_call | solution.py:1212

commit v10 on v9

--- a/solution.py
+++ b/solution.py
@@ -902,8 +902,8 @@
         spot, copies, s.part.at[0], s.landing.at[0], s.total.at[0], s.dbl_sems.at[0]
     )
     x_dbl.push()
+    cot.first(1)
     inz.first()
-    cot.first(1)
     x_dbl.middle()
     outp.push((1, 0))
     cot.first(2)

time: 175 us -> 175 us (level)
  no operation moved by 1% of the time
where the time goes in v10:
time: 175 us; the launch traced here: 174 us
  Pallas kernels  174 us (99%)
    pallas_call x1, Pallas kernels, block_call(): pl.pallas_call(functools.partial(block_kernel, list(held)), out_shape=out...  169 us
    pallas_call x1, Pallas kernels, finish_call(): pl.pallas_call(functools.partial(finish_kernel, 1.0 / (2 * block.shape[0]...  4.33 us

profile of v10, /device:TPU:0, one launch (start us, length us, event | category | flops | bytes accessed | tf_op | source)
XLA Modules:
  0.0 174.4 jit_solution(10590867891404686864)
XLA Ops:
  0.7 169.2 %block.1 = (f32[64,2048]{1,0:T(8,128)}, f32[64,2048]{1,0:T(8,128)}, f32[8,128]{1,0:T(8,128)}, bf16[4,128,512]{2,1,0:T(8,128)(2,1)}, bf16[4,128,512]{2,1,0:T(8,12...) custom-call(bf16[128,2048]{1,0:T(8,128)(2,1)} %refs_0_.1, ...), custom_call_target="tpu_custom_call" | custom-call | tf_op jit(solution)/shard_map/block/pallas_call | solution.py:1132
  169.9 4.3 %finish.1 = (f32[64,2048]{1,0:T(8,128)}, f32[64,2048]{1,0:T(8,128)}, f32[128,2048]{1,0:T(8,128)}, f32[128,2048]{1,0:T(8,128)}, f32[128,2048]{1,0:T(8,128)}, /*in...) custom-call(f32[64,2048]{1,0:T(8,128)} %get-tuple-element.39.block_i, ...), custom_call_target="tpu_custom_call" | custom-call | tf_op jit(solution)/shard_map/finish/pallas_call | solution.py:1212
